TPU v7x, 256 devices: a whole 4x4x8 slice. The times are simulated.
256 devices in a mesh: gx: 8 (over x, core), gy: 8 (over z), gz: 4 (over y).
Axes of the slice: x: 4, y: 4, z: 8, core: 2. Of those that a mesh axis runs over, the one named last changes fastest.
Arguments:
- coarse_state: float32 [5, 128, 128, 256], P(None, 'gx', 'gy', 'gz'), may hold values from -1 to 5.75, as said below
- fine_state: float32 [2048, 5, 4096], P(('gx', 'gy', 'gz')), may hold values from -1 to 5.75, as said below
- slot_parent: int32 [2048], replicated, may hold values from -1 to 255, as said below
- slot_corner: int32 [2048, 3], replicated, may hold values from 0 to 55, as said below
Outputs:
- coarse_next: float32 [5, 128, 128, 256], P(None, 'gx', 'gy', 'gz')
- fine_next: float32 [2048, 5, 4096], P(('gx', 'gy', 'gz'))
Inputs may be any that keep to these rules, and one draw needn't show every extreme that they name: `coarse_state`: each cell is a gas state with density and pressure in [0.5, 2] and velocity components in [-0.5, 0.5]. `fine_state`: each cell is a gas state with density and pressure in [0.5, 2] and velocity components in [-0.5, 0.5]. `slot_parent`: slots d * 8 to d * 8 + 7 belong to device d (gx slowest, gz fastest); a device's filled slots come first. A parent has the same gx index as the owner. Every device is the parent of exactly 4 boxes, owned by 4 different devices. In every draw some device fills all 8 slots. `slot_corner`: for a filled slot, the footprint and the cycle of coarse cells around it lie inside the parent's block of 16 x 16 x 64 cells, and footprints and cycles of different boxes are disjoint. Empty slots hold 0, 0, 0.
All inputs are finite; a program needn't handle non-finite values.
Results may differ from a plain program's by a relative error of at most 0.0003.
Values sent between devices are 32-bit elements; how exact they have to be, the bound alone decides.
A program may use at most 128 MiB of HBM per device.

v0:
```python
import jax
import jax.numpy as jnp
from jax import lax
from jax.sharding import PartitionSpec as P

FX = 16
FY = 16
FZ = 16
REGIONS = 4


ADIABATIC = 1.4
COURANT = 0.04


def extended(cells, sides, width):
    for axis, dim in sides:
        count = lax.axis_size(axis)
        head = lax.slice_in_dim(cells, 0, width, axis=dim)
        tail = lax.slice_in_dim(cells, cells.shape[dim] - width, cells.shape[dim], axis=dim)
        cells = jnp.concatenate(
            [
                lax.ppermute(tail, axis, [(i, (i + 1) % count) for i in range(count)]),
                cells,
                lax.ppermute(head, axis, [((i + 1) % count, i) for i in range(count)]),
            ],
            axis=dim,
        )
    return cells


def face_flux(padded, direction):
    window = [slice(1, -1)] * 3
    window[direction] = slice(None)
    window = tuple(window)
    values = padded[(slice(None),) + window]
    inverse = 1.0 / values[0]
    kinetic = (
        0.5 * (values[1] * values[1] + values[2] * values[2] + values[3] * values[3]) * inverse
    )
    pressure = (ADIABATIC - 1.0) * (values[4] - kinetic)
    sound_speed = jnp.sqrt(ADIABATIC * pressure * inverse)
    velocity = values[1 + direction] * inverse
    signal = jnp.abs(velocity) + sound_speed
    pieces = [
        values[0] * velocity,
        values[1] * velocity,
        values[2] * velocity,
        values[3] * velocity,
        (values[4] + pressure) * velocity,
    ]
    pieces[1 + direction] = pieces[1 + direction] + pressure
    physical = jnp.stack(pieces)
    lower_face = [slice(None)] * 3
    upper_face = [slice(None)] * 3
    lower_face[direction] = slice(0, -1)
    upper_face[direction] = slice(1, None)
    lower_face = tuple(lower_face)
    upper_face = tuple(upper_face)
    whole_lower = (slice(None),) + lower_face
    whole_upper = (slice(None),) + upper_face
    return 0.5 * (physical[whole_lower] + physical[whole_upper]) - 0.5 * jnp.maximum(
        signal[lower_face], signal[upper_face]
    ) * (values[whole_upper] - values[whole_lower])


def advance(padded):
    fluxes = (face_flux(padded, 0), face_flux(padded, 1), face_flux(padded, 2))
    change = (
        fluxes[0][:, 1:]
        - fluxes[0][:, :-1]
        + (fluxes[1][:, :, 1:] - fluxes[1][:, :, :-1])
        + (fluxes[2][:, :, :, 1:] - fluxes[2][:, :, :, :-1])
    )
    return (padded[:, 1:-1, 1:-1, 1:-1] - COURANT * change, fluxes)


def widen_face(face_plane):
    fields, height, across = face_plane.shape
    return jnp.broadcast_to(
        face_plane[:, :, None, :, None], (fields, height, 2, across, 2)
    ).reshape(fields, 2 * height, 2 * across)


def coarsen(face_plane):
    fields, height, across = face_plane.shape
    return face_plane.reshape(fields, height // 2, 2, across // 2, 2).sum(axis=(2, 4))


def pack_faces(side_list, end_list):
    side_cells = jnp.stack(side_list, axis=1)
    end_cells = jnp.stack(end_list, axis=1)
    return (side_cells.reshape(side_cells.shape[0], -1), end_cells.reshape(end_cells.shape[0], -1))


def boundary_faces(fluxes):
    along_x, along_y, along_z = fluxes
    return (
        [along_x[:, 0], along_x[:, -1], along_y[:, :, 0], along_y[:, :, -1]],
        [along_z[:, :, :, 0], along_z[:, :, :, -1]],
    )


def patch_rims(patch):
    return pack_faces(
        [
            patch[:, 0, 1:-1, 1:-1],
            patch[:, -1, 1:-1, 1:-1],
            patch[:, 1:-1, 0, 1:-1],
            patch[:, 1:-1, -1, 1:-1],
        ],
        [patch[:, 1:-1, 1:-1, 0], patch[:, 1:-1, 1:-1, -1]],
    )


def ghost_box(fine_box, side_rims, end_rims):
    fields, span_x, span_y, span_z = fine_box.shape
    coarse_x = span_x // 2
    coarse_z = span_z // 2
    side_cells = side_rims.reshape(fields, 4, coarse_x, coarse_z)
    end_cells = end_rims.reshape(fields, 2, coarse_x, coarse_x)
    padded = jnp.pad(fine_box, ((0, 0), (1, 1), (1, 1), (1, 1)), mode="edge")
    padded = padded.at[:, 0, 1:-1, 1:-1].set(widen_face(side_cells[:, 0]))
    padded = padded.at[:, -1, 1:-1, 1:-1].set(widen_face(side_cells[:, 1]))
    padded = padded.at[:, 1:-1, 0, 1:-1].set(widen_face(side_cells[:, 2]))
    padded = padded.at[:, 1:-1, -1, 1:-1].set(widen_face(side_cells[:, 3]))
    padded = padded.at[:, 1:-1, 1:-1, 0].set(widen_face(end_cells[:, 0]))
    padded = padded.at[:, 1:-1, 1:-1, -1].set(widen_face(end_cells[:, 1]))
    return padded


def fine_registers(fluxes):
    side_list, end_list = boundary_faces(fluxes)
    return pack_faces(
        [coarsen(member) for member in side_list], [coarsen(member) for member in end_list]
    )


def fine_first(fine_box, old_sides, old_ends):
    halfway, fluxes = advance(ghost_box(fine_box, old_sides, old_ends))
    side_sum, end_sum = fine_registers(fluxes)
    return (halfway, side_sum, end_sum)


def fine_second(halfway, old_sides, old_ends, new_sides, new_ends, side_sum, end_sum):
    second, fluxes = advance(
        ghost_box(halfway, 0.5 * (old_sides + new_sides), 0.5 * (old_ends + new_ends))
    )
    side_more, end_more = fine_registers(fluxes)
    fields, span_x, span_y, span_z = second.shape
    average = 0.125 * second.reshape(fields, span_x // 2, 2, span_y // 2, 2, span_z // 2, 2).sum(
        axis=(2, 4, 6)
    )
    return (
        second,
        average.reshape(fields, -1),
        0.125 * (side_sum + side_more),
        0.125 * (end_sum + end_more),
    )


def settle(patch, average, side_reg, end_reg, coarse_sides, coarse_ends):
    fields = patch.shape[0]
    inner_x = patch.shape[1] - 2
    inner_z = patch.shape[3] - 2
    side_fix = (COURANT * (side_reg - coarse_sides)).reshape(fields, 4, inner_x, inner_z)
    end_fix = (COURANT * (end_reg - coarse_ends)).reshape(fields, 2, inner_x, inner_x)
    patch = patch.at[:, 1:-1, 1:-1, 1:-1].set(average.reshape(fields, inner_x, inner_x, inner_z))
    patch = patch.at[:, 0, 1:-1, 1:-1].add(-side_fix[:, 0])
    patch = patch.at[:, -1, 1:-1, 1:-1].add(side_fix[:, 1])
    patch = patch.at[:, 1:-1, 0, 1:-1].add(-side_fix[:, 2])
    patch = patch.at[:, 1:-1, -1, 1:-1].add(side_fix[:, 3])
    patch = patch.at[:, 1:-1, 1:-1, 0].add(-end_fix[:, 0])
    patch = patch.at[:, 1:-1, 1:-1, -1].add(end_fix[:, 1])
    return patch


def cut_patches(field_block, corners, extent):

    def cut_single(corner):
        return lax.dynamic_slice(
            field_block, (jnp.int32(0), corner[0] - 1, corner[1] - 1, corner[2] - 1), extent
        )

    return jax.vmap(cut_single)(corners)


def child_faces(coarse_fluxes, corners, fields, coarse_x, coarse_z):
    along_x, along_y, along_z = coarse_fluxes

    def child_single(corner):
        anchor = jnp.int32(0)
        corner_x = corner[0]
        corner_y = corner[1]
        corner_z = corner[2]
        x_lower = lax.dynamic_slice(
            along_x, (anchor, corner_x, corner_y, corner_z), (fields, 1, coarse_x, coarse_z)
        )[:, 0]
        x_upper = lax.dynamic_slice(
            along_x,
            (anchor, corner_x + coarse_x, corner_y, corner_z),
            (fields, 1, coarse_x, coarse_z),
        )[:, 0]
        y_lower = lax.dynamic_slice(
            along_y, (anchor, corner_x, corner_y, corner_z), (fields, coarse_x, 1, coarse_z)
        )[:, :, 0]
        y_upper = lax.dynamic_slice(
            along_y,
            (anchor, corner_x, corner_y + coarse_x, corner_z),
            (fields, coarse_x, 1, coarse_z),
        )[:, :, 0]
        z_lower = lax.dynamic_slice(
            along_z, (anchor, corner_x, corner_y, corner_z), (fields, coarse_x, coarse_x, 1)
        )[:, :, :, 0]
        z_upper = lax.dynamic_slice(
            along_z,
            (anchor, corner_x, corner_y, corner_z + coarse_z),
            (fields, coarse_x, coarse_x, 1),
        )[:, :, :, 0]
        return pack_faces([x_lower, x_upper, y_lower, y_upper], [z_lower, z_upper])

    return jax.vmap(child_single)(corners)


def spread_rows(rows_in, targets, members):
    return (
        jnp.zeros((members,) + rows_in.shape[1:], rows_in.dtype)
        .at[targets]
        .set(rows_in, mode="drop")
    )


def owner_first(fine_state, old_rows, fetch_row, filled):
    capacity, fields, fine_cells = fine_state.shape
    side_rows, end_rows = old_rows

    def advance_slot(position, carried):
        working, side_sums, end_sums = carried
        sender = fetch_row[position]
        fine_box = lax.dynamic_index_in_dim(working, position, 0, keepdims=False).reshape(
            fields, FX, FY, FZ
        )
        halfway, side_sum, end_sum = fine_first(fine_box, side_rows[sender], end_rows[sender])
        working = lax.dynamic_update_index_in_dim(
            working, halfway.reshape(fields, fine_cells), position, 0
        )
        side_sums = lax.dynamic_update_index_in_dim(side_sums, side_sum, position, 0)
        end_sums = lax.dynamic_update_index_in_dim(end_sums, end_sum, position, 0)
        return (working, side_sums, end_sums)

    initial = (
        fine_state,
        jnp.zeros((capacity, fields, side_rows.shape[2]), jnp.float32),
        jnp.zeros((capacity, fields, end_rows.shape[2]), jnp.float32),
    )
    return lax.fori_loop(jnp.int32(0), filled, advance_slot, initial)


def owner_second(working, side_sums, end_sums, old_rows, new_rows, fetch_row, filled, members):
    capacity, fields, fine_cells = working.shape
    coarse_x = FX // 2
    coarse_z = FZ // 2

    def advance_slot(position, carried):
        boxes, averages, side_regs, end_regs = carried
        sender = fetch_row[position]
        halfway = lax.dynamic_index_in_dim(boxes, position, 0, keepdims=False).reshape(
            fields, FX, FY, FZ
        )
        second, average, side_reg, end_reg = fine_second(
            halfway,
            old_rows[0][sender],
            old_rows[1][sender],
            new_rows[0][sender],
            new_rows[1][sender],
            side_sums[position],
            end_sums[position],
        )
        boxes = lax.dynamic_update_index_in_dim(
            boxes, second.reshape(fields, fine_cells), position, 0
        )
        averages = lax.dynamic_update_index_in_dim(averages, average, sender, 0)
        side_regs = lax.dynamic_update_index_in_dim(side_regs, side_reg, sender, 0)
        end_regs = lax.dynamic_update_index_in_dim(end_regs, end_reg, sender, 0)
        return (boxes, averages, side_regs, end_regs)

    initial = (
        working,
        jnp.zeros((members, fields, coarse_x * coarse_x * coarse_z), jnp.float32),
        jnp.zeros((members, fields, side_sums.shape[2]), jnp.float32),
        jnp.zeros((members, fields, end_sums.shape[2]), jnp.float32),
    )
    return lax.fori_loop(jnp.int32(0), filled, advance_slot, initial)


def settle_children(coarse_new, child_corner, averages, side_regs, end_regs, coarse_faces, extent):

    def settle_child(position, coarse_out):
        corner = child_corner[position]
        starts = (jnp.int32(0), corner[0] - 1, corner[1] - 1, corner[2] - 1)
        current = lax.dynamic_slice(coarse_out, starts, extent)
        settled = settle(
            current,
            averages[position],
            side_regs[position],
            end_regs[position],
            coarse_faces[0][position],
            coarse_faces[1][position],
        )
        return lax.dynamic_update_slice(coarse_out, settled, starts)

    return lax.fori_loop(jnp.int32(0), jnp.int32(child_corner.shape[0]), settle_child, coarse_new)


def on_device(coarse_state, fine_state, slot_parent, slot_corner):
    fields = coarse_state.shape[0]
    capacity = fine_state.shape[0]
    members = lax.axis_size(("gy", "gz"))
    plane_index = lax.axis_index("gx")
    within = lax.axis_index(("gy", "gz"))
    myself = plane_index * members + within
    coarse_x = FX // 2
    coarse_z = FZ // 2
    extent = (fields, coarse_x + 2, coarse_x + 2, coarse_z + 2)
    plane_start = plane_index * (members * capacity)
    plane_parent = lax.dynamic_slice_in_dim(
        slot_parent, plane_start, members * capacity, 0
    ).reshape(members, capacity)
    plane_corner = lax.dynamic_slice_in_dim(
        slot_corner, plane_start, members * capacity, 0
    ).reshape(members, capacity, 3)
    own_parent = lax.dynamic_index_in_dim(plane_parent, within, 0, keepdims=False)
    occupied = own_parent >= 0
    filled = jnp.sum(occupied.astype(jnp.int32))
    source = jnp.where(occupied, own_parent % members, members)
    fetch_row = jnp.minimum(source, members - 1)
    parent_hit = plane_parent == myself
    holder = jnp.any(parent_hit, axis=1)
    ranking = jnp.cumsum(holder.astype(jnp.int32)) - 1
    peer_ids = jnp.arange(members, dtype=jnp.int32)
    chosen = holder[None, :] & (ranking[None, :] == jnp.arange(REGIONS, dtype=jnp.int32)[:, None])
    child_peer = jnp.sum(jnp.where(chosen, peer_ids[None, :], 0), axis=1)
    peer_corner = jnp.sum(jnp.where(parent_hit[:, :, None], plane_corner, 0), axis=1)
    child_corner = jnp.sum(jnp.where(chosen[:, :, None], peer_corner[None, :, :], 0), axis=1)
    old_rims = jax.vmap(patch_rims)(cut_patches(coarse_state, child_corner, extent))
    padded = extended(coarse_state, (("gx", 1), ("gy", 2), ("gz", 3)), 1)
    coarse_new, coarse_fluxes = advance(padded)
    new_rims = jax.vmap(patch_rims)(cut_patches(coarse_new, child_corner, extent))
    coarse_faces = child_faces(coarse_fluxes, child_corner, fields, coarse_x, coarse_z)
    all_rims = (
        lax.all_to_all(
            spread_rows(old_rims[0], child_peer, members),
            ("gy", "gz"),
            split_axis=0,
            concat_axis=0,
            tiled=True,
        ),
        lax.all_to_all(
            spread_rows(old_rims[1], child_peer, members),
            ("gy", "gz"),
            split_axis=0,
            concat_axis=0,
            tiled=True,
        ),
        lax.all_to_all(
            spread_rows(new_rims[0], child_peer, members),
            ("gy", "gz"),
            split_axis=0,
            concat_axis=0,
            tiled=True,
        ),
        lax.all_to_all(
            spread_rows(new_rims[1], child_peer, members),
            ("gy", "gz"),
            split_axis=0,
            concat_axis=0,
            tiled=True,
        ),
    )
    old_rows = (all_rims[0], all_rims[1])
    new_rows = (all_rims[2], all_rims[3])
    working, side_sums, end_sums = owner_first(fine_state, old_rows, fetch_row, filled)
    fine_next, averages, side_regs, end_regs = owner_second(
        working, side_sums, end_sums, old_rows, new_rows, fetch_row, filled, members
    )
    answers = (
        lax.all_to_all(averages, ("gy", "gz"), split_axis=0, concat_axis=0, tiled=True),
        lax.all_to_all(side_regs, ("gy", "gz"), split_axis=0, concat_axis=0, tiled=True),
        lax.all_to_all(end_regs, ("gy", "gz"), split_axis=0, concat_axis=0, tiled=True),
    )
    coarse_next = settle_children(
        coarse_new,
        child_corner,
        answers[0][child_peer],
        answers[1][child_peer],
        answers[2][child_peer],
        coarse_faces,
        extent,
    )
    return (coarse_next, fine_next)


def solution(mesh):
    return jax.shard_map(
        on_device,
        mesh=mesh,
        in_specs=(P(None, "gx", "gy", "gz"), P(("gx", "gy", "gz"), None, None), P(), P()),
        out_specs=(P(None, "gx", "gy", "gz"), P(("gx", "gy", "gz"), None, None)),
        check_vma=False,
    )
```

profile of v0, /device:TPU:4, one launch (start us, length us, event | category | flops | bytes accessed | tf_op | source)
XLA Modules:
  0.0 1798.1 jit_solution(1736819745741763518)
XLA Ops:
  5.3 10.6 while.75
  23.0 11.6 all-to-all-start.1
  75.8 10.6 while.76
  136.1 648.8 %while.72 = (s32[]{:T(128)}, f32[8,5,4096]{2,1,0:T(8,128)}, f32[8,5,256]{2,1,0:T(8,128)S(1)}, f32[8,5,128]{2,1,0:T(8,128)S(1)}, s32[]{:T(128)}, /*index=5*/s32[8...) while((s32[]{:T(128)}, f32[8,5,4096]{2,1,0:T(8,128)}, ...), condition=%wide.region_15.16_spmd, body=%wide.region_8.15_spmd.sunk | while | flops 1246709 | bytes 13849765 | solution.py:256
  153.4 14.6 scatter.120
  168.0 14.6 scatter.121
  188.2 16.4 scatter.123
  232.6 14.6 scatter.120
  247.2 14.6 scatter.121
  267.4 16.4 scatter.123
  311.7 14.6 scatter.120
  326.4 14.6 scatter.121
  346.5 16.4 scatter.123
  390.9 14.6 scatter.120
  405.5 14.6 scatter.121
  425.7 16.4 scatter.123
  470.0 14.6 scatter.120
  484.7 14.6 scatter.121
  504.8 16.4 scatter.123
  549.2 14.6 scatter.120
  563.8 14.6 scatter.121
  584.0 16.4 scatter.123
  628.3 14.6 scatter.120
  643.0 14.6 scatter.121
  663.1 16.4 scatter.123
  707.5 14.6 scatter.120
  722.1 14.6 scatter.121
  742.3 16.4 scatter.123
  787.1 687.4 %while.73 = (s32[]{:T(128)}, f32[8,5,4096]{2,1,0:T(8,128)}, f32[32,5,512]{2,1,0:T(8,128)}, f32[32,5,256]{2,1,0:T(8,128)}, f32[32,5,128]{2,1,0:T(8,128)S(1)}, /*i...) while((s32[]{:T(128)}, f32[8,5,4096]{2,1,0:T(8,128)}, ...), condition=%wide.region_26.27_spmd, body=%wide.region_18.26_spmd.sunk | while | flops 1274869 | bytes 14209245 | solution.py:293
  804.5 14.6 scatter.126
  819.2 14.6 scatter.127
  839.3 16.4 scatter.129
  890.4 14.6 scatter.126
  905.0 14.6 scatter.127
  925.2 16.4 scatter.129
  976.2 14.6 scatter.126
  990.8 14.6 scatter.127
  1011.0 16.4 scatter.129
  1062.0 14.6 scatter.126
  1076.6 14.6 scatter.127
  1096.8 16.4 scatter.129
  1147.8 14.6 scatter.126
  1162.4 14.6 scatter.127
  1182.6 16.4 scatter.129
  1233.6 14.6 scatter.126
  1248.2 14.6 scatter.127
  1268.4 16.4 scatter.129
  1319.4 14.6 scatter.126
  1334.0 14.6 scatter.127
  1354.2 16.4 scatter.129
  1405.2 14.6 scatter.126
  1419.9 14.6 scatter.127
  1440.0 16.4 scatter.129
  1474.6 17.5 all_to_all.35
  1492.1 15.6 all_to_all.36
  1546.8 250.0 %while.74 = (s32[]{:T(128)}, f32[5,16,16,64]{3,2,1,0:T(8,128)S(1)}, s32[4,3]{1,0:T(4,128)S(1)}, f32[4,5,512]{2,1,0:T(8,128)S(1)}, f32[4,5,256]{2,1,0:T(8,128)S(1...) while((s32[]{:T(128)}, f32[5,16,16,64]{3,2,1,0:T(8,128)S(1)}, ...), condition=%wide.region_28.29_spmd, body=%wide.region_27.28_spmd.sunk | while | flops 6734 | bytes 334467 | solution.py:312
  1552.5 11.9 scatter.130
  1587.5 21.9 %dynamic_update_slice.87 = f32[5,16,16,64]{3,2,1,0:T(8,128)S(1)} dynamic-update-slice(f32[5,16,16,64]{3,2,1,0:T(8,128)S(1)} %get-tuple-element.1832, f32[5,10,10,10]{3,2,1,0:T(8,128)S(1)} %copy.1230, s32[]{:T(128)} %constant.1097.clone.1..sunk.2, s32[]{:T(128)S(6)} %select_n.314, s32[]{:T(128)S(6)} %select_n.315, s32[]{:T(128)S(6)} %select_n.316) | dynamic-update-slice | bytes 40004 | tf_op jit(solution)/shard_map/while/body/dynamic_update_slice | solution.py:310
  1615.0 11.9 scatter.130
  1650.0 21.9 %dynamic_update_slice.87 = f32[5,16,16,64]{3,2,1,0:T(8,128)S(1)} dynamic-update-slice(f32[5,16,16,64]{3,2,1,0:T(8,128)S(1)} %get-tuple-element.1832, f32[5,10,10,10]{3,2,1,0:T(8,128)S(1)} %copy.1230, s32[]{:T(128)} %constant.1097.clone.1..sunk.2, s32[]{:T(128)S(6)} %select_n.314, s32[]{:T(128)S(6)} %select_n.315, s32[]{:T(128)S(6)} %select_n.316) | dynamic-update-slice | bytes 40004 | tf_op jit(solution)/shard_map/while/body/dynamic_update_slice | solution.py:310
  1677.5 11.9 scatter.130
  1712.5 21.9 %dynamic_update_slice.87 = f32[5,16,16,64]{3,2,1,0:T(8,128)S(1)} dynamic-update-slice(f32[5,16,16,64]{3,2,1,0:T(8,128)S(1)} %get-tuple-element.1832, f32[5,10,10,10]{3,2,1,0:T(8,128)S(1)} %copy.1230, s32[]{:T(128)} %constant.1097.clone.1..sunk.2, s32[]{:T(128)S(6)} %select_n.314, s32[]{:T(128)S(6)} %select_n.315, s32[]{:T(128)S(6)} %select_n.316) | dynamic-update-slice | bytes 40004 | tf_op jit(solution)/shard_map/while/body/dynamic_update_slice | solution.py:310
  1740.0 11.9 scatter.130
  1775.0 21.9 %dynamic_update_slice.87 = f32[5,16,16,64]{3,2,1,0:T(8,128)S(1)} dynamic-update-slice(f32[5,16,16,64]{3,2,1,0:T(8,128)S(1)} %get-tuple-element.1832, f32[5,10,10,10]{3,2,1,0:T(8,128)S(1)} %copy.1230, s32[]{:T(128)} %constant.1097.clone.1..sunk.2, s32[]{:T(128)S(6)} %select_n.314, s32[]{:T(128)S(6)} %select_n.315, s32[]{:T(128)S(6)} %select_n.316) | dynamic-update-slice | bytes 40004 | tf_op jit(solution)/shard_map/while/body/dynamic_update_slice | solution.py:310
  (1718 shorter events, 805.9 us)
Async XLA Ops:
  0.6 2.2 copy-start
  0.6 4.7 copy-start.5
  1.5 39.2 %collective-permute-start.1 = (f32[5,1,16,64]{3,2,1,0:T(8,128)S(1)}, f32[5,1,16,64]{3,2,1,0:T(8,128)S(1)}, u32[]{:S(2)}, u32[]{:S(2)}) collective-permute-start(f32[5,1,16,64]{3,2,1,0:T(8,128)S(1)} %get-tuple-element.1300), channel_id=1, source_target_pairs={{32,0},{64,32},{96,64},{128,96},{160,128},{192,160},{224,192},{0,2... | collective-permute-start | bytes 61448 | tf_op jit(solution)/shard_map/ppermute | solution.py:25
  1.5 39.1 %collective-permute-start = (f32[5,1,16,64]{3,2,1,0:T(8,128)S(1)}, f32[5,1,16,64]{3,2,1,0:T(8,128)S(1)}, u32[]{:S(2)}, u32[]{:S(2)}) collective-permute-start(f32[5,1,16,64]{3,2,1,0:T(8,128)S(1)} %get-tuple-element.1301), channel_id=1, source_target_pairs={{0,32},{32,64},{64,96},{96,128},{128,160},{160,192},{192,224},{224... | collective-permute-start | bytes 61448 | tf_op jit(solution)/shard_map/ppermute | solution.py:23
  3.4 118.3 %copy-start.27 = (s32[4]{0:T(128)}, s32[4]{0:T(128)S(1)}, u32[]{:S(2)}) copy-start(s32[4]{0:T(128)S(1)} %fusion.130) | copy-start | bytes 52
  3.8 1.5 copy-start.23
  23.0 72.3 %all-to-all-start.1 = ((f32[32,5,128]{2,1,0:T(8,128)}), f32[32,5,128]{2,1,0:T(8,128)}, u32[]{:S(2)}, u32[]{:S(2)}) async-start(f32[32,5,128]{2,1,0:T(8,128)} %scatter_fusion.1), calls=%async_computation.1 | async-start | bytes 262144 | tf_op jit(solution)/shard_map/all_to_all | solution.py:358
  35.3 1.1 copy-start.19
  41.0 5.7 collective-permute-start.2
  42.8 4.1 collective-permute-start.3
  44.6 29.8 %copy-start.6 = (f32[5,17,16,64]{3,2,1,0:T(8,128)}, f32[5,17,16,64]{3,2,1,0:T(8,128)S(1)}, u32[]{:S(2)}) copy-start(f32[5,17,16,64]{3,2,1,0:T(8,128)S(1)} %fusion.89) | copy-start | bytes 1044484
  46.7 0.6 copy-start.15
  46.8 0.6 copy-start.17
  56.3 11.6 collective-permute-start.4
  57.8 8.7 collective-permute-start.5
  65.2 1.3 copy-start.8
  66.5 4.0 copy-start.16
  66.5 4.0 copy-start.18
  72.4 1.2 copy-start.12
  73.6 1.1 copy-start.13
  73.6 1.3 copy-start.14
  74.4 1.2 copy-start.10
  86.4 6.2 copy-start.2
  95.3 19.2 %all-to-all-start.3 = ((f32[32,5,128]{2,1,0:T(8,128)}), f32[32,5,128]{2,1,0:T(8,128)S(1)}, u32[]{:S(2)}, u32[]{:S(2)}) async-start(f32[32,5,128]{2,1,0:T(8,128)} %scatter_fusion.3), calls=%async_computation.3 | async-start | bytes 262144 | tf_op jit(solution)/shard_map/all_to_all | solution.py:372
  114.5 0.7 copy-start.20
  115.1 16.3 all-to-all-start
  131.4 653.4 %all-to-all-start.2 = ((f32[32,5,256]{2,1,0:T(8,128)}), f32[32,5,256]{2,1,0:T(8,128)}, u32[]{:S(2)}, u32[]{:S(2)}) async-start(f32[32,5,256]{2,1,0:T(8,128)} %scatter_fusion.2), calls=%async_computation.2 | async-start | bytes 524288 | tf_op jit(solution)/shard_map/all_to_all | solution.py:365
  784.9 0.6 copy-start.21
  784.9 0.6 copy-start.22
  1474.6 37.0 %copy-start.24 = (s32[4,3]{0,1:T(4,128)S(1)}, s32[4,3]{0,1:T(4,128)}, u32[]{:S(2)}) copy-start(s32[4,3]{0,1:T(4,128)} %copy-done.23) | copy-start | bytes 148
  1474.6 37.1 %copy-start.28 = (s32[4]{0:T(128)S(1)}, s32[4]{0:T(128)}, u32[]{:S(2)}) copy-start(s32[4]{0:T(128)} %copy-done.27) | copy-start | bytes 52
  1474.6 37.1 %copy-start.7 = (f32[5,17,16,64]{3,2,1,0:T(8,128)S(1)}, f32[5,17,16,64]{3,2,1,0:T(8,128)}, u32[]{:S(2)}) copy-start(f32[5,17,16,64]{3,2,1,0:T(8,128)} %copy-done.6) | copy-start | bytes 1044484
  1507.7 38.6 %all-to-all-start.4 = ((f32[32,5,512]{2,1,0:T(8,128)}), f32[32,5,512]{2,1,0:T(8,128)S(1)}, u32[]{:S(2)}, u32[]{:S(2)}) async-start(f32[32,5,512]{2,1,0:T(8,128)} %get-tuple-element.841), calls=%async_computation.4 | async-start | bytes 1048576 | tf_op jit(solution)/shard_map/all_to_all | solution.py:387
  1511.7 7.3 copy-start.32
  1511.7 9.1 copy-start.29
  1519.0 3.4 copy-start.9
  1522.5 7.3 copy-start.31
  1522.5 9.1 copy-start.30
  1531.6 2.0 copy-start.11
  1533.6 5.5 copy-start.26
  1533.6 7.1 copy-start.25
  1542.5 4.3 copy-start.3
  1796.9 0.8 copy-start.4
  1796.9 0.8 copy-start.1
where the time goes:
time: 1810 us; the launch traced here: 1800 us
  local copies, waits for them, and re-layouts  1460 us (81%)
  other arithmetic  159 us (9%)
  loops' own time  80.2 us (4%)
  starting transfers between devices  40.5 us (2%)
  blocking collectives  33.1 us (2%)
  waiting for transfers between devices  19.3 us (1%)
    scatter x16, local copies, waits for them, and re-layouts, ghost_box(): padded = padded.at[:, 1:-1, 1:-1, -1].set(widen_face(end_cells[:, 1]))  263 us
    scatter x16, local copies, waits for them, and re-layouts, ghost_box(): padded = padded.at[:, 1:-1, -1, 1:-1].set(widen_face(side_cells[:, 3]))  234 us
    scatter x16, local copies, waits for them, and re-layouts, ghost_box(): padded = padded.at[:, 1:-1, 0, 1:-1].set(widen_face(side_cells[:, 2]))  234 us
    scatter x16, local copies, waits for them, and re-layouts, ghost_box(): padded = padded.at[:, 1:-1, 1:-1, 0].set(widen_face(end_cells[:, 0]))  88.7 us
    dynamic_update_slice x8, local copies, waits for them, and re-layouts, settle_child(): return lax.dynamic_update_slice(coarse_out, settled, starts)  87.8 us
    another operation x115, local copies, waits for them, and re-layouts  78.6 us
    scatter x4, local copies, waits for them, and re-layouts, settle(): patch.at[:, 1:-1, 1:-1, 1:-1]  47.8 us
    another operation x1, loops' own time, owner_first(): return lax.fori_loop(jnp.int32(0), filled, advance_slot, initial)  38 us
  transfers between devices with their start and end apart: 11, of which 4 were waited for; matrix products, arithmetic and copies ran while one was open for 40% of the time, Pallas kernels for 0%

commit v1 on v0

v1 whole, which is shorter than its diff:
```python
import functools

import jax
import jax.numpy as jnp
from jax import lax
from jax.experimental import pallas as pl
from jax.experimental.pallas import tpu as pltpu
from jax.sharding import PartitionSpec as P

GAMMA = 1.4
COURANT = 0.04
FIELDS = 5
REGIONS = 4
BOXMAX = 8
MESH = pl.DeviceIdType.MESH
F32 = jnp.float32
I32 = jnp.int32


def iota(shape, dim):
    return lax.broadcasted_iota(I32, shape, dim)


def pick(values, lanes):
    numbers = lax.GatherDimensionNumbers(
        offset_dims=(),
        collapsed_slice_dims=(1,),
        start_index_map=(1,),
        operand_batching_dims=(0,),
        start_indices_batching_dims=(0,),
    )
    return lax.gather(
        values,
        lanes[..., None],
        numbers,
        (1, 1),
        mode=lax.GatherScatterMode.PROMISE_IN_BOUNDS,
    )


def prims(q):
    inverse = 1.0 / q[0]
    kinetic = 0.5 * (q[1] * q[1] + q[2] * q[2] + q[3] * q[3]) * inverse
    pressure = (GAMMA - 1.0) * (q[4] - kinetic)
    sound = jnp.sqrt(GAMMA * pressure * inverse)
    return inverse, pressure, sound, q[4] + pressure


def along(q, prim, axis):
    inverse, pressure, sound, total = prim
    velocity = q[1 + axis] * inverse
    flux = [q[1 + axis], q[1] * velocity, q[2] * velocity, q[3] * velocity, total * velocity]
    flux[1 + axis] = flux[1 + axis] + pressure
    return flux, jnp.abs(velocity) + sound


def face(low, low_terms, high, high_terms):
    signal = jnp.maximum(low_terms[1], high_terms[1])
    return [
        (low_terms[0][f] + high_terms[0][f]) - signal * (high[f] - low[f]) for f in range(FIELDS)
    ]


def moved(q, terms, move):
    return [move(v) for v in q], [move(v) for v in terms[0]], move(terms[1])


def fine_step(box, rim, reg, put, second):
    lane = iota((BOXMAX, 128), 1)
    first_row = lane < 16
    last_row = lane >= 112
    k_first = lane % 16 == 0
    k_last = lane % 16 == 15
    half_k = (lane % 16) // 2
    quarter = lane // 32
    squeeze = ((lane % 32) // 8) * 32 + (lane % 8) * 2
    part = (lane % 64) // 8

    def halves(f, plane):
        return [box[f, plane, :, 128 * h : 128 * h + 128] for h in range(2)]

    for f in range(FIELDS):
        for h in range(2):
            spread = (h * 4 + quarter) * 8 + half_k
            box[f, 0, :, 128 * h : 128 * h + 128] = pick(rim[3 * f], spread)
            box[f, 17, :, 128 * h : 128 * h + 128] = pick(rim[3 * f], spread + 64)

    def load(plane):
        both = [halves(f, plane) for f in range(FIELDS)]
        return [[both[f][h] for f in range(FIELDS)] for h in range(2)]

    def x_faces(low, low_prim, high, high_prim):
        return [
            face(low[h], along(low[h], low_prim[h], 0), high[h], along(high[h], high_prim[h], 0))
            for h in range(2)
        ]

    def roll(v, by):
        return pltpu.roll(v, by % 128, 1)

    ghost = load(0)
    here = load(1)
    here_prim = [prims(here[h]) for h in range(2)]
    x_low = x_faces(ghost, [prims(ghost[h]) for h in range(2)], here, here_prim)

    def x_register(faces, side):
        for f in range(FIELDS):
            out = []
            for h in range(2):
                v = faces[h][f]
                v = v + roll(v, -1)
                v = v + roll(v, -16)
                out.append(pick(v, squeeze))
            both = jnp.where((lane % 64) < 32, out[0], out[1])
            mine = (lane < 64) if side == 0 else (lane >= 64)
            reg[7 * f] = reg[7 * f] + jnp.where(mine, both, 0.0)

    x_register(x_low, 0)

    def pair(big, carried):
        here, here_prim, x_low = carried
        y_lanes = big * 8 + half_k + jnp.where(lane >= 64, 64, 0)
        y_ghost = [pick(rim[3 * f + 1], y_lanes) for f in range(FIELDS)]
        y_ghost_terms = along(y_ghost, prims(y_ghost), 1)
        z_ghost = []
        z_ghost_terms = []
        for h in range(2):
            z_lanes = big * 8 + h * 4 + quarter + jnp.where(lane % 16 >= 8, 64, 0)
            ghost = [pick(rim[3 * f + 2], z_lanes) for f in range(FIELDS)]
            z_ghost.append(ghost)
            z_ghost_terms.append(along(ghost, prims(ghost), 2))
        y_sum = [None] * FIELDS
        z_sum = [[None] * FIELDS for _ in range(2)]
        new_sum = [[None] * FIELDS for _ in range(2)]

        def accumulate(total, v):
            return v if total is None else total + v

        for sub in range(2):
            plane = 2 * big + sub
            after = load(plane + 2)
            after_prim = [prims(after[h]) for h in range(2)]
            x_high = x_faces(here, here_prim, after, after_prim)

            y_terms = [along(here[h], here_prim[h], 1) for h in range(2)]
            rolled = [moved(here[h], y_terms[h], lambda v: roll(v, 16)) for h in range(2)]

            def y_select(h, low, high):
                return jnp.where(first_row, low, high)

            low0 = [jnp.where(first_row, y_ghost[f], rolled[0][0][f]) for f in range(FIELDS)]
            low0_terms = (
                [jnp.where(first_row, y_ghost_terms[0][f], rolled[0][1][f]) for f in range(FIELDS)],
                jnp.where(first_row, y_ghost_terms[1], rolled[0][2]),
            )
            low1 = [jnp.where(first_row, rolled[0][0][f], rolled[1][0][f]) for f in range(FIELDS)]
            low1_terms = (
                [jnp.where(first_row, rolled[0][1][f], rolled[1][1][f]) for f in range(FIELDS)],
                jnp.where(first_row, rolled[0][2], rolled[1][2]),
            )
            y0 = face(low0, low0_terms, here[0], y_terms[0])
            y1 = face(low1, low1_terms, here[1], y_terms[1])
            y_end = face(here[1], y_terms[1], y_ghost, y_ghost_terms)
            y_diff = [[], []]
            for f in range(FIELDS):
                up0 = roll(y0[f], -16)
                up1 = roll(y1[f], -16)
                y_diff[0].append(jnp.where(last_row, up1, up0) - y0[f])
                y_diff[1].append(jnp.where(last_row, y_end[f], up1) - y1[f])
                y_sum[f] = accumulate(y_sum[f], jnp.where(lane < 64, y0[f], y_end[f]))

            z_diff = [[], []]
            for h in range(2):
                terms = along(here[h], here_prim[h], 2)
                shifted = moved(here[h], terms, lambda v: roll(v, 1))
                low = [jnp.where(k_first, z_ghost[h][f], shifted[0][f]) for f in range(FIELDS)]
                low_terms = (
                    [
                        jnp.where(k_first, z_ghost_terms[h][0][f], shifted[1][f])
                        for f in range(FIELDS)
                    ],
                    jnp.where(k_first, z_ghost_terms[h][1], shifted[2]),
                )
                z = face(low, low_terms, here[h], terms)
                z_end = face(here[h], terms, z_ghost[h], z_ghost_terms[h])
                for f in range(FIELDS):
                    z_diff[h].append(jnp.where(k_last, z_end[f], roll(z[f], -1)) - z[f])
                    z_sum[h][f] = accumulate(z_sum[h][f], jnp.where(k_last, z_end[f], z[f]))

            for h in range(2):
                for f in range(FIELDS):
                    change = (x_high[h][f] - x_low[h][f]) + y_diff[h][f] + z_diff[h][f]
                    new = here[h][f] - (0.5 * COURANT) * change
                    put(f, plane, h, new)
                    if second:
                        new_sum[h][f] = accumulate(new_sum[h][f], new)
            here, here_prim, x_low = after, after_prim, x_high

        mine = part == big
        y_from = (lane % 8) * 2 + jnp.where(lane >= 64, 112, 0)
        z_from = (lane % 4) * 32 + jnp.where(lane >= 64, 15, 0)
        for f in range(FIELDS):
            v = y_sum[f] + roll(y_sum[f], -1)
            reg[7 * f + 1] = reg[7 * f + 1] + jnp.where(mine, pick(v, y_from), 0.0)
            out = []
            for h in range(2):
                v = z_sum[h][f] + roll(z_sum[h][f], -16)
                out.append(pick(v, z_from))
            v = jnp.where(lane % 8 < 4, out[0], out[1])
            reg[7 * f + 2] = reg[7 * f + 2] + jnp.where(mine, v, 0.0)
            if second:
                out = []
                for h in range(2):
                    v = new_sum[h][f]
                    v = v + roll(v, -1)
                    v = v + roll(v, -16)
                    out.append(pick(v, squeeze))
                v = jnp.where((lane % 64) < 32, out[0], out[1])
                where = 7 * f + 3 + big // 2
                reg[where] = jnp.where(lane // 64 == big % 2, v, reg[where])
        return here, here_prim, x_low

    last = lax.fori_loop(0, 8, pair, (here, here_prim, x_low))
    x_register(last[2], 1)


def coarse_step(block, y_rim, z_rim, new, x_face, y_low, y_high, z_low, z_high):
    lane = iota((16, 128), 1)
    row = iota((16, 128), 0)
    tip = iota((8, 128), 0)

    def load(plane):
        return [block[f, plane] for f in range(FIELDS)]

    ghost = load(0)
    here = load(1)
    here_prim = prims(here)
    low = face(ghost, along(ghost, prims(ghost), 0), here, along(here, here_prim, 0))
    for f in range(FIELDS):
        x_face[f, 0] = low[f]

    def one(x, carried):
        here, here_prim, x_low = carried
        after = load(x + 2)
        after_prim = prims(after)
        x_high = face(here, along(here, here_prim, 0), after, along(after, after_prim, 0))

        tips = []
        wide = []
        column = (x % 8) * 16 + row
        for f in range(FIELDS):
            above = y_rim[1, f, pl.ds(x, 1), :]
            below = y_rim[0, f, pl.ds(x, 1), :]
            tips.append(
                jnp.where(
                    tip == 0,
                    jnp.broadcast_to(above, (8, 128)),
                    jnp.broadcast_to(below, (8, 128)),
                )
            )
            below = jnp.broadcast_to(z_rim[0, x // 8, f : f + 1, :], (16, 128))
            above = jnp.broadcast_to(z_rim[1, x // 8, f : f + 1, :], (16, 128))
            side = jnp.where(lane == 64, pick(above, column), pick(below, column))
            wide.append(jnp.where(lane < 64, here[f], side))

        tall = [jnp.concatenate([here[f], tips[f]], axis=0) for f in range(FIELDS)]
        terms = along(tall, prims(tall), 1)
        shifted = moved(tall, terms, lambda v: pltpu.roll(v, 1, 0))
        y = face(shifted[0], (shifted[1], shifted[2]), tall, terms)

        terms = along(wide, prims(wide), 2)
        shifted = moved(wide, terms, lambda v: pltpu.roll(v, 1, 1))
        z = face(shifted[0], (shifted[1], shifted[2]), wide, terms)
        for f in range(FIELDS):
            up = pltpu.roll(y[f], 23, 0)[:16]
            down = y[f][:16]
            right = pltpu.roll(z[f], 127, 1)
            x_face[f, x + 1] = x_high[f]
            y_low[f, x] = down
            y_high[f, x] = up
            z_low[f, x] = z[f]
            z_high[f, x] = right
            change = (x_high[f] - x_low[f]) + (up - down) + (right - z[f])
            new[f, x] = here[f] - (0.5 * COURANT) * change
        return after, after_prim, x_high

    lax.fori_loop(0, 16, one, (here, here_prim, low))


def cut_rims(source, corner, put):
    cx, cy, cz = corner
    lane = iota((16, 128), 1)
    row = iota((16, 128), 0)
    part = (lane % 64) // 8
    along_z = cz + lane % 8
    rows_x = row - cy == part
    rows_y = row == jnp.where(lane < 64, cy - 1, cy + 8)
    rows_z = row - cy == lane % 8
    ends = jnp.where(lane < 64, cz - 1, cz + 8)
    for f in range(FIELDS):
        low = pick(source(f, cx - 1), along_z)
        high = pick(source(f, cx + 8), along_z)
        v = jnp.where(rows_x, jnp.where(lane < 64, low, high), 0.0)
        put(f, 0, jnp.sum(v, axis=0, keepdims=True))
        y_total = jnp.zeros((16, 128), F32)
        z_total = jnp.zeros((16, 128), F32)
        for big in range(8):
            plane = source(f, cx + big)
            y_total = jnp.where(part == big, pick(plane, along_z), y_total)
            z_total = jnp.where(part == big, pick(plane, ends), z_total)
        put(f, 1, jnp.sum(jnp.where(rows_y, y_total, 0.0), axis=0, keepdims=True))
        put(f, 2, jnp.sum(jnp.where(rows_z, z_total, 0.0), axis=0, keepdims=True))


def settle(corners, answers, new, x_face, y_low, y_high, z_low, z_high, out):
    lane = iota((16, 128), 1)
    row = iota((16, 128), 0)

    def one(x, _):
        values = [jnp.zeros((16, 128), F32) for _ in range(FIELDS)]
        kind = jnp.zeros((16, 128), I32)
        for c in range(REGIONS):
            cx, cy, cz = corners[c]
            step = x - cx
            inside = jnp.logical_and(step >= 0, step < 8)
            big = jnp.clip(step, 0, 7)
            dy = row - cy
            dz = lane - cz
            in_y = jnp.logical_and(dy >= 0, dy < 8)
            in_z = jnp.logical_and(dz >= 0, dz < 8)
            near = jnp.where(dy == -1, 4, jnp.where(dy == 8, 5, 0))
            side = jnp.where(dz == -1, 6, jnp.where(dz == 8, 7, 0))
            plain = jnp.where(
                inside, 1, jnp.where(step == -1, 2, jnp.where(step == 8, 3, 0))
            )
            kind_main = jnp.where(
                jnp.logical_and(in_y, in_z),
                plain,
                jnp.where(
                    inside,
                    jnp.where(in_z, near, jnp.where(in_y, side, 0)),
                    0,
                ),
            )
            ys = jnp.clip(dy, 0, 7)
            zs = jnp.clip(dz, 0, 7)
            main_base = jnp.where(
                inside, (big % 2) * 64, jnp.where(step == 8, 64, 0)
            )
            main_row = jnp.where(inside, 3 + big // 2, 0)
            y_rows = near > 0
            first = jnp.where(
                y_rows,
                jnp.where(near == 5, 64, 0) + big * 8 + zs,
                main_base + ys * 8 + zs,
            )
            ends = jnp.where(side == 7, 64, 0) + big * 8 + ys
            use_end = kind_main >= 6
            used = kind_main > 0
            kind = jnp.where(used, kind_main, kind)
            for f in range(FIELDS):
                main = jnp.broadcast_to(answers[c, pl.ds(7 * f + main_row, 1), :], (16, 128))
                y_face = jnp.broadcast_to(answers[c, 7 * f + 1 : 7 * f + 2, :], (16, 128))
                z_face = jnp.broadcast_to(answers[c, 7 * f + 2 : 7 * f + 3, :], (16, 128))
                v = pick(jnp.where(y_rows, y_face, main), first)
                v = jnp.where(use_end, pick(z_face, ends), v)
                values[f] = jnp.where(used, v, values[f])
        factor = jnp.where(kind < 2, 0.0, jnp.where(kind % 2 == 0, -COURANT, COURANT))
        for f in range(FIELDS):
            flux = jnp.where(
                kind < 4,
                jnp.where(kind == 2, x_face[f, x + 1], x_face[f, x]),
                jnp.where(
                    kind < 6,
                    jnp.where(kind == 4, y_high[f, x], y_low[f, x]),
                    jnp.where(kind == 6, z_high[f, x], z_low[f, x]),
                ),
            )
            plain = new[f, x]
            ring = plain + factor * (0.0625 * values[f] - 0.5 * flux)
            v = jnp.where(kind == 0, plain, jnp.where(kind == 1, 0.125 * values[f], ring))
            out[f, x] = v[:, :64]
        return 0

    lax.fori_loop(0, 16, one, 0)


def whole(
    sizes,
    parent_ref,
    corner_ref,
    coarse_ref,
    fine_ref,
    coarse_out,
    fine_out,
    block,
    new,
    x_face,
    y_low,
    y_high,
    z_low,
    z_high,
    y_stage,
    z_stage,
    x_rim,
    y_rim,
    z_rim,
    cut,
    rim_out,
    rim_in_old,
    rim_in_mid,
    rim,
    box,
    half,
    reg,
    row_stage,
    answer_out,
    answer_in,
    answers,
    table,
    halo_send,
    halo_recv,
    many_send,
    many_recv,
):
    n_gx, n_gy, n_gz = sizes
    members = n_gy * n_gz
    rim_in = (rim_in_old, rim_in_mid)
    gx = lax.axis_index("gx")
    gy = lax.axis_index("gy")
    gz = lax.axis_index("gz")
    within = gy * n_gz + gz
    myself = gx * members + within
    start = gx * (members * BOXMAX)

    def peer(distance):
        other = lax.rem(within + distance, members)
        return other, (gx, other // n_gz, lax.rem(other, n_gz))

    barrier = pltpu.get_barrier_semaphore()

    def greet(distance, _):
        pl.semaphore_signal(barrier, inc=1, device_id=peer(distance)[1], device_id_type=MESH)
        return 0

    lax.fori_loop(1, members, greet, 0)
    x_next = (lax.rem(gx + 1, n_gx), gy, gz)
    x_prev = (lax.rem(gx + n_gx - 1, n_gx), gy, gz)
    y_next = (gx, lax.rem(gy + 1, n_gy), gz)
    y_prev = (gx, lax.rem(gy + n_gy - 1, n_gy), gz)
    z_next = (gx, gy, lax.rem(gz + 1, n_gz))
    z_prev = (gx, gy, lax.rem(gz + n_gz - 1, n_gz))
    pl.semaphore_signal(barrier, inc=1, device_id=x_next, device_id_type=MESH)
    pl.semaphore_signal(barrier, inc=1, device_id=x_prev, device_id_type=MESH)

    def scan(entry, found):
        c0, c1, c2, c3 = found
        hit = parent_ref[start + entry] == myself
        return (
            jnp.where(hit, entry, c0),
            jnp.where(hit, c0, c1),
            jnp.where(hit, c1, c2),
            jnp.where(hit, c2, c3),
        )

    zero = jnp.int32(0)
    children = lax.fori_loop(0, members * BOXMAX, scan, (zero, zero, zero, zero), unroll=8)
    for c in range(REGIONS):
        for k in range(3):
            table[4 * c + k] = jnp.clip(corner_ref[k, start + children[c]], 1, 55 if k == 2 else 7)
    child_peer = [child // BOXMAX for child in children]

    lane16 = iota((16, 128), 1)
    row16 = iota((16, 128), 0)
    for f in range(FIELDS):
        block[f, 1:17, :, 0:64] = coarse_ref[f]
    for f in range(FIELDS):
        y_stage[0, f] = block[f, 1:17, 0, :]
        y_stage[1, f] = block[f, 1:17, 15, :]
        for h in range(2):
            low = jnp.zeros((16, 128), F32)
            high = jnp.zeros((16, 128), F32)
            for x in range(8):
                plane = block[f, 1 + 8 * h + x]
                here = lane16 // 16 == x
                low = jnp.where(here, jnp.broadcast_to(plane[:, 0:1], (16, 128)), low)
                high = jnp.where(here, jnp.broadcast_to(plane[:, 63:64], (16, 128)), high)
            match = row16 == lane16 % 16
            z_stage[0, h, f : f + 1, :] = jnp.sum(
                jnp.where(match, low, 0.0), axis=0, keepdims=True
            )
            z_stage[1, h, f : f + 1, :] = jnp.sum(
                jnp.where(match, high, 0.0), axis=0, keepdims=True
            )

    def cut_all(when, source):
        def one(c, _):
            corner = (table[4 * c], table[4 * c + 1], table[4 * c + 2])

            def put(f, v, line):
                cut[when, c, 3 * f + v : 3 * f + v + 1, :] = line

            cut_rims(source, corner, put)
            return 0

        lax.fori_loop(0, REGIONS, one, 0)

    def copies(outgoing, incoming, index):
        def send(distance, _):
            other, device = peer(distance)
            pltpu.make_async_remote_copy(
                src_ref=outgoing.at[distance - 1],
                dst_ref=incoming.at[distance - 1],
                send_sem=many_send.at[index],
                recv_sem=many_recv.at[index],
                device_id=device,
                device_id_type=MESH,
            ).start()
            return 0

        return send

    def slot_of(other):
        return lax.rem(within - other + 2 * members - 1, members)

    def rank_of(other):
        rank = jnp.where(child_peer[1] == other, 1, 0)
        rank = jnp.where(child_peer[2] == other, 2, rank)
        return jnp.where(child_peer[3] == other, 3, rank)

    def fill_rims(when):
        def fill(distance, _):
            other = lax.rem(within + distance, members)
            rim_out[when, distance - 1] = cut[when, rank_of(other)]
            return 0

        lax.fori_loop(1, members, fill, 0)
        rim_in[when][members - 1] = cut[when, rank_of(within)]

    def wait_many(outgoing, index, semaphores):
        every = outgoing.at[pl.ds(0, members - 1)]
        pltpu.make_async_copy(every, every, semaphores.at[index]).wait()

    cut_all(0, lambda f, x: block[f, x + 1])
    fill_rims(0)

    pl.semaphore_wait(barrier, members + 1)

    def halo(src, dst, index, device):
        copy = pltpu.make_async_remote_copy(
            src_ref=src,
            dst_ref=dst,
            send_sem=halo_send.at[index],
            recv_sem=halo_recv.at[index],
            device_id=device,
            device_id_type=MESH,
        )
        copy.start()
        return copy

    halos = [
        halo(block.at[:, 16], x_rim.at[0], 0, x_next),
        halo(block.at[:, 1], x_rim.at[1], 1, x_prev),
        halo(y_stage.at[1], y_rim.at[0], 2, y_next),
        halo(y_stage.at[0], y_rim.at[1], 3, y_prev),
        halo(z_stage.at[1], z_rim.at[0], 4, z_next),
        halo(z_stage.at[0], z_rim.at[1], 5, z_prev),
    ]
    lax.fori_loop(1, members, copies(rim_out.at[0], rim_in[0], 0), 0)

    for i in range(16):
        for f in range(FIELDS):
            box[f, 1 + i] = fine_ref[f, :, 256 * i : 256 * i + 256]
    for v in range(7 * FIELDS):
        reg[v] = jnp.zeros((BOXMAX, 128), F32)

    for copy in halos:
        copy.wait()
    for f in range(FIELDS):
        block[f, 0] = x_rim[0, f]
        block[f, 17] = x_rim[1, f]
    coarse_step(block, y_rim, z_rim, new, x_face, y_low, y_high, z_low, z_high)
    cut_all(1, lambda f, x: 0.5 * (block[f, x + 1] + new[f, x]))
    fill_rims(1)
    lax.fori_loop(1, members, copies(rim_out.at[1], rim_in[1], 1), 0)

    own = [parent_ref[start + within * BOXMAX + s] for s in range(BOXMAX)]
    own_peer = [lax.rem(jnp.maximum(own[s], 0), members) for s in range(BOXMAX)]
    sub = iota((BOXMAX, 128), 0)
    owner = jnp.zeros((BOXMAX, 128), I32)
    for s in range(BOXMAX):
        owner = jnp.where(sub == s, own[s], owner)
    filled = owner >= 0

    def take_rims(when):
        wait_many(rim_in[when], when, many_recv)
        for s in range(BOXMAX):
            rows = rim_in[when][slot_of(own_peer[s])]
            for v in range(3 * FIELDS):
                rim[v, s : s + 1, :] = rows[v : v + 1, :]

    take_rims(0)

    def put_half(f, plane, h, value):
        half[f, plane + 1, :, 128 * h : 128 * h + 128] = value

    fine_step(box, rim, reg, put_half, False)
    take_rims(1)

    def put_last(f, plane, h, value):
        old = box[f, plane + 1, :, 128 * h : 128 * h + 128]
        where = pl.multiple_of(plane * 256 + h * 128, 128)
        fine_out[f, :, pl.ds(where, 128)] = jnp.where(filled, value, old)

    fine_step(half, rim, reg, put_last, True)

    for s in range(BOXMAX):
        row_stage[s] = reg[:, s, :]

    def pick_row(other):
        found = zero
        for s in range(BOXMAX):
            found = jnp.where(jnp.logical_and(own[s] >= 0, own_peer[s] == other), s, found)
        return found

    def fill_answer(distance, _):
        other = lax.rem(within + distance, members)
        answer_out[distance - 1] = row_stage[pick_row(other)]
        return copies(answer_out, answer_in, 2)(distance, 0)

    lax.fori_loop(1, members, fill_answer, 0)
    answer_in[members - 1] = row_stage[pick_row(within)]
    wait_many(answer_in, 2, many_recv)
    for c in range(REGIONS):
        answers[c] = answer_in[slot_of(child_peer[c])]
    corners = [(table[4 * c], table[4 * c + 1], table[4 * c + 2]) for c in range(REGIONS)]
    settle(corners, answers, new, x_face, y_low, y_high, z_low, z_high, coarse_out)
    wait_many(rim_out.at[0], 0, many_send)
    wait_many(rim_out.at[1], 1, many_send)
    wait_many(answer_out, 2, many_send)


def on_device(sizes, coarse_state, fine_state, slot_parent, slot_corner):
    members = sizes[1] * sizes[2]
    vmem = pl.BlockSpec(memory_space=pltpu.VMEM)
    smem = pl.BlockSpec(memory_space=pltpu.SMEM)
    fine = jnp.transpose(fine_state, (1, 0, 2))
    corner = jnp.transpose(slot_corner, (1, 0))
    field_block = (FIELDS, 16, 16, 128)
    rows = 7 * FIELDS
    coarse_next, fine_next = pl.pallas_call(
        functools.partial(whole, sizes),
        out_shape=(
            jax.ShapeDtypeStruct(coarse_state.shape, F32),
            jax.ShapeDtypeStruct(fine.shape, F32),
        ),
        in_specs=[smem, smem, vmem, vmem],
        out_specs=(vmem, vmem),
        scratch_shapes=[
            pltpu.VMEM((FIELDS, 18, 16, 128), F32),
            pltpu.VMEM(field_block, F32),
            pltpu.VMEM((FIELDS, 17, 16, 128), F32),
            pltpu.VMEM(field_block, F32),
            pltpu.VMEM(field_block, F32),
            pltpu.VMEM(field_block, F32),
            pltpu.VMEM(field_block, F32),
            pltpu.VMEM((2, FIELDS, 16, 128), F32),
            pltpu.VMEM((2, 2, FIELDS, 128), F32),
            pltpu.VMEM((2, FIELDS, 16, 128), F32),
            pltpu.VMEM((2, FIELDS, 16, 128), F32),
            pltpu.VMEM((2, 2, FIELDS, 128), F32),
            pltpu.VMEM((2, REGIONS, 3 * FIELDS, 128), F32),
            pltpu.VMEM((2, members, 3 * FIELDS, 128), F32),
            pltpu.VMEM((members, 3 * FIELDS, 128), F32),
            pltpu.VMEM((members, 3 * FIELDS, 128), F32),
            pltpu.VMEM((3 * FIELDS, BOXMAX, 128), F32),
            pltpu.VMEM((FIELDS, 18, BOXMAX, 256), F32),
            pltpu.VMEM((FIELDS, 18, BOXMAX, 256), F32),
            pltpu.VMEM((rows, BOXMAX, 128), F32),
            pltpu.VMEM((BOXMAX, rows, 128), F32),
            pltpu.VMEM((members, rows, 128), F32),
            pltpu.VMEM((members, rows, 128), F32),
            pltpu.VMEM((REGIONS, rows, 128), F32),
            pltpu.SMEM((4 * REGIONS,), I32),
            pltpu.SemaphoreType.DMA((6,)),
            pltpu.SemaphoreType.DMA((6,)),
            pltpu.SemaphoreType.DMA((3,)),
            pltpu.SemaphoreType.DMA((3,)),
        ],
        compiler_params=pltpu.CompilerParams(
            collective_id=0, has_side_effects=True, vmem_limit_bytes=48 * 1024 * 1024
        ),
    )(slot_parent, corner, coarse_state, fine)
    return coarse_next, jnp.transpose(fine_next, (1, 0, 2))


def solution(mesh):
    sizes = tuple(mesh.shape[name] for name in ("gx", "gy", "gz"))
    return jax.shard_map(
        functools.partial(on_device, sizes),
        mesh=mesh,
        in_specs=(P(None, "gx", "gy", "gz"), P(("gx", "gy", "gz"), None, None), P(), P()),
        out_specs=(P(None, "gx", "gy", "gz"), P(("gx", "gy", "gz"), None, None)),
        check_vma=False,
    )
```

time: 1810 us -> 60.4 us (0.03)
  local copies, waits for them, and re-layouts: 1460 us -> 5.3 us
  other arithmetic: 159 us -> 0 us
  loops' own time: 80.2 us -> 0 us
  Pallas kernels: 0 us -> 53.7 us
  starting transfers between devices: 40.5 us -> 0 us
  blocking collectives: 33.1 us -> 0 us
  waiting for transfers between devices: 19.3 us -> 0 us
    scatter x104 -> x0, local copies, waits for them, and re-layouts: 938 us -> none  [the longest x16 263 us: ghost_box(): padded = padded.at[:, 1:-1, 1:-1, -1].set(widen_face(end_cells[:, 1]))]
    dynamic_update_slice x48 -> x0, local copies, waits for them, and re-layouts: 103 us -> none  [the longest x8 87.8 us: settle_child(): return lax.dynamic_update_slice(coarse_out, settled, starts)]
    scatter-add x24 -> x0, local copies, waits for them, and re-layouts: 89.4 us -> none  [the longest x4 24.4 us: settle(): patch = patch.at[:, 0, 1:-1, 1:-1].add(-side_fix[:, 0])]
    another operation x5 -> x0, loops' own time: 80.2 us -> none  [the longest x1 38 us: owner_first(): return lax.fori_loop(jnp.int32(0), filled, advance_slot, initial)]
    slice x193 -> x0, local copies, waits for them, and re-layouts: 80.1 us -> none  [the longest x32 29.8 us: boundary_faces(): along_z[:, :, :, 0]]
    another operation x115 -> x0, local copies, waits for them, and re-layouts: 78.6 us -> none
    pallas_call x0 -> x1, Pallas kernels: none -> 53.7 us  [on_device(): pl.pallas_call(functools.partial(whole, sizes), out_shape=(jax.ShapeDtype...]
    gather x37 -> x0, local copies, waits for them, and re-layouts: 41.3 us -> none
  transfers between devices with their start and end apart: 11 -> 0, of which waited for: 4 -> 0; matrix products, arithmetic and copies ran while one was open for 40% -> 0% of each run, Pallas kernels for 0% -> 0%
where the time goes in v1:
time: 60.4 us; the launch traced here: 59.6 us
  Pallas kernels  53.7 us (89%)
  local copies, waits for them, and re-layouts  5.3 us (9%)
  between operations  0.65 us (1%)
    pallas_call x1, Pallas kernels, on_device(): pl.pallas_call(functools.partial(whole, sizes), out_shape=(jax.ShapeDtype...  53.7 us
    unnamed x10, local copies, waits for them, and re-layouts  5.3 us

profile of v1, /device:TPU:4, one launch (start us, length us, event | category | flops | bytes accessed | tf_op | source)
XLA Modules:
  0.0 59.6 jit_solution(2716475419080554578)
XLA Ops:
  0.6 0.0 copy-start
  0.6 1.1 %copy-done = f32[5,16,16,64]{3,2,1,0:T(8,128)S(1)} copy-done((f32[5,16,16,64]{3,2,1,0:T(8,128)S(1)}, f32[5,16,16,64]{3,2,1,0:T(8,128)}, u32[]{:S(2)}) %copy-start) | copy-done | bytes 327704
  1.7 0.0 copy-start.1
  1.7 1.1 %copy-done.1 = f32[8,5,4096]{2,0,1:T(8,128)S(1)} copy-done((f32[8,5,4096]{2,0,1:T(8,128)S(1)}, f32[8,5,4096]{2,0,1:T(8,128)}, u32[]{:S(2)}) %copy-start.1) | copy-done | bytes 655384
  2.8 0.0 copy-start.2
  2.8 0.8 %copy-done.2 = s32[2048,3]{0,1:T(4,128)S(1)} copy-done((s32[2048,3]{0,1:T(4,128)S(1)}, s32[2048,3]{0,1:T(4,128)}, u32[]{:S(2)}) %copy-start.2) | copy-done | bytes 24600
  3.6 0.0 copy-start.3
  3.6 0.7 %copy-done.3 = s32[2048]{0:T(1024)S(1)} copy-done((s32[2048]{0:T(1024)S(1)}, s32[2048]{0:T(1024)}, u32[]{:S(2)}) %copy-start.3) | copy-done | bytes 8216
  4.3 53.7 %shard_map.59 = (f32[5,16,16,64]{3,2,1,0:T(8,128)S(1)}, f32[5,8,4096]{2,1,0:T(8,128)S(1)}) custom-call(s32[2048]{0:T(1024)S(1)} %copy-done.3, s32[3,2048]{1,0:T(4,128)S(1)} %bitcast.5, f32[5,16,16,64]{3,2,1,0:T(8,128)S(1)} %copy-done, f32[5,8,4096]{2,1,0:T(8,128)S(1)} %bitcast.3), custom_call_target="tpu_custom_call" | custom-call | tf_op jit(solution)/shard_map/pallas_call | solution.py:651
  58.0 0.8 %copy.8 = f32[5,16,16,64]{3,2,1,0:T(8,128)} copy(f32[5,16,16,64]{3,2,1,0:T(8,128)S(1)} %get-tuple-element.8) | data formatting | bytes 655360
  58.8 0.8 %copy.9 = f32[8,5,4096]{2,0,1:T(8,128)} copy(f32[8,5,4096]{2,0,1:T(8,128)S(1)} %bitcast.4) | data formatting | bytes 1310720
Async XLA Ops:
  0.6 1.1 %copy-start = (f32[5,16,16,64]{3,2,1,0:T(8,128)S(1)}, f32[5,16,16,64]{3,2,1,0:T(8,128)}, u32[]{:S(2)}) copy-start(f32[5,16,16,64]{3,2,1,0:T(8,128)} %coarse_ref.1) | copy-start | bytes 983044
  1.7 1.1 %copy-start.1 = (f32[8,5,4096]{2,0,1:T(8,128)S(1)}, f32[8,5,4096]{2,0,1:T(8,128)}, u32[]{:S(2)}) copy-start(f32[8,5,4096]{2,0,1:T(8,128)} %param.5) | copy-start | bytes 1966084
  2.8 0.8 %copy-start.2 = (s32[2048,3]{0,1:T(4,128)S(1)}, s32[2048,3]{0,1:T(4,128)}, u32[]{:S(2)}) copy-start(s32[2048,3]{0,1:T(4,128)} %param.7) | copy-start | bytes 73732
  3.6 0.7 %copy-start.3 = (s32[2048]{0:T(1024)S(1)}, s32[2048]{0:T(1024)}, u32[]{:S(2)}) copy-start(s32[2048]{0:T(1024)} %parent_ref.1) | copy-start | bytes 24580

commit v2 on v1

--- a/solution.py
+++ b/solution.py
@@ -39,10 +39,12 @@
 
 
 def prims(q):
-    inverse = 1.0 / q[0]
+    inverse = pl.reciprocal(q[0], approx=True)
+    inverse = inverse * (2.0 - q[0] * inverse)
     kinetic = 0.5 * (q[1] * q[1] + q[2] * q[2] + q[3] * q[3]) * inverse
     pressure = (GAMMA - 1.0) * (q[4] - kinetic)
-    sound = jnp.sqrt(GAMMA * pressure * inverse)
+    square = GAMMA * pressure * inverse
+    sound = square * lax.rsqrt(jnp.maximum(square, 1e-30))
     return inverse, pressure, sound, q[4] + pressure
 
 
@@ -65,7 +67,7 @@
     return [move(v) for v in q], [move(v) for v in terms[0]], move(terms[1])
 
 
-def fine_step(box, rim, reg, put, second):
+def fine_step(box, rim, reg, filled, put, second, done=None):
     lane = iota((BOXMAX, 128), 1)
     first_row = lane < 16
     last_row = lane >= 112
@@ -112,7 +114,7 @@
                 v = v + roll(v, -16)
                 out.append(pick(v, squeeze))
             both = jnp.where((lane % 64) < 32, out[0], out[1])
-            mine = (lane < 64) if side == 0 else (lane >= 64)
+            mine = jnp.logical_and(filled, (lane < 64) if side == 0 else (lane >= 64))
             reg[7 * f] = reg[7 * f] + jnp.where(mine, both, 0.0)
 
     x_register(x_low, 0)
@@ -196,7 +198,7 @@
                         new_sum[h][f] = accumulate(new_sum[h][f], new)
             here, here_prim, x_low = after, after_prim, x_high
 
-        mine = part == big
+        mine = jnp.logical_and(filled, part == big)
         y_from = (lane % 8) * 2 + jnp.where(lane >= 64, 112, 0)
         z_from = (lane % 4) * 32 + jnp.where(lane >= 64, 15, 0)
         for f in range(FIELDS):
@@ -216,8 +218,11 @@
                     v = v + roll(v, -16)
                     out.append(pick(v, squeeze))
                 v = jnp.where((lane % 64) < 32, out[0], out[1])
+                v = jnp.where(filled, v, 0.0)
                 where = 7 * f + 3 + big // 2
                 reg[where] = jnp.where(lane // 64 == big % 2, v, reg[where])
+        if second:
+            done(big)
         return here, here_prim, x_low
 
     last = lax.fori_loop(0, 8, pair, (here, here_prim, x_low))
@@ -230,7 +235,15 @@
     tip = iota((8, 128), 0)
 
     def load(plane):
-        return [block[f, plane] for f in range(FIELDS)]
+        x = jnp.clip(plane - 1, 0, 15)
+        column = (x % 8) * 16 + row
+        cells = []
+        for f in range(FIELDS):
+            below = jnp.broadcast_to(z_rim[0, x // 8, f : f + 1, :], (16, 128))
+            above = jnp.broadcast_to(z_rim[1, x // 8, f : f + 1, :], (16, 128))
+            side = jnp.where(lane == 64, pick(above, column), pick(below, column))
+            cells.append(jnp.where(lane < 64, block[f, plane], side))
+        return cells
 
     ghost = load(0)
     here = load(1)
@@ -246,8 +259,6 @@
         x_high = face(here, along(here, here_prim, 0), after, along(after, after_prim, 0))
 
         tips = []
-        wide = []
-        column = (x % 8) * 16 + row
         for f in range(FIELDS):
             above = y_rim[1, f, pl.ds(x, 1), :]
             below = y_rim[0, f, pl.ds(x, 1), :]
@@ -258,19 +269,20 @@
                     jnp.broadcast_to(below, (8, 128)),
                 )
             )
-            below = jnp.broadcast_to(z_rim[0, x // 8, f : f + 1, :], (16, 128))
-            above = jnp.broadcast_to(z_rim[1, x // 8, f : f + 1, :], (16, 128))
-            side = jnp.where(lane == 64, pick(above, column), pick(below, column))
-            wide.append(jnp.where(lane < 64, here[f], side))
-
-        tall = [jnp.concatenate([here[f], tips[f]], axis=0) for f in range(FIELDS)]
-        terms = along(tall, prims(tall), 1)
-        shifted = moved(tall, terms, lambda v: pltpu.roll(v, 1, 0))
-        y = face(shifted[0], (shifted[1], shifted[2]), tall, terms)
-
-        terms = along(wide, prims(wide), 2)
-        shifted = moved(wide, terms, lambda v: pltpu.roll(v, 1, 1))
-        z = face(shifted[0], (shifted[1], shifted[2]), wide, terms)
+        tip_terms = along(tips, prims(tips), 1)
+        terms = along(here, here_prim, 1)
+
+        def tall(low, high):
+            return jnp.concatenate([low, high], axis=0)
+
+        cells = [tall(here[f], tips[f]) for f in range(FIELDS)]
+        terms = ([tall(terms[0][f], tip_terms[0][f]) for f in range(FIELDS)], tall(terms[1], tip_terms[1]))
+        shifted = moved(cells, terms, lambda v: pltpu.roll(v, 1, 0))
+        y = face(shifted[0], (shifted[1], shifted[2]), cells, terms)
+
+        terms = along(here, here_prim, 2)
+        shifted = moved(here, terms, lambda v: pltpu.roll(v, 1, 1))
+        z = face(shifted[0], (shifted[1], shifted[2]), here, terms)
         for f in range(FIELDS):
             up = pltpu.roll(y[f], 23, 0)[:16]
             down = y[f][:16]
@@ -312,12 +324,11 @@
         put(f, 2, jnp.sum(jnp.where(rows_z, z_total, 0.0), axis=0, keepdims=True))
 
 
-def settle(corners, answers, new, x_face, y_low, y_high, z_low, z_high, out):
+def plan_settle(corners, new, x_face, y_low, y_high, z_low, z_high, weight, index):
     lane = iota((16, 128), 1)
     row = iota((16, 128), 0)
 
     def one(x, _):
-        values = [jnp.zeros((16, 128), F32) for _ in range(FIELDS)]
         kind = jnp.zeros((16, 128), I32)
         for c in range(REGIONS):
             cx, cy, cz = corners[c]
@@ -330,42 +341,27 @@
             in_z = jnp.logical_and(dz >= 0, dz < 8)
             near = jnp.where(dy == -1, 4, jnp.where(dy == 8, 5, 0))
             side = jnp.where(dz == -1, 6, jnp.where(dz == 8, 7, 0))
-            plain = jnp.where(
-                inside, 1, jnp.where(step == -1, 2, jnp.where(step == 8, 3, 0))
-            )
-            kind_main = jnp.where(
+            plain = jnp.where(inside, 1, jnp.where(step == -1, 2, jnp.where(step == 8, 3, 0)))
+            mine = jnp.where(
                 jnp.logical_and(in_y, in_z),
                 plain,
-                jnp.where(
-                    inside,
-                    jnp.where(in_z, near, jnp.where(in_y, side, 0)),
-                    0,
-                ),
+                jnp.where(inside, jnp.where(in_z, near, jnp.where(in_y, side, 0)), 0),
             )
             ys = jnp.clip(dy, 0, 7)
             zs = jnp.clip(dz, 0, 7)
-            main_base = jnp.where(
-                inside, (big % 2) * 64, jnp.where(step == 8, 64, 0)
-            )
-            main_row = jnp.where(inside, 3 + big // 2, 0)
-            y_rows = near > 0
+            base = jnp.where(inside, (big % 2) * 64, jnp.where(step == 8, 64, 0))
             first = jnp.where(
-                y_rows,
+                near > 0,
                 jnp.where(near == 5, 64, 0) + big * 8 + zs,
-                main_base + ys * 8 + zs,
+                base + ys * 8 + zs,
             )
             ends = jnp.where(side == 7, 64, 0) + big * 8 + ys
-            use_end = kind_main >= 6
-            used = kind_main > 0
-            kind = jnp.where(used, kind_main, kind)
-            for f in range(FIELDS):
-                main = jnp.broadcast_to(answers[c, pl.ds(7 * f + main_row, 1), :], (16, 128))
-                y_face = jnp.broadcast_to(answers[c, 7 * f + 1 : 7 * f + 2, :], (16, 128))
-                z_face = jnp.broadcast_to(answers[c, 7 * f + 2 : 7 * f + 3, :], (16, 128))
-                v = pick(jnp.where(y_rows, y_face, main), first)
-                v = jnp.where(use_end, pick(z_face, ends), v)
-                values[f] = jnp.where(used, v, values[f])
+            used = mine > 0
+            kind = jnp.where(used, mine, kind)
+            index[x, c, 0] = first + jnp.where(used, 128, 0)
+            index[x, c, 1] = ends + jnp.where(mine >= 6, 128, 0)
         factor = jnp.where(kind < 2, 0.0, jnp.where(kind % 2 == 0, -COURANT, COURANT))
+        weight[x] = jnp.where(kind == 1, 0.125, 0.0625 * factor)
         for f in range(FIELDS):
             flux = jnp.where(
                 kind < 4,
@@ -377,8 +373,40 @@
                 ),
             )
             plain = new[f, x]
-            ring = plain + factor * (0.0625 * values[f] - 0.5 * flux)
-            v = jnp.where(kind == 0, plain, jnp.where(kind == 1, 0.125 * values[f], ring))
+            ring = jnp.where(kind >= 2, plain - 0.5 * factor * flux, plain)
+            new[f, x] = jnp.where(kind == 1, 0.0, ring)
+        return 0
+
+    lax.fori_loop(0, 16, one, 0)
+
+
+def settle(corners, answers, new, weight, index, out):
+    row = iota((16, 128), 0)
+    y_rows = [
+        jnp.logical_or(row == corners[c][1] - 1, row == corners[c][1] + 8) for c in range(REGIONS)
+    ]
+
+    def one(x, _):
+        values = [jnp.zeros((16, 128), F32) for _ in range(FIELDS)]
+        for c in range(REGIONS):
+            step = x - corners[c][0]
+            inside = jnp.logical_and(step >= 0, step < 8)
+            main_row = jnp.where(inside, 3 + jnp.clip(step, 0, 7) // 2, 0)
+            first = index[x, c, 0]
+            ends = index[x, c, 1]
+            used = first >= 128
+            use_end = ends >= 128
+            first = first & 127
+            ends = ends & 127
+            for f in range(FIELDS):
+                main = jnp.broadcast_to(answers[7 * f + main_row, c : c + 1, :], (16, 128))
+                y_face = jnp.broadcast_to(answers[7 * f + 1, c : c + 1, :], (16, 128))
+                z_face = jnp.broadcast_to(answers[7 * f + 2, c : c + 1, :], (16, 128))
+                v = pick(jnp.where(y_rows[c], y_face, main), first)
+                v = jnp.where(use_end, pick(z_face, ends), v)
+                values[f] = jnp.where(used, v, values[f])
+        for f in range(FIELDS):
+            v = new[f, x] + weight[x] * values[f]
             out[f, x] = v[:, :64]
         return 0
 
@@ -387,12 +415,17 @@
 
 def whole(
     sizes,
+    parent_hbm,
+    plane_hbm,
+    corner_hbm,
+    coarse_hbm,
+    fine_hbm,
+    coarse_out,
+    fine_out,
     parent_ref,
     corner_ref,
+    plane_ref,
     coarse_ref,
-    fine_ref,
-    coarse_out,
-    fine_out,
     block,
     new,
     x_face,
@@ -400,6 +433,8 @@
     y_high,
     z_low,
     z_high,
+    weight,
+    index,
     y_stage,
     z_stage,
     x_rim,
@@ -410,14 +445,20 @@
     rim_in_old,
     rim_in_mid,
     rim,
+    fine_ref,
     box,
     half,
     reg,
+    route,
+    relay_in,
+    relay_out,
     row_stage,
-    answer_out,
+    direct_out,
+    direct_in,
     answer_in,
     answers,
     table,
+    load_sems,
     halo_send,
     halo_recv,
     many_send,
@@ -425,6 +466,8 @@
 ):
     n_gx, n_gy, n_gz = sizes
     members = n_gy * n_gz
+    relayed = min(members, 7 * FIELDS)
+    direct = 7 * FIELDS - relayed
     rim_in = (rim_in_old, rim_in_mid)
     gx = lax.axis_index("gx")
     gy = lax.axis_index("gy")
@@ -443,7 +486,6 @@
         pl.semaphore_signal(barrier, inc=1, device_id=peer(distance)[1], device_id_type=MESH)
         return 0
 
-    lax.fori_loop(1, members, greet, 0)
     x_next = (lax.rem(gx + 1, n_gx), gy, gz)
     x_prev = (lax.rem(gx + n_gx - 1, n_gx), gy, gz)
     y_next = (gx, lax.rem(gy + 1, n_gy), gz)
@@ -452,26 +494,22 @@
     z_prev = (gx, gy, lax.rem(gz + n_gz - 1, n_gz))
     pl.semaphore_signal(barrier, inc=1, device_id=x_next, device_id_type=MESH)
     pl.semaphore_signal(barrier, inc=1, device_id=x_prev, device_id_type=MESH)
-
-    def scan(entry, found):
-        c0, c1, c2, c3 = found
-        hit = parent_ref[start + entry] == myself
-        return (
-            jnp.where(hit, entry, c0),
-            jnp.where(hit, c0, c1),
-            jnp.where(hit, c1, c2),
-            jnp.where(hit, c2, c3),
-        )
-
-    zero = jnp.int32(0)
-    children = lax.fori_loop(0, members * BOXMAX, scan, (zero, zero, zero, zero), unroll=8)
-    for c in range(REGIONS):
-        for k in range(3):
-            table[4 * c + k] = jnp.clip(corner_ref[k, start + children[c]], 1, 55 if k == 2 else 7)
-    child_peer = [child // BOXMAX for child in children]
+    lax.fori_loop(1, members, greet, 0)
+
+    def fetch(src, dst, index):
+        copy = pltpu.make_async_copy(src, dst, load_sems.at[index])
+        copy.start()
+        return copy
+
+    coarse_load = fetch(coarse_hbm, coarse_ref, 0)
+    parent_load = fetch(parent_hbm, parent_ref, 1)
+    corner_load = fetch(corner_hbm, corner_ref, 2)
+    plane_load = fetch(plane_hbm, plane_ref, 3)
+    fine_load = fetch(fine_hbm, fine_ref, 4)
 
     lane16 = iota((16, 128), 1)
     row16 = iota((16, 128), 0)
+    coarse_load.wait()
     for f in range(FIELDS):
         block[f, 1:17, :, 0:64] = coarse_ref[f]
     for f in range(FIELDS):
@@ -493,57 +531,6 @@
                 jnp.where(match, high, 0.0), axis=0, keepdims=True
             )
 
-    def cut_all(when, source):
-        def one(c, _):
-            corner = (table[4 * c], table[4 * c + 1], table[4 * c + 2])
-
-            def put(f, v, line):
-                cut[when, c, 3 * f + v : 3 * f + v + 1, :] = line
-
-            cut_rims(source, corner, put)
-            return 0
-
-        lax.fori_loop(0, REGIONS, one, 0)
-
-    def copies(outgoing, incoming, index):
-        def send(distance, _):
-            other, device = peer(distance)
-            pltpu.make_async_remote_copy(
-                src_ref=outgoing.at[distance - 1],
-                dst_ref=incoming.at[distance - 1],
-                send_sem=many_send.at[index],
-                recv_sem=many_recv.at[index],
-                device_id=device,
-                device_id_type=MESH,
-            ).start()
-            return 0
-
-        return send
-
-    def slot_of(other):
-        return lax.rem(within - other + 2 * members - 1, members)
-
-    def rank_of(other):
-        rank = jnp.where(child_peer[1] == other, 1, 0)
-        rank = jnp.where(child_peer[2] == other, 2, rank)
-        return jnp.where(child_peer[3] == other, 3, rank)
-
-    def fill_rims(when):
-        def fill(distance, _):
-            other = lax.rem(within + distance, members)
-            rim_out[when, distance - 1] = cut[when, rank_of(other)]
-            return 0
-
-        lax.fori_loop(1, members, fill, 0)
-        rim_in[when][members - 1] = cut[when, rank_of(within)]
-
-    def wait_many(outgoing, index, semaphores):
-        every = outgoing.at[pl.ds(0, members - 1)]
-        pltpu.make_async_copy(every, every, semaphores.at[index]).wait()
-
-    cut_all(0, lambda f, x: block[f, x + 1])
-    fill_rims(0)
-
     pl.semaphore_wait(barrier, members + 1)
 
     def halo(src, dst, index, device):
@@ -566,8 +553,118 @@
         halo(z_stage.at[1], z_rim.at[0], 4, z_next),
         halo(z_stage.at[0], z_rim.at[1], 5, z_prev),
     ]
-    lax.fori_loop(1, members, copies(rim_out.at[0], rim_in[0], 0), 0)
-
+
+    parent_load.wait()
+    corner_load.wait()
+
+    def scan(entry, found):
+        c0, c1, c2, c3 = found
+        hit = parent_ref[start + entry] == myself
+        return (
+            jnp.where(hit, c1, c0),
+            jnp.where(hit, c2, c1),
+            jnp.where(hit, c3, c2),
+            jnp.where(hit, entry, c3),
+        )
+
+    zero = jnp.int32(0)
+    children = lax.fori_loop(0, members * BOXMAX, scan, (zero, zero, zero, zero), unroll=8)
+    for c in range(REGIONS):
+        for k in range(3):
+            table[4 * c + k] = jnp.clip(corner_ref[k, start + children[c]], 1, 55 if k == 2 else 7)
+    child_peer = [child // BOXMAX for child in children]
+    own = [parent_ref[start + within * BOXMAX + s] for s in range(BOXMAX)]
+    own_peer = [lax.rem(jnp.maximum(own[s], 0), members) for s in range(BOXMAX)]
+
+    def look_up(distance, _):
+        other = lax.rem(within + distance, members)
+        rank = zero
+        for c in range(1, REGIONS):
+            rank = jnp.where(child_peer[c] == other, c, rank)
+        found = zero
+        for s in range(BOXMAX):
+            found = jnp.where(jnp.logical_and(own[s] >= 0, own_peer[s] == other), s, found)
+        table[32 + distance] = rank
+        table[32 + members + distance] = found
+        return 0
+
+    lax.fori_loop(0, members, look_up, 0)
+
+    def cut_all(when, source):
+        def one(c, _):
+            corner = (table[4 * c], table[4 * c + 1], table[4 * c + 2])
+
+            def put(f, v, line):
+                cut[when, c, 3 * f + v : 3 * f + v + 1, :] = line
+
+            cut_rims(source, corner, put)
+            return 0
+
+        lax.fori_loop(0, REGIONS, one, 0)
+
+    def ship(src, dst, index, device):
+        pltpu.make_async_remote_copy(
+            src_ref=src,
+            dst_ref=dst,
+            send_sem=many_send.at[index],
+            recv_sem=many_recv.at[index],
+            device_id=device,
+            device_id_type=MESH,
+        ).start()
+
+    def slot_of(other):
+        return lax.rem(within - other + 2 * members - 1, members)
+
+    def wait_many(every, index, semaphores):
+        pltpu.make_async_copy(every, every, semaphores.at[index]).wait()
+
+    others = pl.ds(0, members - 1)
+
+    def send_rims(when):
+        def one(distance, _):
+            rim_out[when, distance - 1] = cut[when, table[32 + distance]]
+            ship(
+                rim_out.at[when, distance - 1],
+                rim_in[when].at[distance - 1],
+                when,
+                peer(distance)[1],
+            )
+            return 0
+
+        lax.fori_loop(1, members, one, 0)
+        rim_in[when][members - 1] = cut[when, table[32]]
+
+    cut_all(0, lambda f, x: block[f, x + 1])
+    send_rims(0)
+
+    plane_load.wait()
+    n_rows = REGIONS * members
+    columns = members * BOXMAX
+    row = iota((n_rows, columns), 0)
+    column = iota((n_rows, columns), 1)
+    slots = plane_ref[pl.ds(gx * (columns // 128), columns // 128), :] if columns >= 128 else None
+    if columns >= 128:
+        slots = jnp.concatenate(
+            [
+                jnp.broadcast_to(slots[h : h + 1, :], (n_rows, 128))
+                for h in range(columns // 128)
+            ],
+            axis=1,
+        )
+    else:
+        slots = jnp.broadcast_to(plane_ref[0:1, 0:columns], (n_rows, columns))
+    number = column.astype(F32)
+    far = 65536.0
+    candidate = jnp.where(slots == row // REGIONS + gx * members, number, far)
+    chosen = jnp.full((n_rows, 1), far)
+    for r in range(REGIONS):
+        least = jnp.min(candidate, axis=1, keepdims=True)
+        chosen = jnp.where(row[:, 0:1] % REGIONS == r, least, chosen)
+        candidate = jnp.where(candidate == least, far, candidate)
+    arrival = lax.rem(within - column // BOXMAX - 1 + members, members) * BOXMAX + column % BOXMAX
+    route[...] = jnp.where(arrival.astype(F32) == chosen, 1.0, 0.0)
+
+    fine_load.wait()
     for i in range(16):
         for f in range(FIELDS):
             box[f, 1 + i] = fine_ref[f, :, 256 * i : 256 * i + 256]
@@ -581,11 +678,8 @@
         block[f, 17] = x_rim[1, f]
     coarse_step(block, y_rim, z_rim, new, x_face, y_low, y_high, z_low, z_high)
     cut_all(1, lambda f, x: 0.5 * (block[f, x + 1] + new[f, x]))
-    fill_rims(1)
-    lax.fori_loop(1, members, copies(rim_out.at[1], rim_in[1], 1), 0)
-
-    own = [parent_ref[start + within * BOXMAX + s] for s in range(BOXMAX)]
-    own_peer = [lax.rem(jnp.maximum(own[s], 0), members) for s in range(BOXMAX)]
+    send_rims(1)
+
     sub = iota((BOXMAX, 128), 0)
     owner = jnp.zeros((BOXMAX, 128), I32)
     for s in range(BOXMAX):
@@ -593,7 +687,7 @@
     filled = owner >= 0
 
     def take_rims(when):
-        wait_many(rim_in[when], when, many_recv)
+        wait_many(rim_in[when].at[others], when, many_recv)
         for s in range(BOXMAX):
             rows = rim_in[when][slot_of(own_peer[s])]
             for v in range(3 * FIELDS):
@@ -604,7 +698,7 @@
     def put_half(f, plane, h, value):
         half[f, plane + 1, :, 128 * h : 128 * h + 128] = value
 
-    fine_step(box, rim, reg, put_half, False)
+    fine_step(box, rim, reg, filled, put_half, False)
     take_rims(1)
 
     def put_last(f, plane, h, value):
@@ -612,51 +706,100 @@
         where = pl.multiple_of(plane * 256 + h * 128, 128)
         fine_out[f, :, pl.ds(where, 128)] = jnp.where(filled, value, old)
 
-    fine_step(half, rim, reg, put_last, True)
-
-    for s in range(BOXMAX):
-        row_stage[s] = reg[:, s, :]
-
-    def pick_row(other):
-        found = zero
+    def relay(tile):
+        @pl.when(jnp.logical_and(tile != within, tile < relayed))
+        def _():
+            distance = lax.rem(tile - within + members, members)
+            device = (gx, tile // n_gz, lax.rem(tile, n_gz))
+            ship(reg.at[tile], relay_in.at[distance - 1], 2, device)
+
+    def relay_ready(big):
+        @pl.when(big % 2 == 1)
+        def _():
+            for f in range(FIELDS):
+                relay(7 * f + 3 + big // 2)
+
+    fine_step(half, rim, reg, filled, put_last, True, relay_ready)
+    for f in range(FIELDS):
+        for v in range(3):
+            relay(7 * f + v)
+    relay_in[members - 1] = reg[within]
+
+    if direct:
         for s in range(BOXMAX):
-            found = jnp.where(jnp.logical_and(own[s] >= 0, own_peer[s] == other), s, found)
-        return found
-
-    def fill_answer(distance, _):
-        other = lax.rem(within + distance, members)
-        answer_out[distance - 1] = row_stage[pick_row(other)]
-        return copies(answer_out, answer_in, 2)(distance, 0)
-
-    lax.fori_loop(1, members, fill_answer, 0)
-    answer_in[members - 1] = row_stage[pick_row(within)]
-    wait_many(answer_in, 2, many_recv)
-    for c in range(REGIONS):
-        answers[c] = answer_in[slot_of(child_peer[c])]
+            row_stage[s] = reg[relayed:, s, :]
+
+        def direct_one(distance, _):
+            direct_out[distance - 1] = row_stage[table[32 + members + distance]]
+            ship(direct_out.at[distance - 1], direct_in.at[distance - 1], 3, peer(distance)[1])
+            return 0
+
+        lax.fori_loop(1, members, direct_one, 0)
+        direct_in[members - 1] = row_stage[table[32 + members]]
+
+    wait_many(relay_in.at[others], 2, many_recv)
+    sorted_rows = jnp.dot(
+        route[...],
+        relay_in[...].reshape(columns, 128),
+        precision=lax.Precision.HIGHEST,
+        preferred_element_type=F32,
+    )
+    for p in range(members):
+        relay_out[p] = sorted_rows[REGIONS * p : REGIONS * p + REGIONS]
+
+    def answer_one(distance, _):
+        other, device = peer(distance)
+        ship(relay_out.at[other], answer_in.at[distance - 1], 4, device)
+        return 0
+
+    lax.fori_loop(1, members, answer_one, 0)
+    answer_in[members - 1] = relay_out[within]
+
     corners = [(table[4 * c], table[4 * c + 1], table[4 * c + 2]) for c in range(REGIONS)]
-    settle(corners, answers, new, x_face, y_low, y_high, z_low, z_high, coarse_out)
-    wait_many(rim_out.at[0], 0, many_send)
-    wait_many(rim_out.at[1], 1, many_send)
-    wait_many(answer_out, 2, many_send)
+    plan_settle(corners, new, x_face, y_low, y_high, z_low, z_high, weight, index)
+
+    if direct:
+        wait_many(direct_in.at[others], 3, many_recv)
+        for c in range(REGIONS):
+            rows = direct_in[slot_of(child_peer[c])]
+            for v in range(direct):
+                answers[relayed + v, c : c + 1, :] = rows[v : v + 1, :]
+    wait_many(answer_in.at[others], 4, many_recv)
+    for v in range(relayed):
+        answers[v] = answer_in[lax.rem(within - v + 2 * members - 1, members)]
+    settle(corners, answers, new, weight, index, coarse_out)
+    wait_many(rim_out.at[0, others], 0, many_send)
+    wait_many(rim_out.at[1, others], 1, many_send)
+    wait_many(relay_in.at[others], 2, many_send)
+    if direct:
+        wait_many(direct_out.at[others], 3, many_send)
+    wait_many(relay_out.at[others], 4, many_send)
 
 
 def on_device(sizes, coarse_state, fine_state, slot_parent, slot_corner):
     members = sizes[1] * sizes[2]
+    relayed = min(members, 7 * FIELDS)
     vmem = pl.BlockSpec(memory_space=pltpu.VMEM)
-    smem = pl.BlockSpec(memory_space=pltpu.SMEM)
+    hbm = pl.BlockSpec(memory_space=pltpu.HBM)
     fine = jnp.transpose(fine_state, (1, 0, 2))
     corner = jnp.transpose(slot_corner, (1, 0))
+    plane = slot_parent.reshape(-1, min(128, slot_parent.shape[0]))
     field_block = (FIELDS, 16, 16, 128)
     rows = 7 * FIELDS
+    direct = max(rows - relayed, 1)
     coarse_next, fine_next = pl.pallas_call(
         functools.partial(whole, sizes),
         out_shape=(
             jax.ShapeDtypeStruct(coarse_state.shape, F32),
             jax.ShapeDtypeStruct(fine.shape, F32),
         ),
-        in_specs=[smem, smem, vmem, vmem],
+        in_specs=[hbm] * 5,
         out_specs=(vmem, vmem),
         scratch_shapes=[
+            pltpu.SMEM(slot_parent.shape, I32),
+            pltpu.SMEM(corner.shape, I32),
+            pltpu.VMEM(plane.shape, I32),
+            pltpu.VMEM(coarse_state.shape, F32),
             pltpu.VMEM((FIELDS, 18, 16, 128), F32),
             pltpu.VMEM(field_block, F32),
             pltpu.VMEM((FIELDS, 17, 16, 128), F32),
@@ -664,6 +807,8 @@
             pltpu.VMEM(field_block, F32),
             pltpu.VMEM(field_block, F32),
             pltpu.VMEM(field_block, F32),
+            pltpu.VMEM((16, 16, 128), F32),
+            pltpu.VMEM((16, REGIONS, 2, 16, 128), I32),
             pltpu.VMEM((2, FIELDS, 16, 128), F32),
             pltpu.VMEM((2, 2, FIELDS, 128), F32),
             pltpu.VMEM((2, FIELDS, 16, 128), F32),
@@ -674,23 +819,29 @@
             pltpu.VMEM((members, 3 * FIELDS, 128), F32),
             pltpu.VMEM((members, 3 * FIELDS, 128), F32),
             pltpu.VMEM((3 * FIELDS, BOXMAX, 128), F32),
+            pltpu.VMEM(fine.shape, F32),
             pltpu.VMEM((FIELDS, 18, BOXMAX, 256), F32),
             pltpu.VMEM((FIELDS, 18, BOXMAX, 256), F32),
             pltpu.VMEM((rows, BOXMAX, 128), F32),
-            pltpu.VMEM((BOXMAX, rows, 128), F32),
-            pltpu.VMEM((members, rows, 128), F32),
-            pltpu.VMEM((members, rows, 128), F32),
-            pltpu.VMEM((REGIONS, rows, 128), F32),
-            pltpu.SMEM((4 * REGIONS,), I32),
+            pltpu.VMEM((REGIONS * members, BOXMAX * members), F32),
+            pltpu.VMEM((members, BOXMAX, 128), F32),
+            pltpu.VMEM((members, REGIONS, 128), F32),
+            pltpu.VMEM((BOXMAX, direct, 128), F32),
+            pltpu.VMEM((members, direct, 128), F32),
+            pltpu.VMEM((members, direct, 128), F32),
+            pltpu.VMEM((members, REGIONS, 128), F32),
+            pltpu.VMEM((rows, REGIONS, 128), F32),
+            pltpu.SMEM((32 + 2 * members,), I32),
+            pltpu.SemaphoreType.DMA((5,)),
             pltpu.SemaphoreType.DMA((6,)),
             pltpu.SemaphoreType.DMA((6,)),
-            pltpu.SemaphoreType.DMA((3,)),
-            pltpu.SemaphoreType.DMA((3,)),
+            pltpu.SemaphoreType.DMA((5,)),
+            pltpu.SemaphoreType.DMA((5,)),
         ],
         compiler_params=pltpu.CompilerParams(
             collective_id=0, has_side_effects=True, vmem_limit_bytes=48 * 1024 * 1024
         ),
-    )(slot_parent, corner, coarse_state, fine)
+    )(slot_parent, plane, corner, coarse_state, fine)
     return coarse_next, jnp.transpose(fine_next, (1, 0, 2))
 
 

time: 60.4 us -> 55.7 us (0.922)
  Pallas kernels: 53.7 us -> 49.5 us
    pallas_call x1, Pallas kernels: 53.7 us -> 49.5 us  [on_device(): pl.pallas_call(functools.partial(whole, sizes), out_shape=(jax.ShapeDtype...]
where the time goes in v2:
time: 55.7 us; the launch traced here: 55.4 us
  Pallas kernels  49.5 us (89%)
  local copies, waits for them, and re-layouts  5.3 us (10%)
  between operations  0.65 us (1%)
    pallas_call x1, Pallas kernels, on_device(): pl.pallas_call(functools.partial(whole, sizes), out_shape=(jax.ShapeDtype...  49.5 us
    unnamed x10, local copies, waits for them, and re-layouts  5.3 us

profile of v2, /device:TPU:4, one launch (start us, length us, event | category | flops | bytes accessed | tf_op | source)
XLA Modules:
  0.0 55.4 jit_solution(13089050764024117147)
XLA Ops:
  0.6 0.0 copy-start
  0.6 1.1 %copy-done = f32[5,16,16,64]{3,2,1,0:T(8,128)S(1)} copy-done((f32[5,16,16,64]{3,2,1,0:T(8,128)S(1)}, f32[5,16,16,64]{3,2,1,0:T(8,128)}, u32[]{:S(2)}) %copy-start) | copy-done | bytes 327704
  1.7 0.0 copy-start.1
  1.7 1.1 %copy-done.1 = f32[8,5,4096]{2,0,1:T(8,128)S(1)} copy-done((f32[8,5,4096]{2,0,1:T(8,128)S(1)}, f32[8,5,4096]{2,0,1:T(8,128)}, u32[]{:S(2)}) %copy-start.1) | copy-done | bytes 655384
  2.8 0.0 copy-start.2
  2.8 0.7 %copy-done.2 = s32[2048]{0:T(1024)S(1)} copy-done((s32[2048]{0:T(1024)S(1)}, s32[2048]{0:T(1024)}, u32[]{:S(2)}) %copy-start.2) | copy-done | bytes 8216
  3.5 0.0 copy-start.3
  3.5 0.8 %copy-done.3 = s32[2048,3]{0,1:T(4,128)S(1)} copy-done((s32[2048,3]{0,1:T(4,128)S(1)}, s32[2048,3]{0,1:T(4,128)}, u32[]{:S(2)}) %copy-start.3) | copy-done | bytes 24600
  4.3 49.5 %shard_map.59 = (f32[5,16,16,64]{3,2,1,0:T(8,128)S(1)}, f32[5,8,4096]{2,1,0:T(8,128)S(1)}) custom-call(s32[2048]{0:T(1024)S(1)} %copy-done.2, s32[16,128]{1,0:T(8,128)S(1)} %bitcast.6, s32[3,2048]{1,0:T(4,128)S(1)} %bitcast.7, f32[5,16,16,64]{3,2,1,0:T(8,128)S(1)} %copy-done, f32[5,8,4096]{2,1,0:T(8,128)S(1)} %bitcast.4), custom_call_target="tpu_custom_call" | custom-call | tf_op jit(solution)/shard_map/pallas_call | solution.py:790
  53.8 0.8 %copy.8 = f32[5,16,16,64]{3,2,1,0:T(8,128)} copy(f32[5,16,16,64]{3,2,1,0:T(8,128)S(1)} %get-tuple-element.8) | data formatting | bytes 655360
  54.6 0.8 %copy.9 = f32[8,5,4096]{2,0,1:T(8,128)} copy(f32[8,5,4096]{2,0,1:T(8,128)S(1)} %bitcast.5) | data formatting | bytes 1310720
Async XLA Ops:
  0.6 1.1 %copy-start = (f32[5,16,16,64]{3,2,1,0:T(8,128)S(1)}, f32[5,16,16,64]{3,2,1,0:T(8,128)}, u32[]{:S(2)}) copy-start(f32[5,16,16,64]{3,2,1,0:T(8,128)} %coarse_hbm.1) | copy-start | bytes 983044
  1.7 1.1 %copy-start.1 = (f32[8,5,4096]{2,0,1:T(8,128)S(1)}, f32[8,5,4096]{2,0,1:T(8,128)}, u32[]{:S(2)}) copy-start(f32[8,5,4096]{2,0,1:T(8,128)} %param.5) | copy-start | bytes 1966084
  2.8 0.7 %copy-start.2 = (s32[2048]{0:T(1024)S(1)}, s32[2048]{0:T(1024)}, u32[]{:S(2)}) copy-start(s32[2048]{0:T(1024)} %parent_hbm.1) | copy-start | bytes 24580
  3.5 0.8 %copy-start.3 = (s32[2048,3]{0,1:T(4,128)S(1)}, s32[2048,3]{0,1:T(4,128)}, u32[]{:S(2)}) copy-start(s32[2048,3]{0,1:T(4,128)} %param.7) | copy-start | bytes 73732

commit v3 on v2

--- a/solution.py
+++ b/solution.py
@@ -9,6 +9,10 @@
 
 GAMMA = 1.4
 COURANT = 0.04
+FINE_UNROLL = 1
+COARSE_UNROLL = 4
+CUT_UNROLL = 4
+SETTLE_UNROLL = 4
 FIELDS = 5
 REGIONS = 4
 BOXMAX = 8
@@ -225,7 +229,7 @@
             done(big)
         return here, here_prim, x_low
 
-    last = lax.fori_loop(0, 8, pair, (here, here_prim, x_low))
+    last = lax.fori_loop(0, 8, pair, (here, here_prim, x_low), unroll=FINE_UNROLL)
     x_register(last[2], 1)
 
 
@@ -235,15 +239,18 @@
     tip = iota((8, 128), 0)
 
     def load(plane):
-        x = jnp.clip(plane - 1, 0, 15)
+        return [block[f, plane] for f in range(FIELDS)]
+
+    def widen(x, _):
         column = (x % 8) * 16 + row
-        cells = []
         for f in range(FIELDS):
             below = jnp.broadcast_to(z_rim[0, x // 8, f : f + 1, :], (16, 128))
             above = jnp.broadcast_to(z_rim[1, x // 8, f : f + 1, :], (16, 128))
             side = jnp.where(lane == 64, pick(above, column), pick(below, column))
-            cells.append(jnp.where(lane < 64, block[f, plane], side))
-        return cells
+            block[f, x + 1] = jnp.where(lane < 64, block[f, x + 1], side)
+        return 0
+
+    lax.fori_loop(0, 16, widen, 0, unroll=4)
 
     ghost = load(0)
     here = load(1)
@@ -296,32 +303,35 @@
             new[f, x] = here[f] - (0.5 * COURANT) * change
         return after, after_prim, x_high
 
-    lax.fori_loop(0, 16, one, (here, here_prim, low))
+    lax.fori_loop(0, 16, one, (here, here_prim, low), unroll=COARSE_UNROLL)
 
 
 def cut_rims(source, corner, put):
     cx, cy, cz = corner
-    lane = iota((16, 128), 1)
-    row = iota((16, 128), 0)
+    lane = iota((8, 128), 1)
+    row = iota((8, 128), 0)
+    low_half = lane < 64
     part = (lane % 64) // 8
     along_z = cz + lane % 8
-    rows_x = row - cy == part
-    rows_y = row == jnp.where(lane < 64, cy - 1, cy + 8)
-    rows_z = row - cy == lane % 8
-    ends = jnp.where(lane < 64, cz - 1, cz + 8)
+    ends = jnp.where(low_half, cz - 1, cz + 8)
+    rows_x = row == part
+    rows_z = row == lane % 8
     for f in range(FIELDS):
-        low = pick(source(f, cx - 1), along_z)
-        high = pick(source(f, cx + 8), along_z)
-        v = jnp.where(rows_x, jnp.where(lane < 64, low, high), 0.0)
+        low = pick(source(f, cx - 1, cy, 8), along_z)
+        high = pick(source(f, cx + 8, cy, 8), along_z)
+        v = jnp.where(rows_x, jnp.where(low_half, low, high), 0.0)
         put(f, 0, jnp.sum(v, axis=0, keepdims=True))
-        y_total = jnp.zeros((16, 128), F32)
-        z_total = jnp.zeros((16, 128), F32)
+        low = jnp.zeros((8, 128), F32)
+        high = jnp.zeros((8, 128), F32)
+        total = jnp.zeros((8, 128), F32)
         for big in range(8):
-            plane = source(f, cx + big)
-            y_total = jnp.where(part == big, pick(plane, along_z), y_total)
-            z_total = jnp.where(part == big, pick(plane, ends), z_total)
-        put(f, 1, jnp.sum(jnp.where(rows_y, y_total, 0.0), axis=0, keepdims=True))
-        put(f, 2, jnp.sum(jnp.where(rows_z, z_total, 0.0), axis=0, keepdims=True))
+            here = row == big
+            low = jnp.where(here, jnp.broadcast_to(source(f, cx + big, cy - 1, 1), (8, 128)), low)
+            high = jnp.where(here, jnp.broadcast_to(source(f, cx + big, cy + 8, 1), (8, 128)), high)
+            total = jnp.where(part == big, pick(source(f, cx + big, cy, 8), ends), total)
+        v = jnp.where(low_half, pick(low, along_z), pick(high, along_z))
+        put(f, 1, jnp.sum(jnp.where(rows_x, v, 0.0), axis=0, keepdims=True))
+        put(f, 2, jnp.sum(jnp.where(rows_z, total, 0.0), axis=0, keepdims=True))
 
 
 def plan_settle(corners, new, x_face, y_low, y_high, z_low, z_high, weight, index):
@@ -334,7 +344,6 @@
             cx, cy, cz = corners[c]
             step = x - cx
             inside = jnp.logical_and(step >= 0, step < 8)
-            big = jnp.clip(step, 0, 7)
             dy = row - cy
             dz = lane - cz
             in_y = jnp.logical_and(dy >= 0, dy < 8)
@@ -349,17 +358,10 @@
             )
             ys = jnp.clip(dy, 0, 7)
             zs = jnp.clip(dz, 0, 7)
-            base = jnp.where(inside, (big % 2) * 64, jnp.where(step == 8, 64, 0))
-            first = jnp.where(
-                near > 0,
-                jnp.where(near == 5, 64, 0) + big * 8 + zs,
-                base + ys * 8 + zs,
-            )
-            ends = jnp.where(side == 7, 64, 0) + big * 8 + ys
+            lanes = jnp.where(mine < 4, ys * 8 + zs, 32 + 8 * mine + jnp.where(mine < 6, zs, ys))
             used = mine > 0
             kind = jnp.where(used, mine, kind)
-            index[x, c, 0] = first + jnp.where(used, 128, 0)
-            index[x, c, 1] = ends + jnp.where(mine >= 6, 128, 0)
+            index[x, c] = jnp.where(used, lanes + 128, 0)
         factor = jnp.where(kind < 2, 0.0, jnp.where(kind % 2 == 0, -COURANT, COURANT))
         weight[x] = jnp.where(kind == 1, 0.125, 0.0625 * factor)
         for f in range(FIELDS):
@@ -380,37 +382,42 @@
     lax.fori_loop(0, 16, one, 0)
 
 
-def settle(corners, answers, new, weight, index, out):
-    row = iota((16, 128), 0)
-    y_rows = [
-        jnp.logical_or(row == corners[c][1] - 1, row == corners[c][1] + 8) for c in range(REGIONS)
-    ]
-
+def settle_rows(answers, rows):
+    lane = iota((REGIONS, 128), 1)
+    spot = ((lane % 16) // 8) * 64 + lane % 8
+    for f in range(FIELDS):
+        ends = answers[7 * f]
+        rows[f, 0] = ends
+        rows[f, 9] = pltpu.roll(ends, 64, 1)
+        y_face = answers[7 * f + 1]
+        z_face = answers[7 * f + 2]
+        for big in range(8):
+            cells = answers[7 * f + 3 + big // 2]
+            if big % 2:
+                cells = pltpu.roll(cells, 64, 1)
+            around = jnp.where(
+                lane < 80, pick(y_face, spot + 8 * big), pick(z_face, spot + 8 * big)
+            )
+            rows[f, 1 + big] = jnp.where(lane < 64, cells, around)
+
+
+def settle(corners, rows, new, weight, index, out):
     def one(x, _):
         values = [jnp.zeros((16, 128), F32) for _ in range(FIELDS)]
         for c in range(REGIONS):
-            step = x - corners[c][0]
-            inside = jnp.logical_and(step >= 0, step < 8)
-            main_row = jnp.where(inside, 3 + jnp.clip(step, 0, 7) // 2, 0)
-            first = index[x, c, 0]
-            ends = index[x, c, 1]
-            used = first >= 128
-            use_end = ends >= 128
-            first = first & 127
-            ends = ends & 127
+            which = jnp.clip(x - corners[c][0] + 1, 0, 9)
+            lanes = index[x, c]
+            used = lanes >= 128
+            lanes = lanes & 127
             for f in range(FIELDS):
-                main = jnp.broadcast_to(answers[7 * f + main_row, c : c + 1, :], (16, 128))
-                y_face = jnp.broadcast_to(answers[7 * f + 1, c : c + 1, :], (16, 128))
-                z_face = jnp.broadcast_to(answers[7 * f + 2, c : c + 1, :], (16, 128))
-                v = pick(jnp.where(y_rows[c], y_face, main), first)
-                v = jnp.where(use_end, pick(z_face, ends), v)
-                values[f] = jnp.where(used, v, values[f])
+                line = jnp.broadcast_to(rows[f, which, c : c + 1, :], (16, 128))
+                values[f] = jnp.where(used, pick(line, lanes), values[f])
         for f in range(FIELDS):
             v = new[f, x] + weight[x] * values[f]
             out[f, x] = v[:, :64]
         return 0
 
-    lax.fori_loop(0, 16, one, 0)
+    lax.fori_loop(0, 16, one, 0, unroll=SETTLE_UNROLL)
 
 
 def whole(
@@ -457,6 +464,7 @@
     direct_in,
     answer_in,
     answers,
+    answer_rows,
     table,
     load_sems,
     halo_send,
@@ -600,7 +608,7 @@
             cut_rims(source, corner, put)
             return 0
 
-        lax.fori_loop(0, REGIONS, one, 0)
+        lax.fori_loop(0, REGIONS, one, 0, unroll=CUT_UNROLL)
 
     def ship(src, dst, index, device):
         pltpu.make_async_remote_copy(
@@ -634,7 +642,7 @@
         lax.fori_loop(1, members, one, 0)
         rim_in[when][members - 1] = cut[when, table[32]]
 
-    cut_all(0, lambda f, x: block[f, x + 1])
+    cut_all(0, lambda f, x, y, n: block[f, x + 1, pl.ds(y, n), :])
     send_rims(0)
 
     plane_load.wait()
@@ -677,7 +685,10 @@
         block[f, 0] = x_rim[0, f]
         block[f, 17] = x_rim[1, f]
     coarse_step(block, y_rim, z_rim, new, x_face, y_low, y_high, z_low, z_high)
-    cut_all(1, lambda f, x: 0.5 * (block[f, x + 1] + new[f, x]))
+    cut_all(
+        1,
+        lambda f, x, y, n: 0.5 * (block[f, x + 1, pl.ds(y, n), :] + new[f, x, pl.ds(y, n), :]),
+    )
     send_rims(1)
 
     sub = iota((BOXMAX, 128), 0)
@@ -767,7 +778,8 @@
     wait_many(answer_in.at[others], 4, many_recv)
     for v in range(relayed):
         answers[v] = answer_in[lax.rem(within - v + 2 * members - 1, members)]
-    settle(corners, answers, new, weight, index, coarse_out)
+    settle_rows(answers, answer_rows)
+    settle(corners, answer_rows, new, weight, index, coarse_out)
     wait_many(rim_out.at[0, others], 0, many_send)
     wait_many(rim_out.at[1, others], 1, many_send)
     wait_many(relay_in.at[others], 2, many_send)
@@ -808,7 +820,7 @@
             pltpu.VMEM(field_block, F32),
             pltpu.VMEM(field_block, F32),
             pltpu.VMEM((16, 16, 128), F32),
-            pltpu.VMEM((16, REGIONS, 2, 16, 128), I32),
+            pltpu.VMEM((16, REGIONS, 16, 128), I32),
             pltpu.VMEM((2, FIELDS, 16, 128), F32),
             pltpu.VMEM((2, 2, FIELDS, 128), F32),
             pltpu.VMEM((2, FIELDS, 16, 128), F32),
@@ -831,6 +843,7 @@
             pltpu.VMEM((members, direct, 128), F32),
             pltpu.VMEM((members, REGIONS, 128), F32),
             pltpu.VMEM((rows, REGIONS, 128), F32),
+            pltpu.VMEM((FIELDS, 10, REGIONS, 128), F32),
             pltpu.SMEM((32 + 2 * members,), I32),
             pltpu.SemaphoreType.DMA((5,)),
             pltpu.SemaphoreType.DMA((6,)),
@@ -839,7 +852,7 @@
             pltpu.SemaphoreType.DMA((5,)),
         ],
         compiler_params=pltpu.CompilerParams(
-            collective_id=0, has_side_effects=True, vmem_limit_bytes=48 * 1024 * 1024
+            collective_id=0, has_side_effects=True, vmem_limit_bytes=62 * 1024 * 1024
         ),
     )(slot_parent, plane, corner, coarse_state, fine)
     return coarse_next, jnp.transpose(fine_next, (1, 0, 2))

time: 55.7 us -> 50.3 us (0.903)
  Pallas kernels: 49.5 us -> 46.6 us
  local copies, waits for them, and re-layouts: 5.3 us -> 2.9 us
    pallas_call x1, Pallas kernels: 49.5 us -> 46.6 us  [on_device(): pl.pallas_call(functools.partial(whole, sizes), out_shape=(jax.ShapeDtype...]
    unnamed x10 -> x4, local copies, waits for them, and re-layouts: 5.3 us -> 2.9 us
where the time goes in v3:
time: 50.3 us; the launch traced here: 50.1 us
  Pallas kernels  46.6 us (93%)
  local copies, waits for them, and re-layouts  2.9 us (6%)
  between operations  0.65 us (1%)
    pallas_call x1, Pallas kernels, on_device(): pl.pallas_call(functools.partial(whole, sizes), out_shape=(jax.ShapeDtype...  46.6 us
    unnamed x4, local copies, waits for them, and re-layouts  2.9 us

profile of v3, /device:TPU:4, one launch (start us, length us, event | category | flops | bytes accessed | tf_op | source)
XLA Modules:
  0.0 50.1 jit_solution(13574393039928292423)
XLA Ops:
  0.6 46.6 %shard_map.59 = (f32[5,16,16,64]{3,2,1,0:T(8,128)}, f32[5,8,4096]{2,1,0:T(8,128)}) custom-call(s32[2048]{0:T(1024)} %parent_hbm.1, s32[16,128]{1,0:T(8,128)} %bitcast.6, s32[3,2048]{1,0:T(4,128)} %bitcast.7, f32[5,16,16,64]{3,2,1,0:T(8,128)} %coarse_hbm.1, f32[5,8,4096]{2,1,0:T(8,128)} %bitcast.4), custom_call_target="tpu_custom_call" | custom-call | tf_op jit(solution)/shard_map/pallas_call | solution.py:802
  47.2 0.0 copy-start
  47.2 2.1 %copy.8 = f32[5,16,16,64]{3,2,1,0:T(8,128)} copy(f32[5,16,16,64]{3,2,1,0:T(8,128)} %get-tuple-element.8) | data formatting | bytes 655360
  49.3 0.0 copy-done
  49.3 0.8 %copy.9 = f32[8,5,4096]{2,0,1:T(8,128)} copy(f32[8,5,4096]{2,0,1:T(8,128)S(1)} %bitcast.5) | data formatting | bytes 1310720
Async XLA Ops:
  47.2 2.1 %copy-start = (f32[5,8,4096]{2,1,0:T(8,128)S(1)}, f32[5,8,4096]{2,1,0:T(8,128)}, u32[]{:S(2)}) copy-start(f32[5,8,4096]{2,1,0:T(8,128)} %get-tuple-element.5) | copy-start | bytes 1966084

commit v4 on v3

--- a/solution.py
+++ b/solution.py
@@ -9,7 +9,10 @@
 
 GAMMA = 1.4
 COURANT = 0.04
-FINE_UNROLL = 1
+PRIM_UNROLL = 2
+X_UNROLL = 5
+YZ_UNROLL = 4
+OUTER_UNROLL = 4
 COARSE_UNROLL = 4
 CUT_UNROLL = 4
 SETTLE_UNROLL = 4
@@ -71,67 +74,150 @@
     return [move(v) for v in q], [move(v) for v in terms[0]], move(terms[1])
 
 
-def fine_step(box, rim, reg, filled, put, second, done=None):
+def span(plane, h):
+    return pl.ds(pl.multiple_of(plane * 256 + h * 128, 128), 128)
+
+
+def roll(v, by):
+    return pltpu.roll(v, by % 128, 1)
+
+
+def fine_prims(cells, prim):
+    def one(plane, _):
+        for h in range(2):
+            where = span(plane, h)
+            inverse, pressure, sound, _ = prims([cells[f, :, where] for f in range(FIELDS)])
+            prim[0, :, where] = inverse
+            prim[1, :, where] = pressure
+            prim[2, :, where] = sound
+        return 0
+
+    lax.fori_loop(0, 16, one, 0, unroll=PRIM_UNROLL)
+
+
+def fine_inner(cells, prim, out):
     lane = iota((BOXMAX, 128), 1)
     first_row = lane < 16
     last_row = lane >= 112
     k_first = lane % 16 == 0
-    k_last = lane % 16 == 15
-    half_k = (lane % 16) // 2
+
+    def load(plane, h):
+        where = span(plane, h)
+        q = [cells[f, :, where] for f in range(FIELDS)]
+        pressure = prim[1, :, where]
+        return q, (prim[0, :, where], pressure, prim[2, :, where], q[4] + pressure)
+
+    def x_one(plane, low):
+        high = []
+        for h in range(2):
+            q, q_prim = load(plane, h)
+            up, up_prim = load(plane + 1, h)
+            flux = face(q, along(q, q_prim, 0), up, along(up, up_prim, 0))
+            for f in range(FIELDS):
+                out[f, :, span(plane, h)] = q[f] - (0.5 * COURANT) * (flux[f] - low[h][f])
+            high.append(flux)
+        return high
+
+    none = [[jnp.zeros((BOXMAX, 128), F32)] * FIELDS] * 2
+    high = lax.fori_loop(0, 15, x_one, none, unroll=X_UNROLL)
+    for h in range(2):
+        for f in range(FIELDS):
+            out[f, :, span(15, h)] = cells[f, :, span(15, h)] + (0.5 * COURANT) * high[h][f]
+
+    def yz_one(plane, _):
+        for h in range(2):
+            q, q_prim = load(plane, h)
+            terms = along(q, q_prim, 2)
+            shifted = moved(q, terms, lambda v: roll(v, 1))
+            z = face(shifted[0], (shifted[1], shifted[2]), q, terms)
+            for f in range(FIELDS):
+                low = jnp.where(k_first, 0.0, z[f])
+                where = span(plane, h)
+                out[f, :, where] = out[f, :, where] - (0.5 * COURANT) * (roll(low, -1) - low)
+        q0, prim0 = load(plane, 0)
+        q1, prim1 = load(plane, 1)
+        terms0 = along(q0, prim0, 1)
+        terms1 = along(q1, prim1, 1)
+        shifted0 = moved(q0, terms0, lambda v: roll(v, 16))
+        shifted1 = moved(q1, terms1, lambda v: roll(v, 16))
+
+        def seam(low, high):
+            return jnp.where(first_row, low, high)
+
+        low1 = (
+            [seam(shifted0[0][f], shifted1[0][f]) for f in range(FIELDS)],
+            ([seam(shifted0[1][f], shifted1[1][f]) for f in range(FIELDS)], seam(shifted0[2], shifted1[2])),
+        )
+        y0 = face(shifted0[0], (shifted0[1], shifted0[2]), q0, terms0)
+        y1 = face(low1[0], low1[1], q1, terms1)
+        for f in range(FIELDS):
+            low = jnp.where(first_row, 0.0, y0[f])
+            up0 = roll(low, -16)
+            up1 = roll(y1[f], -16)
+            for h, up, down in ((0, jnp.where(last_row, up1, up0), low), (1, jnp.where(last_row, up0, up1), y1[f])):
+                where = span(plane, h)
+                out[f, :, where] = out[f, :, where] - (0.5 * COURANT) * (up - down)
+        return 0
+
+    lax.fori_loop(0, 16, yz_one, 0, unroll=YZ_UNROLL)
+
+
+def fine_outer(cells, prim, rim, reg, filled, out, old):
+    second = old is not None
+    lane = iota((BOXMAX, 128), 1)
+    k = lane % 16
+    half_k = k // 2
     quarter = lane // 32
     squeeze = ((lane % 32) // 8) * 32 + (lane % 8) * 2
     part = (lane % 64) // 8
-
-    def halves(f, plane):
-        return [box[f, plane, :, 128 * h : 128 * h + 128] for h in range(2)]
-
-    for f in range(FIELDS):
+    low_half = lane < 64
+    step = 0.5 * COURANT
+    y_sign = jnp.where(low_half, 1.0, -1.0)
+    z_sign = jnp.where(k < 8, 1.0, -1.0)
+    y_weight = (jnp.where(lane < 16, step, 0.0), jnp.where(lane >= 112, -step, 0.0))
+    z_weight = jnp.where(k == 0, step, jnp.where(k == 15, -step, 0.0))
+
+    def load(plane, h):
+        where = span(plane, h)
+        q = [cells[f, :, where] for f in range(FIELDS)]
+        pressure = prim[1, :, where]
+        return q, (prim[0, :, where], pressure, prim[2, :, where], q[4] + pressure)
+
+    def edge(ghost, ghost_terms, q, terms, sign):
+        signal = jnp.maximum(ghost_terms[1], terms[1]) * sign
+        return [
+            (ghost_terms[0][f] + terms[0][f]) - signal * (q[f] - ghost[f]) for f in range(FIELDS)
+        ]
+
+    for plane, side, sign in ((0, 0, 1.0), (15, 64, -1.0)):
+        flux = []
         for h in range(2):
-            spread = (h * 4 + quarter) * 8 + half_k
-            box[f, 0, :, 128 * h : 128 * h + 128] = pick(rim[3 * f], spread)
-            box[f, 17, :, 128 * h : 128 * h + 128] = pick(rim[3 * f], spread + 64)
-
-    def load(plane):
-        both = [halves(f, plane) for f in range(FIELDS)]
-        return [[both[f][h] for f in range(FIELDS)] for h in range(2)]
-
-    def x_faces(low, low_prim, high, high_prim):
-        return [
-            face(low[h], along(low[h], low_prim[h], 0), high[h], along(high[h], high_prim[h], 0))
-            for h in range(2)
-        ]
-
-    def roll(v, by):
-        return pltpu.roll(v, by % 128, 1)
-
-    ghost = load(0)
-    here = load(1)
-    here_prim = [prims(here[h]) for h in range(2)]
-    x_low = x_faces(ghost, [prims(ghost[h]) for h in range(2)], here, here_prim)
-
-    def x_register(faces, side):
+            spread = (h * 4 + quarter) * 8 + half_k + side
+            ghost = [pick(rim[3 * f], spread) for f in range(FIELDS)]
+            q, q_prim = load(plane, h)
+            flux.append(edge(ghost, along(ghost, prims(ghost), 0), q, along(q, q_prim, 0), sign))
+            for f in range(FIELDS):
+                where = span(plane, h)
+                out[f, :, where] = out[f, :, where] + (sign * step) * flux[h][f]
+        mine = jnp.logical_and(filled, low_half if side == 0 else lane >= 64)
         for f in range(FIELDS):
-            out = []
+            found = []
             for h in range(2):
-                v = faces[h][f]
+                v = flux[h][f]
                 v = v + roll(v, -1)
                 v = v + roll(v, -16)
-                out.append(pick(v, squeeze))
-            both = jnp.where((lane % 64) < 32, out[0], out[1])
-            mine = jnp.logical_and(filled, (lane < 64) if side == 0 else (lane >= 64))
+                found.append(pick(v, squeeze))
+            both = jnp.where((lane % 64) < 32, found[0], found[1])
             reg[7 * f] = reg[7 * f] + jnp.where(mine, both, 0.0)
 
-    x_register(x_low, 0)
-
-    def pair(big, carried):
-        here, here_prim, x_low = carried
-        y_lanes = big * 8 + half_k + jnp.where(lane >= 64, 64, 0)
+    def pair(big, _):
+        y_lanes = big * 8 + half_k + jnp.where(low_half, 0, 64)
         y_ghost = [pick(rim[3 * f + 1], y_lanes) for f in range(FIELDS)]
         y_ghost_terms = along(y_ghost, prims(y_ghost), 1)
         z_ghost = []
         z_ghost_terms = []
         for h in range(2):
-            z_lanes = big * 8 + h * 4 + quarter + jnp.where(lane % 16 >= 8, 64, 0)
+            z_lanes = big * 8 + h * 4 + quarter + jnp.where(k >= 8, 64, 0)
             ghost = [pick(rim[3 * f + 2], z_lanes) for f in range(FIELDS)]
             z_ghost.append(ghost)
             z_ghost_terms.append(along(ghost, prims(ghost), 2))
@@ -144,93 +230,49 @@
 
         for sub in range(2):
             plane = 2 * big + sub
-            after = load(plane + 2)
-            after_prim = [prims(after[h]) for h in range(2)]
-            x_high = x_faces(here, here_prim, after, after_prim)
-
-            y_terms = [along(here[h], here_prim[h], 1) for h in range(2)]
-            rolled = [moved(here[h], y_terms[h], lambda v: roll(v, 16)) for h in range(2)]
-
-            def y_select(h, low, high):
-                return jnp.where(first_row, low, high)
-
-            low0 = [jnp.where(first_row, y_ghost[f], rolled[0][0][f]) for f in range(FIELDS)]
-            low0_terms = (
-                [jnp.where(first_row, y_ghost_terms[0][f], rolled[0][1][f]) for f in range(FIELDS)],
-                jnp.where(first_row, y_ghost_terms[1], rolled[0][2]),
-            )
-            low1 = [jnp.where(first_row, rolled[0][0][f], rolled[1][0][f]) for f in range(FIELDS)]
-            low1_terms = (
-                [jnp.where(first_row, rolled[0][1][f], rolled[1][1][f]) for f in range(FIELDS)],
-                jnp.where(first_row, rolled[0][2], rolled[1][2]),
-            )
-            y0 = face(low0, low0_terms, here[0], y_terms[0])
-            y1 = face(low1, low1_terms, here[1], y_terms[1])
-            y_end = face(here[1], y_terms[1], y_ghost, y_ghost_terms)
-            y_diff = [[], []]
+            q, q_prim = zip(*[load(plane, h) for h in range(2)])
+            near = [jnp.where(low_half, q[0][f], q[1][f]) for f in range(FIELDS)]
+            near_prim = [jnp.where(low_half, q_prim[0][i], q_prim[1][i]) for i in range(4)]
+            y = edge(y_ghost, y_ghost_terms, near, along(near, near_prim, 1), y_sign)
             for f in range(FIELDS):
-                up0 = roll(y0[f], -16)
-                up1 = roll(y1[f], -16)
-                y_diff[0].append(jnp.where(last_row, up1, up0) - y0[f])
-                y_diff[1].append(jnp.where(last_row, y_end[f], up1) - y1[f])
-                y_sum[f] = accumulate(y_sum[f], jnp.where(lane < 64, y0[f], y_end[f]))
-
-            z_diff = [[], []]
+                y_sum[f] = accumulate(y_sum[f], y[f])
             for h in range(2):
-                terms = along(here[h], here_prim[h], 2)
-                shifted = moved(here[h], terms, lambda v: roll(v, 1))
-                low = [jnp.where(k_first, z_ghost[h][f], shifted[0][f]) for f in range(FIELDS)]
-                low_terms = (
-                    [
-                        jnp.where(k_first, z_ghost_terms[h][0][f], shifted[1][f])
-                        for f in range(FIELDS)
-                    ],
-                    jnp.where(k_first, z_ghost_terms[h][1], shifted[2]),
-                )
-                z = face(low, low_terms, here[h], terms)
-                z_end = face(here[h], terms, z_ghost[h], z_ghost_terms[h])
+                z = edge(z_ghost[h], z_ghost_terms[h], q[h], along(q[h], q_prim[h], 2), z_sign)
                 for f in range(FIELDS):
-                    z_diff[h].append(jnp.where(k_last, z_end[f], roll(z[f], -1)) - z[f])
-                    z_sum[h][f] = accumulate(z_sum[h][f], jnp.where(k_last, z_end[f], z[f]))
-
-            for h in range(2):
-                for f in range(FIELDS):
-                    change = (x_high[h][f] - x_low[h][f]) + y_diff[h][f] + z_diff[h][f]
-                    new = here[h][f] - (0.5 * COURANT) * change
-                    put(f, plane, h, new)
+                    z_sum[h][f] = accumulate(z_sum[h][f], z[f])
+                    where = span(plane, h)
+                    new = out[f, :, where] + y_weight[h] * y[f] + z_weight * z[f]
                     if second:
                         new_sum[h][f] = accumulate(new_sum[h][f], new)
-            here, here_prim, x_low = after, after_prim, x_high
+                        new = jnp.where(filled, new, old[f, :, where])
+                    out[f, :, where] = new
 
         mine = jnp.logical_and(filled, part == big)
-        y_from = (lane % 8) * 2 + jnp.where(lane >= 64, 112, 0)
-        z_from = (lane % 4) * 32 + jnp.where(lane >= 64, 15, 0)
+        y_from = (lane % 8) * 2 + jnp.where(low_half, 0, 112)
+        z_from = (lane % 4) * 32 + jnp.where(low_half, 0, 15)
         for f in range(FIELDS):
             v = y_sum[f] + roll(y_sum[f], -1)
             reg[7 * f + 1] = reg[7 * f + 1] + jnp.where(mine, pick(v, y_from), 0.0)
-            out = []
+            found = []
             for h in range(2):
                 v = z_sum[h][f] + roll(z_sum[h][f], -16)
-                out.append(pick(v, z_from))
-            v = jnp.where(lane % 8 < 4, out[0], out[1])
+                found.append(pick(v, z_from))
+            v = jnp.where(lane % 8 < 4, found[0], found[1])
             reg[7 * f + 2] = reg[7 * f + 2] + jnp.where(mine, v, 0.0)
             if second:
-                out = []
+                found = []
                 for h in range(2):
                     v = new_sum[h][f]
                     v = v + roll(v, -1)
                     v = v + roll(v, -16)
-                    out.append(pick(v, squeeze))
-                v = jnp.where((lane % 64) < 32, out[0], out[1])
+                    found.append(pick(v, squeeze))
+                v = jnp.where((lane % 64) < 32, found[0], found[1])
                 v = jnp.where(filled, v, 0.0)
                 where = 7 * f + 3 + big // 2
                 reg[where] = jnp.where(lane // 64 == big % 2, v, reg[where])
-        if second:
-            done(big)
-        return here, here_prim, x_low
-
-    last = lax.fori_loop(0, 8, pair, (here, here_prim, x_low), unroll=FINE_UNROLL)
-    x_register(last[2], 1)
+        return 0
+
+    lax.fori_loop(0, 8, pair, 0, unroll=OUTER_UNROLL)
 
 
 def coarse_step(block, y_rim, z_rim, new, x_face, y_low, y_high, z_low, z_high):
@@ -401,8 +443,9 @@
             rows[f, 1 + big] = jnp.where(lane < 64, cells, around)
 
 
-def settle(corners, rows, new, weight, index, out):
-    def one(x, _):
+def settle(corners, rows, new, weight, index, out, start):
+    def one(step, _):
+        x = start + step
         values = [jnp.zeros((16, 128), F32) for _ in range(FIELDS)]
         for c in range(REGIONS):
             which = jnp.clip(x - corners[c][0] + 1, 0, 9)
@@ -417,7 +460,7 @@
             out[f, x] = v[:, :64]
         return 0
 
-    lax.fori_loop(0, 16, one, 0, unroll=SETTLE_UNROLL)
+    lax.fori_loop(0, 8, one, 0, unroll=SETTLE_UNROLL)
 
 
 def whole(
@@ -453,8 +496,10 @@
     rim_in_mid,
     rim,
     fine_ref,
-    box,
+    prim,
     half,
+    fine_new,
+    coarse_new,
     reg,
     route,
     relay_in,
@@ -645,6 +690,21 @@
     cut_all(0, lambda f, x, y, n: block[f, x + 1, pl.ds(y, n), :])
     send_rims(0)
 
+    for v in range(7 * FIELDS):
+        reg[v] = jnp.zeros((BOXMAX, 128), F32)
+
+    for copy in halos:
+        copy.wait()
+    for f in range(FIELDS):
+        block[f, 0] = x_rim[0, f]
+        block[f, 17] = x_rim[1, f]
+    coarse_step(block, y_rim, z_rim, new, x_face, y_low, y_high, z_low, z_high)
+    cut_all(
+        1,
+        lambda f, x, y, n: 0.5 * (block[f, x + 1, pl.ds(y, n), :] + new[f, x, pl.ds(y, n), :]),
+    )
+    send_rims(1)
+
     plane_load.wait()
     n_rows = REGIONS * members
     columns = members * BOXMAX
@@ -673,23 +733,8 @@
     route[...] = jnp.where(arrival.astype(F32) == chosen, 1.0, 0.0)
 
     fine_load.wait()
-    for i in range(16):
-        for f in range(FIELDS):
-            box[f, 1 + i] = fine_ref[f, :, 256 * i : 256 * i + 256]
-    for v in range(7 * FIELDS):
-        reg[v] = jnp.zeros((BOXMAX, 128), F32)
-
-    for copy in halos:
-        copy.wait()
-    for f in range(FIELDS):
-        block[f, 0] = x_rim[0, f]
-        block[f, 17] = x_rim[1, f]
-    coarse_step(block, y_rim, z_rim, new, x_face, y_low, y_high, z_low, z_high)
-    cut_all(
-        1,
-        lambda f, x, y, n: 0.5 * (block[f, x + 1, pl.ds(y, n), :] + new[f, x, pl.ds(y, n), :]),
-    )
-    send_rims(1)
+    fine_prims(fine_ref, prim)
+    fine_inner(fine_ref, prim, half)
 
     sub = iota((BOXMAX, 128), 0)
     owner = jnp.zeros((BOXMAX, 128), I32)
@@ -705,17 +750,11 @@
                 rim[v, s : s + 1, :] = rows[v : v + 1, :]
 
     take_rims(0)
-
-    def put_half(f, plane, h, value):
-        half[f, plane + 1, :, 128 * h : 128 * h + 128] = value
-
-    fine_step(box, rim, reg, filled, put_half, False)
+    fine_outer(fine_ref, prim, rim, reg, filled, half, None)
+    fine_prims(half, prim)
+    fine_inner(half, prim, fine_new)
     take_rims(1)
-
-    def put_last(f, plane, h, value):
-        old = box[f, plane + 1, :, 128 * h : 128 * h + 128]
-        where = pl.multiple_of(plane * 256 + h * 128, 128)
-        fine_out[f, :, pl.ds(where, 128)] = jnp.where(filled, value, old)
+    fine_outer(half, prim, rim, reg, filled, fine_new, fine_ref)
 
     def relay(tile):
         @pl.when(jnp.logical_and(tile != within, tile < relayed))
@@ -724,18 +763,11 @@
             device = (gx, tile // n_gz, lax.rem(tile, n_gz))
             ship(reg.at[tile], relay_in.at[distance - 1], 2, device)
 
-    def relay_ready(big):
-        @pl.when(big % 2 == 1)
-        def _():
-            for f in range(FIELDS):
-                relay(7 * f + 3 + big // 2)
-
-    fine_step(half, rim, reg, filled, put_last, True, relay_ready)
-    for f in range(FIELDS):
-        for v in range(3):
-            relay(7 * f + v)
+    for tile in range(relayed):
+        relay(tile)
     relay_in[members - 1] = reg[within]
 
+    fine_store = fetch(fine_new, fine_out, 5)
     if direct:
         for s in range(BOXMAX):
             row_stage[s] = reg[relayed:, s, :]
@@ -779,19 +811,36 @@
     for v in range(relayed):
         answers[v] = answer_in[lax.rem(within - v + 2 * members - 1, members)]
     settle_rows(answers, answer_rows)
-    settle(corners, answer_rows, new, weight, index, coarse_out)
+    coarse_stores = []
+    for part in range(2):
+        settle(corners, answer_rows, new, weight, index, coarse_new, 8 * part)
+        planes = pl.ds(8 * part, 8)
+        coarse_stores.append(fetch(coarse_new.at[:, planes], coarse_out.at[:, planes], 6 + part))
     wait_many(rim_out.at[0, others], 0, many_send)
     wait_many(rim_out.at[1, others], 1, many_send)
     wait_many(relay_in.at[others], 2, many_send)
     if direct:
         wait_many(direct_out.at[others], 3, many_send)
     wait_many(relay_out.at[others], 4, many_send)
+    fine_store.wait()
+    for copy in coarse_stores:
+        copy.wait()
+
+
+def hand_over(coarse_in, fine_in, coarse_out, fine_out, sems):
+    copies = [
+        pltpu.make_async_copy(coarse_in, coarse_out, sems.at[0]),
+        pltpu.make_async_copy(fine_in, fine_out, sems.at[1]),
+    ]
+    for copy in copies:
+        copy.start()
+    for copy in copies:
+        copy.wait()
 
 
 def on_device(sizes, coarse_state, fine_state, slot_parent, slot_corner):
     members = sizes[1] * sizes[2]
     relayed = min(members, 7 * FIELDS)
-    vmem = pl.BlockSpec(memory_space=pltpu.VMEM)
     hbm = pl.BlockSpec(memory_space=pltpu.HBM)
     fine = jnp.transpose(fine_state, (1, 0, 2))
     corner = jnp.transpose(slot_corner, (1, 0))
@@ -806,7 +855,7 @@
             jax.ShapeDtypeStruct(fine.shape, F32),
         ),
         in_specs=[hbm] * 5,
-        out_specs=(vmem, vmem),
+        out_specs=(hbm, hbm),
         scratch_shapes=[
             pltpu.SMEM(slot_parent.shape, I32),
             pltpu.SMEM(corner.shape, I32),
@@ -832,8 +881,10 @@
             pltpu.VMEM((members, 3 * FIELDS, 128), F32),
             pltpu.VMEM((3 * FIELDS, BOXMAX, 128), F32),
             pltpu.VMEM(fine.shape, F32),
-            pltpu.VMEM((FIELDS, 18, BOXMAX, 256), F32),
-            pltpu.VMEM((FIELDS, 18, BOXMAX, 256), F32),
+            pltpu.VMEM((3,) + fine.shape[1:], F32),
+            pltpu.VMEM(fine.shape, F32),
+            pltpu.VMEM(fine.shape, F32),
+            pltpu.VMEM(coarse_state.shape, F32),
             pltpu.VMEM((rows, BOXMAX, 128), F32),
             pltpu.VMEM((REGIONS * members, BOXMAX * members), F32),
             pltpu.VMEM((members, BOXMAX, 128), F32),
@@ -845,7 +896,7 @@
             pltpu.VMEM((rows, REGIONS, 128), F32),
             pltpu.VMEM((FIELDS, 10, REGIONS, 128), F32),
             pltpu.SMEM((32 + 2 * members,), I32),
-            pltpu.SemaphoreType.DMA((5,)),
+            pltpu.SemaphoreType.DMA((8,)),
             pltpu.SemaphoreType.DMA((6,)),
             pltpu.SemaphoreType.DMA((6,)),
             pltpu.SemaphoreType.DMA((5,)),
@@ -855,6 +906,16 @@
             collective_id=0, has_side_effects=True, vmem_limit_bytes=62 * 1024 * 1024
         ),
     )(slot_parent, plane, corner, coarse_state, fine)
+    coarse_next, fine_next = pl.pallas_call(
+        hand_over,
+        out_shape=(
+            jax.ShapeDtypeStruct(coarse_state.shape, F32),
+            jax.ShapeDtypeStruct(fine.shape, F32),
+        ),
+        in_specs=[hbm] * 2,
+        out_specs=(hbm, hbm),
+        scratch_shapes=[pltpu.SemaphoreType.DMA((2,))],
+    )(coarse_next, fine_next)
     return coarse_next, jnp.transpose(fine_next, (1, 0, 2))
 
 

time: 50.3 us -> 87.3 us (1.74)
  Pallas kernels: 46.6 us -> 86.5 us
  local copies, waits for them, and re-layouts: 2.9 us -> 0 us
    pallas_call x0 -> x1, Pallas kernels: none -> 40.8 us  [on_device(): pl.pallas_call(hand_over, out_shape=(jax.ShapeDtypeStruct(coarse_state.sh...]
    unnamed x4 -> x0, local copies, waits for them, and re-layouts: 2.9 us -> none
    pallas_call x1, Pallas kernels: 46.6 us -> 45.6 us  [on_device(): pl.pallas_call(functools.partial(whole, sizes), out_shape=(jax.ShapeDtype...]
where the time goes in v4:
time: 87.3 us; the launch traced here: 87.1 us
  Pallas kernels  86.5 us (99%)
    pallas_call x1, Pallas kernels, on_device(): pl.pallas_call(functools.partial(whole, sizes), out_shape=(jax.ShapeDtype...  45.6 us
    pallas_call x1, Pallas kernels, on_device(): pl.pallas_call(hand_over, out_shape=(jax.ShapeDtypeStruct(coarse_state.sh...  40.8 us

profile of v4, /device:TPU:4, one launch (start us, length us, event | category | flops | bytes accessed | tf_op | source)
XLA Modules:
  0.0 87.1 jit_solution(1047611493479531628)
XLA Ops:
  0.6 45.6 %shard_map.59 = (f32[5,16,16,64]{3,2,1,0:T(8,128)}, f32[5,8,4096]{2,1,0:T(8,128)}) custom-call(s32[2048]{0:T(1024)} %parent_hbm.1, s32[16,128]{1,0:T(8,128)} %bitcast.5, s32[3,2048]{1,0:T(4,128)} %bitcast.6, f32[5,16,16,64]{3,2,1,0:T(8,128)} %coarse_hbm.1, f32[5,8,4096]{2,1,0:T(8,128)} %bitcast.4), custom_call_target="tpu_custom_call" | custom-call | tf_op jit(solution)/shard_map/pallas_call | solution.py:851
  46.3 40.8 %shard_map.60 = (f32[5,16,16,64]{3,2,1,0:T(8,128)}, f32[5,8,4096]{2,1,0:T(8,128)}) custom-call(f32[5,16,16,64]{3,2,1,0:T(8,128)} %get-tuple-element.6.coarse_in, f32[5,8,4096]{2,1,0:T(8,128)} %get-tuple-element.7.fine_in), custom_call_target="tpu_custom_call" | custom-call | tf_op jit(solution)/shard_map/pallas_call | solution.py:909

commit v5 on v4

--- a/solution.py
+++ b/solution.py
@@ -519,7 +519,7 @@
 ):
     n_gx, n_gy, n_gz = sizes
     members = n_gy * n_gz
-    relayed = min(members, 7 * FIELDS)
+    relayed = members
     direct = 7 * FIELDS - relayed
     rim_in = (rim_in_old, rim_in_mid)
     gx = lax.axis_index("gx")
@@ -529,15 +529,19 @@
     myself = gx * members + within
     start = gx * (members * BOXMAX)
 
-    def peer(distance):
-        other = lax.rem(within + distance, members)
-        return other, (gx, other // n_gz, lax.rem(other, n_gz))
+    def hops(move):
+        return min(move[0], n_gy - move[0]) + min(move[1], n_gz - move[1])
+
+    moves = [(dy, dz) for dy in range(n_gy) for dz in range(n_gz) if dy or dz]
+    peers = []
+    for dy, dz in sorted(moves, key=hops, reverse=True):
+        other_y = lax.rem(gy + dy, n_gy)
+        other_z = lax.rem(gz + dz, n_gz)
+        peers.append((other_y * n_gz + other_z, (gx, other_y, other_z)))
 
     barrier = pltpu.get_barrier_semaphore()
-
-    def greet(distance, _):
-        pl.semaphore_signal(barrier, inc=1, device_id=peer(distance)[1], device_id_type=MESH)
-        return 0
+    for _, device in peers:
+        pl.semaphore_signal(barrier, inc=1, device_id=device, device_id_type=MESH)
 
     x_next = (lax.rem(gx + 1, n_gx), gy, gz)
     x_prev = (lax.rem(gx + n_gx - 1, n_gx), gy, gz)
@@ -547,7 +551,6 @@
     z_prev = (gx, gy, lax.rem(gz + n_gz - 1, n_gz))
     pl.semaphore_signal(barrier, inc=1, device_id=x_next, device_id_type=MESH)
     pl.semaphore_signal(barrier, inc=1, device_id=x_prev, device_id_type=MESH)
-    lax.fori_loop(1, members, greet, 0)
 
     def fetch(src, dst, index):
         copy = pltpu.make_async_copy(src, dst, load_sems.at[index])
@@ -559,6 +562,80 @@
     corner_load = fetch(corner_hbm, corner_ref, 2)
     plane_load = fetch(plane_hbm, plane_ref, 3)
     fine_load = fetch(fine_hbm, fine_ref, 4)
+
+    parent_load.wait()
+    corner_load.wait()
+
+    def scan(entry, found):
+        c0, c1, c2, c3 = found
+        hit = parent_ref[start + entry] == myself
+        return (
+            jnp.where(hit, c1, c0),
+            jnp.where(hit, c2, c1),
+            jnp.where(hit, c3, c2),
+            jnp.where(hit, entry, c3),
+        )
+
+    zero = jnp.int32(0)
+    children = lax.fori_loop(0, members * BOXMAX, scan, (zero, zero, zero, zero), unroll=8)
+    for c in range(REGIONS):
+        for k in range(3):
+            table[4 * c + k] = jnp.clip(corner_ref[k, start + children[c]], 1, 55 if k == 2 else 7)
+    child_peer = [child // BOXMAX for child in children]
+    own = [parent_ref[start + within * BOXMAX + s] for s in range(BOXMAX)]
+    own_peer = [lax.rem(jnp.maximum(own[s], 0), members) for s in range(BOXMAX)]
+
+    def look_up(other, _):
+        rank = zero
+        for c in range(1, REGIONS):
+            rank = jnp.where(child_peer[c] == other, c, rank)
+        found = zero
+        for s in range(BOXMAX):
+            found = jnp.where(jnp.logical_and(own[s] >= 0, own_peer[s] == other), s, found)
+        table[32 + other] = rank
+        table[32 + members + other] = found
+        return 0
+
+    lax.fori_loop(0, members, look_up, 0, unroll=4)
+
+    def cut_all(when, source):
+        def one(c, _):
+            corner = (table[4 * c], table[4 * c + 1], table[4 * c + 2])
+
+            def put(f, v, line):
+                cut[when, c, 3 * f + v : 3 * f + v + 1, :] = line
+
+            cut_rims(source, corner, put)
+            return 0
+
+        lax.fori_loop(0, REGIONS, one, 0, unroll=CUT_UNROLL)
+
+    def ship(src, dst, index, device):
+        pltpu.make_async_remote_copy(
+            src_ref=src,
+            dst_ref=dst,
+            send_sem=many_send.at[index],
+            recv_sem=many_recv.at[index],
+            device_id=device,
+            device_id_type=MESH,
+        ).start()
+
+    def wait_many(every, index, semaphores):
+        pltpu.make_async_copy(every, every, semaphores.at[index]).wait()
+
+    others = pl.ds(0, members - 1)
+
+    def fill_rims(when):
+        def one(other, _):
+            rim_out[when, other] = cut[when, table[32 + other]]
+            return 0
+
+        lax.fori_loop(0, members, one, 0, unroll=4)
+        rim_in[when][within] = rim_out[when, within]
+
+    def send_rims(when):
+        for other, device in peers:
+            ship(rim_out.at[when, other], rim_in[when].at[within], when, device)
 
     lane16 = iota((16, 128), 1)
     row16 = iota((16, 128), 0)
@@ -584,6 +661,9 @@
                 jnp.where(match, high, 0.0), axis=0, keepdims=True
             )
 
+    cut_all(0, lambda f, x, y, n: block[f, x + 1, pl.ds(y, n), :])
+    fill_rims(0)
+
     pl.semaphore_wait(barrier, members + 1)
 
     def halo(src, dst, index, device):
@@ -607,87 +687,6 @@
         halo(z_stage.at[0], z_rim.at[1], 5, z_prev),
     ]
 
-    parent_load.wait()
-    corner_load.wait()
-
-    def scan(entry, found):
-        c0, c1, c2, c3 = found
-        hit = parent_ref[start + entry] == myself
-        return (
-            jnp.where(hit, c1, c0),
-            jnp.where(hit, c2, c1),
-            jnp.where(hit, c3, c2),
-            jnp.where(hit, entry, c3),
-        )
-
-    zero = jnp.int32(0)
-    children = lax.fori_loop(0, members * BOXMAX, scan, (zero, zero, zero, zero), unroll=8)
-    for c in range(REGIONS):
-        for k in range(3):
-            table[4 * c + k] = jnp.clip(corner_ref[k, start + children[c]], 1, 55 if k == 2 else 7)
-    child_peer = [child // BOXMAX for child in children]
-    own = [parent_ref[start + within * BOXMAX + s] for s in range(BOXMAX)]
-    own_peer = [lax.rem(jnp.maximum(own[s], 0), members) for s in range(BOXMAX)]
-
-    def look_up(distance, _):
-        other = lax.rem(within + distance, members)
-        rank = zero
-        for c in range(1, REGIONS):
-            rank = jnp.where(child_peer[c] == other, c, rank)
-        found = zero
-        for s in range(BOXMAX):
-            found = jnp.where(jnp.logical_and(own[s] >= 0, own_peer[s] == other), s, found)
-        table[32 + distance] = rank
-        table[32 + members + distance] = found
-        return 0
-
-    lax.fori_loop(0, members, look_up, 0)
-
-    def cut_all(when, source):
-        def one(c, _):
-            corner = (table[4 * c], table[4 * c + 1], table[4 * c + 2])
-
-            def put(f, v, line):
-                cut[when, c, 3 * f + v : 3 * f + v + 1, :] = line
-
-            cut_rims(source, corner, put)
-            return 0
-
-        lax.fori_loop(0, REGIONS, one, 0, unroll=CUT_UNROLL)
-
-    def ship(src, dst, index, device):
-        pltpu.make_async_remote_copy(
-            src_ref=src,
-            dst_ref=dst,
-            send_sem=many_send.at[index],
-            recv_sem=many_recv.at[index],
-            device_id=device,
-            device_id_type=MESH,
-        ).start()
-
-    def slot_of(other):
-        return lax.rem(within - other + 2 * members - 1, members)
-
-    def wait_many(every, index, semaphores):
-        pltpu.make_async_copy(every, every, semaphores.at[index]).wait()
-
-    others = pl.ds(0, members - 1)
-
-    def send_rims(when):
-        def one(distance, _):
-            rim_out[when, distance - 1] = cut[when, table[32 + distance]]
-            ship(
-                rim_out.at[when, distance - 1],
-                rim_in[when].at[distance - 1],
-                when,
-                peer(distance)[1],
-            )
-            return 0
-
-        lax.fori_loop(1, members, one, 0)
-        rim_in[when][members - 1] = cut[when, table[32]]
-
-    cut_all(0, lambda f, x, y, n: block[f, x + 1, pl.ds(y, n), :])
     send_rims(0)
 
     for v in range(7 * FIELDS):
@@ -703,6 +702,7 @@
         1,
         lambda f, x, y, n: 0.5 * (block[f, x + 1, pl.ds(y, n), :] + new[f, x, pl.ds(y, n), :]),
     )
+    fill_rims(1)
     send_rims(1)
 
     plane_load.wait()
@@ -729,8 +729,7 @@
         least = jnp.min(candidate, axis=1, keepdims=True)
         chosen = jnp.where(row[:, 0:1] % REGIONS == r, least, chosen)
         candidate = jnp.where(candidate == least, far, candidate)
-    arrival = lax.rem(within - column // BOXMAX - 1 + members, members) * BOXMAX + column % BOXMAX
-    route[...] = jnp.where(arrival.astype(F32) == chosen, 1.0, 0.0)
+    route[...] = jnp.where(number == chosen, 1.0, 0.0)
 
     fine_load.wait()
     fine_prims(fine_ref, prim)
@@ -745,7 +744,7 @@
     def take_rims(when):
         wait_many(rim_in[when].at[others], when, many_recv)
         for s in range(BOXMAX):
-            rows = rim_in[when][slot_of(own_peer[s])]
+            rows = rim_in[when][own_peer[s]]
             for v in range(3 * FIELDS):
                 rim[v, s : s + 1, :] = rows[v : v + 1, :]
 
@@ -756,29 +755,19 @@
     take_rims(1)
     fine_outer(half, prim, rim, reg, filled, fine_new, fine_ref)
 
-    def relay(tile):
-        @pl.when(jnp.logical_and(tile != within, tile < relayed))
-        def _():
-            distance = lax.rem(tile - within + members, members)
-            device = (gx, tile // n_gz, lax.rem(tile, n_gz))
-            ship(reg.at[tile], relay_in.at[distance - 1], 2, device)
-
-    for tile in range(relayed):
-        relay(tile)
-    relay_in[members - 1] = reg[within]
+    for other, device in peers:
+        ship(reg.at[other], relay_in.at[within], 2, device)
+    relay_in[within] = reg[within]
 
     fine_store = fetch(fine_new, fine_out, 5)
     if direct:
         for s in range(BOXMAX):
             row_stage[s] = reg[relayed:, s, :]
 
-        def direct_one(distance, _):
-            direct_out[distance - 1] = row_stage[table[32 + members + distance]]
-            ship(direct_out.at[distance - 1], direct_in.at[distance - 1], 3, peer(distance)[1])
-            return 0
-
-        lax.fori_loop(1, members, direct_one, 0)
-        direct_in[members - 1] = row_stage[table[32 + members]]
+        for other, device in peers:
+            direct_out[other] = row_stage[table[32 + members + other]]
+            ship(direct_out.at[other], direct_in.at[within], 3, device)
+        direct_in[within] = row_stage[table[32 + members + within]]
 
     wait_many(relay_in.at[others], 2, many_recv)
     sorted_rows = jnp.dot(
@@ -790,13 +779,9 @@
     for p in range(members):
         relay_out[p] = sorted_rows[REGIONS * p : REGIONS * p + REGIONS]
 
-    def answer_one(distance, _):
-        other, device = peer(distance)
-        ship(relay_out.at[other], answer_in.at[distance - 1], 4, device)
-        return 0
-
-    lax.fori_loop(1, members, answer_one, 0)
-    answer_in[members - 1] = relay_out[within]
+    for other, device in peers:
+        ship(relay_out.at[other], answer_in.at[within], 4, device)
+    answer_in[within] = relay_out[within]
 
     corners = [(table[4 * c], table[4 * c + 1], table[4 * c + 2]) for c in range(REGIONS)]
     plan_settle(corners, new, x_face, y_low, y_high, z_low, z_high, weight, index)
@@ -804,12 +789,12 @@
     if direct:
         wait_many(direct_in.at[others], 3, many_recv)
         for c in range(REGIONS):
-            rows = direct_in[slot_of(child_peer[c])]
+            rows = direct_in[child_peer[c]]
             for v in range(direct):
                 answers[relayed + v, c : c + 1, :] = rows[v : v + 1, :]
     wait_many(answer_in.at[others], 4, many_recv)
     for v in range(relayed):
-        answers[v] = answer_in[lax.rem(within - v + 2 * members - 1, members)]
+        answers[v] = answer_in[v]
     settle_rows(answers, answer_rows)
     coarse_stores = []
     for part in range(2):
@@ -827,20 +812,25 @@
         copy.wait()
 
 
-def hand_over(coarse_in, fine_in, coarse_out, fine_out, sems):
-    copies = [
-        pltpu.make_async_copy(coarse_in, coarse_out, sems.at[0]),
-        pltpu.make_async_copy(fine_in, fine_out, sems.at[1]),
-    ]
-    for copy in copies:
-        copy.start()
-    for copy in copies:
-        copy.wait()
+def hand_over(coarse_in, fine_in, coarse_out, fine_out, coarse_held, fine_held, arrive, leave):
+    moves = []
+    for f in range(FIELDS):
+        for n, (src, held, dst) in enumerate(
+            ((coarse_in, coarse_held, coarse_out), (fine_in, fine_held, fine_out))
+        ):
+            first = pltpu.make_async_copy(src.at[f], held.at[f], arrive.at[2 * f + n])
+            first.start()
+            moves.append((first, pltpu.make_async_copy(held.at[f], dst.at[f], leave.at[2 * f + n])))
+    for first, second in moves:
+        first.wait()
+        second.start()
+    for _, second in moves:
+        second.wait()
 
 
 def on_device(sizes, coarse_state, fine_state, slot_parent, slot_corner):
     members = sizes[1] * sizes[2]
-    relayed = min(members, 7 * FIELDS)
+    relayed = members
     hbm = pl.BlockSpec(memory_space=pltpu.HBM)
     fine = jnp.transpose(fine_state, (1, 0, 2))
     corner = jnp.transpose(slot_corner, (1, 0))
@@ -914,7 +904,13 @@
         ),
         in_specs=[hbm] * 2,
         out_specs=(hbm, hbm),
-        scratch_shapes=[pltpu.SemaphoreType.DMA((2,))],
+        scratch_shapes=[
+            pltpu.VMEM(coarse_state.shape, F32),
+            pltpu.VMEM(fine.shape, F32),
+            pltpu.SemaphoreType.DMA((2 * FIELDS,)),
+            pltpu.SemaphoreType.DMA((2 * FIELDS,)),
+        ],
+        compiler_params=pltpu.CompilerParams(vmem_limit_bytes=62 * 1024 * 1024),
     )(coarse_next, fine_next)
     return coarse_next, jnp.transpose(fine_next, (1, 0, 2))
 

time: 87.3 us -> 46.2 us (0.53)
  Pallas kernels: 86.5 us -> 45.3 us
    pallas_call x1, Pallas kernels: 40.8 us -> 2.21 us  [on_device(): pl.pallas_call(hand_over, out_shape=(jax.ShapeDtypeStruct(coarse_state.sh...]
    pallas_call x1, Pallas kernels: 45.6 us -> 43.1 us  [on_device(): pl.pallas_call(functools.partial(whole, sizes), out_shape=(jax.ShapeDtype...]
where the time goes in v5:
time: 46.2 us; the launch traced here: 45.9 us
  Pallas kernels  45.3 us (98%)
  between operations  0.64 us (1%)
    pallas_call x1, Pallas kernels, on_device(): pl.pallas_call(functools.partial(whole, sizes), out_shape=(jax.ShapeDtype...  43.1 us
    pallas_call x1, Pallas kernels, on_device(): pl.pallas_call(hand_over, out_shape=(jax.ShapeDtypeStruct(coarse_state.sh...  2.21 us

profile of v5, /device:TPU:4, one launch (start us, length us, event | category | flops | bytes accessed | tf_op | source)
XLA Modules:
  0.0 45.9 jit_solution(15809446989222409770)
XLA Ops:
  0.6 43.1 %shard_map.59 = (f32[5,16,16,64]{3,2,1,0:T(8,128)}, f32[5,8,4096]{2,1,0:T(8,128)}) custom-call(s32[2048]{0:T(1024)} %parent_hbm.1, s32[16,128]{1,0:T(8,128)} %bitcast.5, s32[3,2048]{1,0:T(4,128)} %bitcast.6, f32[5,16,16,64]{3,2,1,0:T(8,128)} %coarse_hbm.1, f32[5,8,4096]{2,1,0:T(8,128)} %bitcast.4), custom_call_target="tpu_custom_call" | custom-call | tf_op jit(solution)/shard_map/pallas_call | solution.py:841
  43.7 2.2 %shard_map.60 = (f32[5,16,16,64]{3,2,1,0:T(8,128)}, f32[5,8,4096]{2,1,0:T(8,128)}) custom-call(f32[5,16,16,64]{3,2,1,0:T(8,128)} %get-tuple-element.6.coarse_in, f32[5,8,4096]{2,1,0:T(8,128)} %get-tuple-element.7.fine_in), custom_call_target="tpu_custom_call" | custom-call | tf_op jit(solution)/shard_map/pallas_call | solution.py:899

commit v6 on v5

--- a/solution.py
+++ b/solution.py
@@ -10,12 +10,12 @@
 GAMMA = 1.4
 COURANT = 0.04
 PRIM_UNROLL = 2
-X_UNROLL = 5
-YZ_UNROLL = 4
+X_UNROLL = 15
+YZ_UNROLL = 2
 OUTER_UNROLL = 4
 COARSE_UNROLL = 4
 CUT_UNROLL = 4
-SETTLE_UNROLL = 4
+SETTLE_UNROLL = 8
 FIELDS = 5
 REGIONS = 4
 BOXMAX = 8
@@ -108,14 +108,21 @@
         return q, (prim[0, :, where], pressure, prim[2, :, where], q[4] + pressure)
 
     def x_one(plane, low):
-        high = []
+        here = [load(plane, h) for h in range(2)]
+        after = [load(plane + 1, h) for h in range(2)]
+        high = [
+            face(
+                here[h][0],
+                along(here[h][0], here[h][1], 0),
+                after[h][0],
+                along(after[h][0], after[h][1], 0),
+            )
+            for h in range(2)
+        ]
         for h in range(2):
-            q, q_prim = load(plane, h)
-            up, up_prim = load(plane + 1, h)
-            flux = face(q, along(q, q_prim, 0), up, along(up, up_prim, 0))
             for f in range(FIELDS):
-                out[f, :, span(plane, h)] = q[f] - (0.5 * COURANT) * (flux[f] - low[h][f])
-            high.append(flux)
+                new = here[h][0][f] - (0.5 * COURANT) * (high[h][f] - low[h][f])
+                out[f, :, span(plane, h)] = new
         return high
 
     none = [[jnp.zeros((BOXMAX, 128), F32)] * FIELDS] * 2
@@ -125,17 +132,18 @@
             out[f, :, span(15, h)] = cells[f, :, span(15, h)] + (0.5 * COURANT) * high[h][f]
 
     def yz_one(plane, _):
+        cell = [load(plane, h) for h in range(2)]
+        partial = [[out[f, :, span(plane, h)] for f in range(FIELDS)] for h in range(2)]
         for h in range(2):
-            q, q_prim = load(plane, h)
+            q, q_prim = cell[h]
             terms = along(q, q_prim, 2)
             shifted = moved(q, terms, lambda v: roll(v, 1))
             z = face(shifted[0], (shifted[1], shifted[2]), q, terms)
             for f in range(FIELDS):
                 low = jnp.where(k_first, 0.0, z[f])
-                where = span(plane, h)
-                out[f, :, where] = out[f, :, where] - (0.5 * COURANT) * (roll(low, -1) - low)
-        q0, prim0 = load(plane, 0)
-        q1, prim1 = load(plane, 1)
+                partial[h][f] = partial[h][f] - (0.5 * COURANT) * (roll(low, -1) - low)
+        q0, prim0 = cell[0]
+        q1, prim1 = cell[1]
         terms0 = along(q0, prim0, 1)
         terms1 = along(q1, prim1, 1)
         shifted0 = moved(q0, terms0, lambda v: roll(v, 16))
@@ -146,7 +154,10 @@
 
         low1 = (
             [seam(shifted0[0][f], shifted1[0][f]) for f in range(FIELDS)],
-            ([seam(shifted0[1][f], shifted1[1][f]) for f in range(FIELDS)], seam(shifted0[2], shifted1[2])),
+            (
+                [seam(shifted0[1][f], shifted1[1][f]) for f in range(FIELDS)],
+                seam(shifted0[2], shifted1[2]),
+            ),
         )
         y0 = face(shifted0[0], (shifted0[1], shifted0[2]), q0, terms0)
         y1 = face(low1[0], low1[1], q1, terms1)
@@ -154,9 +165,13 @@
             low = jnp.where(first_row, 0.0, y0[f])
             up0 = roll(low, -16)
             up1 = roll(y1[f], -16)
-            for h, up, down in ((0, jnp.where(last_row, up1, up0), low), (1, jnp.where(last_row, up0, up1), y1[f])):
-                where = span(plane, h)
-                out[f, :, where] = out[f, :, where] - (0.5 * COURANT) * (up - down)
+            change0 = jnp.where(last_row, up1, up0) - low
+            change1 = jnp.where(last_row, up0, up1) - y1[f]
+            partial[0][f] = partial[0][f] - (0.5 * COURANT) * change0
+            partial[1][f] = partial[1][f] - (0.5 * COURANT) * change1
+        for h in range(2):
+            for f in range(FIELDS):
+                out[f, :, span(plane, h)] = partial[h][f]
         return 0
 
     lax.fori_loop(0, 16, yz_one, 0, unroll=YZ_UNROLL)
@@ -189,6 +204,7 @@
             (ghost_terms[0][f] + terms[0][f]) - signal * (q[f] - ghost[f]) for f in range(FIELDS)
         ]
 
+    results = []
     for plane, side, sign in ((0, 0, 1.0), (15, 64, -1.0)):
         flux = []
         for h in range(2):
@@ -196,10 +212,9 @@
             ghost = [pick(rim[3 * f], spread) for f in range(FIELDS)]
             q, q_prim = load(plane, h)
             flux.append(edge(ghost, along(ghost, prims(ghost), 0), q, along(q, q_prim, 0), sign))
-            for f in range(FIELDS):
-                where = span(plane, h)
-                out[f, :, where] = out[f, :, where] + (sign * step) * flux[h][f]
-        mine = jnp.logical_and(filled, low_half if side == 0 else lane >= 64)
+            results.append(
+                [out[f, :, span(plane, h)] + (sign * step) * flux[h][f] for f in range(FIELDS)]
+            )
         for f in range(FIELDS):
             found = []
             for h in range(2):
@@ -207,8 +222,14 @@
                 v = v + roll(v, -1)
                 v = v + roll(v, -16)
                 found.append(pick(v, squeeze))
-            both = jnp.where((lane % 64) < 32, found[0], found[1])
-            reg[7 * f] = reg[7 * f] + jnp.where(mine, both, 0.0)
+            results.append(jnp.where((lane % 64) < 32, found[0], found[1]))
+    for plane, first in ((0, 0), (15, 2 + FIELDS)):
+        for h in range(2):
+            for f in range(FIELDS):
+                out[f, :, span(plane, h)] = results[first + h][f]
+    for f in range(FIELDS):
+        v = jnp.where(low_half, results[2 + f], results[4 + FIELDS + f])
+        reg[3 * f] = reg[3 * f] + jnp.where(filled, v, 0.0)
 
     def pair(big, _):
         y_lanes = big * 8 + half_k + jnp.where(low_half, 0, 64)
@@ -223,7 +244,6 @@
             z_ghost_terms.append(along(ghost, prims(ghost), 2))
         y_sum = [None] * FIELDS
         z_sum = [[None] * FIELDS for _ in range(2)]
-        new_sum = [[None] * FIELDS for _ in range(2)]
 
         def accumulate(total, v):
             return v if total is None else total + v
@@ -233,46 +253,86 @@
             q, q_prim = zip(*[load(plane, h) for h in range(2)])
             near = [jnp.where(low_half, q[0][f], q[1][f]) for f in range(FIELDS)]
             near_prim = [jnp.where(low_half, q_prim[0][i], q_prim[1][i]) for i in range(4)]
+            before = [[out[f, :, span(plane, h)] for f in range(FIELDS)] for h in range(2)]
+            if second:
+                kept = [[old[f, :, span(plane, h)] for f in range(FIELDS)] for h in range(2)]
             y = edge(y_ghost, y_ghost_terms, near, along(near, near_prim, 1), y_sign)
             for f in range(FIELDS):
                 y_sum[f] = accumulate(y_sum[f], y[f])
+            news = []
             for h in range(2):
                 z = edge(z_ghost[h], z_ghost_terms[h], q[h], along(q[h], q_prim[h], 2), z_sign)
                 for f in range(FIELDS):
                     z_sum[h][f] = accumulate(z_sum[h][f], z[f])
-                    where = span(plane, h)
-                    new = out[f, :, where] + y_weight[h] * y[f] + z_weight * z[f]
+                    new = before[h][f] + y_weight[h] * y[f] + z_weight * z[f]
                     if second:
-                        new_sum[h][f] = accumulate(new_sum[h][f], new)
-                        new = jnp.where(filled, new, old[f, :, where])
-                    out[f, :, where] = new
+                        new = jnp.where(filled, new, kept[h][f])
+                    news.append((f, h, new))
+            for f, h, new in news:
+                out[f, :, span(plane, h)] = new
 
         mine = jnp.logical_and(filled, part == big)
         y_from = (lane % 8) * 2 + jnp.where(low_half, 0, 112)
         z_from = (lane % 4) * 32 + jnp.where(low_half, 0, 15)
+        old_regs = [[reg[3 * f + t] for t in (1, 2)] for f in range(FIELDS)]
         for f in range(FIELDS):
             v = y_sum[f] + roll(y_sum[f], -1)
-            reg[7 * f + 1] = reg[7 * f + 1] + jnp.where(mine, pick(v, y_from), 0.0)
+            old_regs[f][0] = old_regs[f][0] + jnp.where(mine, pick(v, y_from), 0.0)
             found = []
             for h in range(2):
                 v = z_sum[h][f] + roll(z_sum[h][f], -16)
                 found.append(pick(v, z_from))
             v = jnp.where(lane % 8 < 4, found[0], found[1])
-            reg[7 * f + 2] = reg[7 * f + 2] + jnp.where(mine, v, 0.0)
-            if second:
-                found = []
+            old_regs[f][1] = old_regs[f][1] + jnp.where(mine, v, 0.0)
+        for f in range(FIELDS):
+            for t in (1, 2):
+                reg[3 * f + t] = old_regs[f][t - 1]
+        return 0
+
+    lax.fori_loop(0, 8, pair, 0, unroll=OUTER_UNROLL)
+
+
+def through(tx, ty, tz, group):
+    lane = iota(tx.shape, 1)
+    x = 2 * group + lane // 64
+    y = (lane % 64) // 8
+    z = lane % 8
+
+    def sign(place):
+        return jnp.where(place == 0, 1.0, jnp.where(place == 7, -1.0, 0.0))
+
+    total = sign(y) * pick(ty, x * 8 + z + jnp.where(y == 7, 64, 0))
+    total = total + sign(z) * pick(tz, x * 8 + y + jnp.where(z == 7, 64, 0))
+    if group == 0:
+        total = total + jnp.where(lane < 64, tx, 0.0)
+    if group == 3:
+        total = total - jnp.where(lane < 64, 0.0, tx)
+    return total
+
+
+def fine_average(cells, reg, filled, sums):
+    lane = iota((BOXMAX, 128), 1)
+    squeeze = ((lane % 32) // 8) * 32 + (lane % 8) * 2
+    faces = [reg[v] for v in range(3 * FIELDS)]
+    for group in range(4):
+        tiles = []
+        for f in range(FIELDS):
+            for sub in range(2):
                 for h in range(2):
-                    v = new_sum[h][f]
-                    v = v + roll(v, -1)
-                    v = v + roll(v, -16)
-                    found.append(pick(v, squeeze))
-                v = jnp.where((lane % 64) < 32, found[0], found[1])
-                v = jnp.where(filled, v, 0.0)
-                where = 7 * f + 3 + big // 2
-                reg[where] = jnp.where(lane // 64 == big % 2, v, reg[where])
-        return 0
-
-    lax.fori_loop(0, 8, pair, 0, unroll=OUTER_UNROLL)
+                    plane = 4 * group + 2 * sub
+                    tiles.append(cells[f, :, span(plane, h)] + cells[f, :, span(plane + 1, h)])
+        tiles = [v + roll(v, -1) for v in tiles]
+        tiles = [v + roll(v, -16) for v in tiles]
+        tiles = [pick(v, squeeze) for v in tiles]
+        crossed = [through(*faces[3 * f : 3 * f + 3], group) for f in range(FIELDS)]
+        results = []
+        for f in range(FIELDS):
+            low = jnp.where(lane < 32, tiles[4 * f], tiles[4 * f + 1])
+            high = jnp.where(lane < 96, tiles[4 * f + 2], tiles[4 * f + 3])
+            v = jnp.where(lane < 64, low, high) - (0.5 * COURANT) * crossed[f]
+            results.append(jnp.where(filled, v, 0.0))
+        for f in range(FIELDS):
+            sums[4 * f + group] = results[f]
 
 
 def coarse_step(block, y_rim, z_rim, new, x_face, y_low, y_high, z_low, z_high):
@@ -424,23 +484,23 @@
     lax.fori_loop(0, 16, one, 0)
 
 
-def settle_rows(answers, rows):
+def settle_rows(sums, faces, rows):
     lane = iota((REGIONS, 128), 1)
     spot = ((lane % 16) // 8) * 64 + lane % 8
+    results = []
     for f in range(FIELDS):
-        ends = answers[7 * f]
-        rows[f, 0] = ends
-        rows[f, 9] = pltpu.roll(ends, 64, 1)
-        y_face = answers[7 * f + 1]
-        z_face = answers[7 * f + 2]
-        for big in range(8):
-            cells = answers[7 * f + 3 + big // 2]
-            if big % 2:
-                cells = pltpu.roll(cells, 64, 1)
-            around = jnp.where(
-                lane < 80, pick(y_face, spot + 8 * big), pick(z_face, spot + 8 * big)
-            )
-            rows[f, 1 + big] = jnp.where(lane < 64, cells, around)
+        tx, ty, tz = faces[3 * f], faces[3 * f + 1], faces[3 * f + 2]
+        results.append((f, 0, tx))
+        results.append((f, 9, pltpu.roll(tx, 64, 1)))
+        for group in range(4):
+            cells = sums[4 * f + group] + (0.5 * COURANT) * through(tx, ty, tz, group)
+            for sub in range(2):
+                big = 2 * group + sub
+                around = jnp.where(lane < 80, pick(ty, spot + 8 * big), pick(tz, spot + 8 * big))
+                mine = pltpu.roll(cells, 64, 1) if sub else cells
+                results.append((f, 1 + big, jnp.where(lane < 64, mine, around)))
+    for f, where, v in results:
+        rows[f, where] = v
 
 
 def settle(corners, rows, new, weight, index, out, start):
@@ -455,9 +515,10 @@
             for f in range(FIELDS):
                 line = jnp.broadcast_to(rows[f, which, c : c + 1, :], (16, 128))
                 values[f] = jnp.where(used, pick(line, lanes), values[f])
-        for f in range(FIELDS):
-            v = new[f, x] + weight[x] * values[f]
-            out[f, x] = v[:, :64]
+        factor = weight[x]
+        results = [new[f, x] + factor * values[f] for f in range(FIELDS)]
+        for f in range(FIELDS):
+            out[f, x] = results[f][:, :64]
         return 0
 
     lax.fori_loop(0, 8, one, 0, unroll=SETTLE_UNROLL)
@@ -504,11 +565,12 @@
     route,
     relay_in,
     relay_out,
+    sums,
+    sums_in,
     row_stage,
-    direct_out,
-    direct_in,
-    answer_in,
-    answers,
+    face_out,
+    face_in,
+    faces,
     answer_rows,
     table,
     load_sems,
@@ -519,8 +581,8 @@
 ):
     n_gx, n_gy, n_gz = sizes
     members = n_gy * n_gz
-    relayed = members
-    direct = 7 * FIELDS - relayed
+    share = -(-4 * FIELDS // members)
+    relays = -(-4 * FIELDS // share)
     rim_in = (rim_in_old, rim_in_mid)
     gx = lax.axis_index("gx")
     gy = lax.axis_index("gy")
@@ -689,7 +751,7 @@
 
     send_rims(0)
 
-    for v in range(7 * FIELDS):
+    for v in range(3 * FIELDS):
         reg[v] = jnp.zeros((BOXMAX, 128), F32)
 
     for copy in halos:
@@ -752,50 +814,66 @@
     fine_outer(fine_ref, prim, rim, reg, filled, half, None)
     fine_prims(half, prim)
     fine_inner(half, prim, fine_new)
+    fine_average(fine_new, reg, filled, sums)
+
+    is_relay = within < relays
+    for other, device in peers:
+
+        @pl.when(other < relays)
+        def _(other=other, device=device):
+            ship(sums.at[pl.ds(other * share, share)], relay_in.at[within], 2, device)
+
+    @pl.when(is_relay)
+    def _():
+        relay_in[within] = sums[pl.ds(within * share, share)]
+
     take_rims(1)
     fine_outer(half, prim, rim, reg, filled, fine_new, fine_ref)
-
+    fine_store = fetch(fine_new, fine_out, 5)
+
+    for s in range(BOXMAX):
+        row_stage[s] = reg[:, s, :]
     for other, device in peers:
-        ship(reg.at[other], relay_in.at[within], 2, device)
-    relay_in[within] = reg[within]
-
-    fine_store = fetch(fine_new, fine_out, 5)
-    if direct:
-        for s in range(BOXMAX):
-            row_stage[s] = reg[relayed:, s, :]
-
+        face_out[other] = row_stage[table[32 + members + other]]
+        ship(face_out.at[other], face_in.at[within], 3, device)
+    face_in[within] = row_stage[table[32 + members + within]]
+
+    @pl.when(is_relay)
+    def _():
+        wait_many(relay_in.at[others], 2, many_recv)
+        for j in range(share):
+            sorted_rows = jnp.dot(
+                route[...],
+                relay_in[:, j].reshape(columns, 128),
+                precision=lax.Precision.HIGHEST,
+                preferred_element_type=F32,
+            )
+            for p in range(members):
+                relay_out[p, j] = sorted_rows[REGIONS * p : REGIONS * p + REGIONS]
         for other, device in peers:
-            direct_out[other] = row_stage[table[32 + members + other]]
-            ship(direct_out.at[other], direct_in.at[within], 3, device)
-        direct_in[within] = row_stage[table[32 + members + within]]
-
-    wait_many(relay_in.at[others], 2, many_recv)
-    sorted_rows = jnp.dot(
-        route[...],
-        relay_in[...].reshape(columns, 128),
-        precision=lax.Precision.HIGHEST,
-        preferred_element_type=F32,
-    )
-    for p in range(members):
-        relay_out[p] = sorted_rows[REGIONS * p : REGIONS * p + REGIONS]
-
-    for other, device in peers:
-        ship(relay_out.at[other], answer_in.at[within], 4, device)
-    answer_in[within] = relay_out[within]
+            ship(relay_out.at[other], sums_in.at[pl.ds(within * share, share)], 4, device)
+        sums_in[pl.ds(within * share, share)] = relay_out[within]
 
     corners = [(table[4 * c], table[4 * c + 1], table[4 * c + 2]) for c in range(REGIONS)]
     plan_settle(corners, new, x_face, y_low, y_high, z_low, z_high, weight, index)
 
-    if direct:
-        wait_many(direct_in.at[others], 3, many_recv)
-        for c in range(REGIONS):
-            rows = direct_in[child_peer[c]]
-            for v in range(direct):
-                answers[relayed + v, c : c + 1, :] = rows[v : v + 1, :]
-    wait_many(answer_in.at[others], 4, many_recv)
-    for v in range(relayed):
-        answers[v] = answer_in[v]
-    settle_rows(answers, answer_rows)
+    wait_many(face_in.at[others], 3, many_recv)
+    for c in range(REGIONS):
+        rows = face_in[child_peer[c]]
+        for v in range(3 * FIELDS):
+            faces[v, c : c + 1, :] = rows[v : v + 1, :]
+
+    def wait_relays(every, index, semaphores):
+        @pl.when(is_relay)
+        def _():
+            wait_many(every.at[pl.ds(0, (relays - 1) * share)], index, semaphores)
+
+        @pl.when(jnp.logical_not(is_relay))
+        def _():
+            wait_many(every.at[pl.ds(0, relays * share)], index, semaphores)
+
+    wait_relays(sums_in, 4, many_recv)
+    settle_rows(sums_in, faces, answer_rows)
     coarse_stores = []
     for part in range(2):
         settle(corners, answer_rows, new, weight, index, coarse_new, 8 * part)
@@ -803,10 +881,13 @@
         coarse_stores.append(fetch(coarse_new.at[:, planes], coarse_out.at[:, planes], 6 + part))
     wait_many(rim_out.at[0, others], 0, many_send)
     wait_many(rim_out.at[1, others], 1, many_send)
-    wait_many(relay_in.at[others], 2, many_send)
-    if direct:
-        wait_many(direct_out.at[others], 3, many_send)
-    wait_many(relay_out.at[others], 4, many_send)
+    wait_relays(sums, 2, many_send)
+    wait_many(face_out.at[others], 3, many_send)
+
+    @pl.when(is_relay)
+    def _():
+        wait_many(relay_out.at[others], 4, many_send)
+
     fine_store.wait()
     for copy in coarse_stores:
         copy.wait()
@@ -830,14 +911,14 @@
 
 def on_device(sizes, coarse_state, fine_state, slot_parent, slot_corner):
     members = sizes[1] * sizes[2]
-    relayed = members
+    share = -(-4 * FIELDS // members)
+    relays = -(-4 * FIELDS // share)
     hbm = pl.BlockSpec(memory_space=pltpu.HBM)
     fine = jnp.transpose(fine_state, (1, 0, 2))
     corner = jnp.transpose(slot_corner, (1, 0))
     plane = slot_parent.reshape(-1, min(128, slot_parent.shape[0]))
     field_block = (FIELDS, 16, 16, 128)
-    rows = 7 * FIELDS
-    direct = max(rows - relayed, 1)
+    rows = 3 * FIELDS
     coarse_next, fine_next = pl.pallas_call(
         functools.partial(whole, sizes),
         out_shape=(
@@ -877,12 +958,13 @@
             pltpu.VMEM(coarse_state.shape, F32),
             pltpu.VMEM((rows, BOXMAX, 128), F32),
             pltpu.VMEM((REGIONS * members, BOXMAX * members), F32),
-            pltpu.VMEM((members, BOXMAX, 128), F32),
-            pltpu.VMEM((members, REGIONS, 128), F32),
-            pltpu.VMEM((BOXMAX, direct, 128), F32),
-            pltpu.VMEM((members, direct, 128), F32),
-            pltpu.VMEM((members, direct, 128), F32),
-            pltpu.VMEM((members, REGIONS, 128), F32),
+            pltpu.VMEM((members, share, BOXMAX, 128), F32),
+            pltpu.VMEM((members, share, REGIONS, 128), F32),
+            pltpu.VMEM((relays * share, BOXMAX, 128), F32),
+            pltpu.VMEM((relays * share, REGIONS, 128), F32),
+            pltpu.VMEM((BOXMAX, rows, 128), F32),
+            pltpu.VMEM((members, rows, 128), F32),
+            pltpu.VMEM((members, rows, 128), F32),
             pltpu.VMEM((rows, REGIONS, 128), F32),
             pltpu.VMEM((FIELDS, 10, REGIONS, 128), F32),
             pltpu.SMEM((32 + 2 * members,), I32),

time: 46.2 us -> 44.7 us (0.968)
  Pallas kernels: 45.3 us -> 43.6 us
    pallas_call x1, Pallas kernels: 43.1 us -> 41.4 us  [on_device(): pl.pallas_call(functools.partial(whole, sizes), out_shape=(jax.ShapeDtype...]
where the time goes in v6:
time: 44.7 us; the launch traced here: 44.2 us
  Pallas kernels  43.6 us (98%)
  between operations  0.64 us (1%)
    pallas_call x1, Pallas kernels, on_device(): pl.pallas_call(functools.partial(whole, sizes), out_shape=(jax.ShapeDtype...  41.4 us
    pallas_call x1, Pallas kernels, on_device(): pl.pallas_call(hand_over, out_shape=(jax.ShapeDtypeStruct(coarse_state.sh...  2.21 us

profile of v6, /device:TPU:4, one launch (start us, length us, event | category | flops | bytes accessed | tf_op | source)
XLA Modules:
  0.0 44.2 jit_solution(16968652803635130471)
XLA Ops:
  0.6 41.4 %shard_map.59 = (f32[5,16,16,64]{3,2,1,0:T(8,128)}, f32[5,8,4096]{2,1,0:T(8,128)}) custom-call(s32[2048]{0:T(1024)} %parent_hbm.1, s32[16,128]{1,0:T(8,128)} %bitcast.5, s32[3,2048]{1,0:T(4,128)} %bitcast.6, f32[5,16,16,64]{3,2,1,0:T(8,128)} %coarse_hbm.1, f32[5,8,4096]{2,1,0:T(8,128)} %bitcast.4), custom_call_target="tpu_custom_call" | custom-call | tf_op jit(solution)/shard_map/pallas_call | solution.py:922
  42.0 2.2 %shard_map.60 = (f32[5,16,16,64]{3,2,1,0:T(8,128)}, f32[5,8,4096]{2,1,0:T(8,128)}) custom-call(f32[5,16,16,64]{3,2,1,0:T(8,128)} %get-tuple-element.6.coarse_in, f32[5,8,4096]{2,1,0:T(8,128)} %get-tuple-element.7.fine_in), custom_call_target="tpu_custom_call" | custom-call | tf_op jit(solution)/shard_map/pallas_call | solution.py:981

commit v7 on v6

--- a/solution.py
+++ b/solution.py
@@ -484,23 +484,24 @@
     lax.fori_loop(0, 16, one, 0)
 
 
-def settle_rows(sums, faces, rows):
+def settle_rows(faces, rows, crossed):
     lane = iota((REGIONS, 128), 1)
     spot = ((lane % 16) // 8) * 64 + lane % 8
     results = []
+    added = []
     for f in range(FIELDS):
         tx, ty, tz = faces[3 * f], faces[3 * f + 1], faces[3 * f + 2]
         results.append((f, 0, tx))
         results.append((f, 9, pltpu.roll(tx, 64, 1)))
+        for big in range(8):
+            around = jnp.where(lane < 80, pick(ty, spot + 8 * big), pick(tz, spot + 8 * big))
+            results.append((f, 1 + big, jnp.where(lane < 64, 0.0, around)))
         for group in range(4):
-            cells = sums[4 * f + group] + (0.5 * COURANT) * through(tx, ty, tz, group)
-            for sub in range(2):
-                big = 2 * group + sub
-                around = jnp.where(lane < 80, pick(ty, spot + 8 * big), pick(tz, spot + 8 * big))
-                mine = pltpu.roll(cells, 64, 1) if sub else cells
-                results.append((f, 1 + big, jnp.where(lane < 64, mine, around)))
+            added.append((0.5 * COURANT) * through(tx, ty, tz, group))
     for f, where, v in results:
         rows[f, where] = v
+    for tile, v in enumerate(added):
+        crossed[tile] = v
 
 
 def settle(corners, rows, new, weight, index, out, start):
@@ -533,6 +534,8 @@
     fine_hbm,
     coarse_out,
     fine_out,
+    sums_out,
+    spots_out,
     parent_ref,
     corner_ref,
     plane_ref,
@@ -572,7 +575,9 @@
     face_in,
     faces,
     answer_rows,
+    crossed,
     table,
+    spots,
     load_sems,
     halo_send,
     halo_recv,
@@ -642,7 +647,11 @@
     children = lax.fori_loop(0, members * BOXMAX, scan, (zero, zero, zero, zero), unroll=8)
     for c in range(REGIONS):
         for k in range(3):
-            table[4 * c + k] = jnp.clip(corner_ref[k, start + children[c]], 1, 55 if k == 2 else 7)
+            spot = jnp.clip(corner_ref[k, start + children[c]], 1, 55 if k == 2 else 7)
+            table[4 * c + k] = spot
+            spots[4 * c + k] = spot
+        spots[4 * c + 3] = zero
+    corner_store = fetch(spots, spots_out, 9)
     child_peer = [child // BOXMAX for child in children]
     own = [parent_ref[start + within * BOXMAX + s] for s in range(BOXMAX)]
     own_peer = [lax.rem(jnp.maximum(own[s], 0), members) for s in range(BOXMAX)]
@@ -872,13 +881,16 @@
         def _():
             wait_many(every.at[pl.ds(0, relays * share)], index, semaphores)
 
-    wait_relays(sums_in, 4, many_recv)
-    settle_rows(sums_in, faces, answer_rows)
+    settle_rows(faces, answer_rows, crossed)
     coarse_stores = []
     for part in range(2):
         settle(corners, answer_rows, new, weight, index, coarse_new, 8 * part)
         planes = pl.ds(8 * part, 8)
         coarse_stores.append(fetch(coarse_new.at[:, planes], coarse_out.at[:, planes], 6 + part))
+    wait_relays(sums_in, 4, many_recv)
+    for tile in range(4 * FIELDS):
+        crossed[tile] = sums_in[tile] + crossed[tile]
+    sums_store = fetch(crossed, sums_out, 8)
     wait_many(rim_out.at[0, others], 0, many_send)
     wait_many(rim_out.at[1, others], 1, many_send)
     wait_relays(sums, 2, many_send)
@@ -889,24 +901,50 @@
         wait_many(relay_out.at[others], 4, many_send)
 
     fine_store.wait()
+    sums_store.wait()
+    corner_store.wait()
     for copy in coarse_stores:
         copy.wait()
 
 
-def hand_over(coarse_in, fine_in, coarse_out, fine_out, coarse_held, fine_held, arrive, leave):
-    moves = []
+def average_down(
+    coarse_in, fine_in, sums_in, spots_in, coarse_out, fine_out, coarse, fine, sums, spots, arrive, leave
+):
+    def move(src, dst, sems, index):
+        copy = pltpu.make_async_copy(src, dst, sems.at[index])
+        copy.start()
+        return copy
+
+    spots_load = move(spots_in, spots, arrive, 2 * FIELDS)
+    sums_load = move(sums_in, sums, arrive, 2 * FIELDS + 1)
+    coarse_loads = [move(coarse_in.at[f], coarse.at[f], arrive, f) for f in range(FIELDS)]
+    fine_loads = [move(fine_in.at[f], fine.at[f], arrive, FIELDS + f) for f in range(FIELDS)]
+    spots_load.wait()
+    sums_load.wait()
+    lane = iota((8, 128), 1)
+    row = iota((8, 128), 0)
+    stores = []
     for f in range(FIELDS):
-        for n, (src, held, dst) in enumerate(
-            ((coarse_in, coarse_held, coarse_out), (fine_in, fine_held, fine_out))
-        ):
-            first = pltpu.make_async_copy(src.at[f], held.at[f], arrive.at[2 * f + n])
-            first.start()
-            moves.append((first, pltpu.make_async_copy(held.at[f], dst.at[f], leave.at[2 * f + n])))
-    for first, second in moves:
-        first.wait()
-        second.start()
-    for _, second in moves:
-        second.wait()
+        coarse_loads[f].wait()
+        for c in range(REGIONS):
+            cx, cy, cz = spots[4 * c], spots[4 * c + 1], spots[4 * c + 2]
+            z = lane - cz
+            inside = jnp.logical_and(z >= 0, z < 8)[:, :64]
+            place = row * 8 + jnp.clip(z, 0, 7)
+            rows = pl.ds(cy, 8)
+            old = [coarse[f, cx + x, rows, :] for x in range(8)]
+            news = []
+            for x in range(8):
+                line = jnp.broadcast_to(sums[4 * f + x // 2, c : c + 1, :], (8, 128))
+                value = 0.125 * pick(line, place + 64 * (x % 2))
+                news.append(jnp.where(inside, value[:, :64], old[x]))
+            for x in range(8):
+                coarse[f, cx + x, rows, :] = news[x]
+        stores.append(move(coarse.at[f], coarse_out.at[f], leave, f))
+        fine_loads[f].wait()
+        stores.append(move(fine.at[f], fine_out.at[f], leave, FIELDS + f))
+    for copy in stores:
+        copy.wait()
 
 
 def on_device(sizes, coarse_state, fine_state, slot_parent, slot_corner):
@@ -919,14 +957,16 @@
     plane = slot_parent.reshape(-1, min(128, slot_parent.shape[0]))
     field_block = (FIELDS, 16, 16, 128)
     rows = 3 * FIELDS
-    coarse_next, fine_next = pl.pallas_call(
+    ringed, fine_next, sums, spots = pl.pallas_call(
         functools.partial(whole, sizes),
         out_shape=(
             jax.ShapeDtypeStruct(coarse_state.shape, F32),
             jax.ShapeDtypeStruct(fine.shape, F32),
+            jax.ShapeDtypeStruct((4 * FIELDS, REGIONS, 128), F32),
+            jax.ShapeDtypeStruct((4 * REGIONS,), I32),
         ),
         in_specs=[hbm] * 5,
-        out_specs=(hbm, hbm),
+        out_specs=(hbm, hbm, hbm, hbm),
         scratch_shapes=[
             pltpu.SMEM(slot_parent.shape, I32),
             pltpu.SMEM(corner.shape, I32),
@@ -967,8 +1007,10 @@
             pltpu.VMEM((members, rows, 128), F32),
             pltpu.VMEM((rows, REGIONS, 128), F32),
             pltpu.VMEM((FIELDS, 10, REGIONS, 128), F32),
+            pltpu.VMEM((4 * FIELDS, REGIONS, 128), F32),
             pltpu.SMEM((32 + 2 * members,), I32),
-            pltpu.SemaphoreType.DMA((8,)),
+            pltpu.SMEM((4 * REGIONS,), I32),
+            pltpu.SemaphoreType.DMA((10,)),
             pltpu.SemaphoreType.DMA((6,)),
             pltpu.SemaphoreType.DMA((6,)),
             pltpu.SemaphoreType.DMA((5,)),
@@ -979,21 +1021,23 @@
         ),
     )(slot_parent, plane, corner, coarse_state, fine)
     coarse_next, fine_next = pl.pallas_call(
-        hand_over,
+        average_down,
         out_shape=(
             jax.ShapeDtypeStruct(coarse_state.shape, F32),
             jax.ShapeDtypeStruct(fine.shape, F32),
         ),
-        in_specs=[hbm] * 2,
+        in_specs=[hbm] * 4,
         out_specs=(hbm, hbm),
         scratch_shapes=[
             pltpu.VMEM(coarse_state.shape, F32),
             pltpu.VMEM(fine.shape, F32),
-            pltpu.SemaphoreType.DMA((2 * FIELDS,)),
+            pltpu.VMEM((4 * FIELDS, REGIONS, 128), F32),
+            pltpu.SMEM((4 * REGIONS,), I32),
+            pltpu.SemaphoreType.DMA((2 * FIELDS + 2,)),
             pltpu.SemaphoreType.DMA((2 * FIELDS,)),
         ],
         compiler_params=pltpu.CompilerParams(vmem_limit_bytes=62 * 1024 * 1024),
-    )(coarse_next, fine_next)
+    )(ringed, fine_next, sums, spots)
     return coarse_next, jnp.transpose(fine_next, (1, 0, 2))
 
 

time: 44.7 us -> 42.6 us (0.953)
  Pallas kernels: 43.6 us -> 41.4 us
    pallas_call x1, Pallas kernels: 41.4 us -> 38.7 us  [on_device(): pl.pallas_call(functools.partial(whole, sizes), out_shape=(jax.ShapeDtype...]
    pallas_call x1, Pallas kernels: 2.21 us -> 2.7 us  [on_device(): pl.pallas_call(average_down, out_shape=(jax.ShapeDtypeStruct(coarse_state...]
where the time goes in v7:
time: 42.6 us; the launch traced here: 42.1 us
  Pallas kernels  41.4 us (97%)
  between operations  0.64 us (2%)
    pallas_call x1, Pallas kernels, on_device(): pl.pallas_call(functools.partial(whole, sizes), out_shape=(jax.ShapeDtype...  38.7 us
    pallas_call x1, Pallas kernels, on_device(): pl.pallas_call(average_down, out_shape=(jax.ShapeDtypeStruct(coarse_state...  2.7 us

profile of v7, /device:TPU:4, one launch (start us, length us, event | category | flops | bytes accessed | tf_op | source)
XLA Modules:
  0.0 42.1 jit_solution(18227685393177145103)
XLA Ops:
  0.6 38.7 %shard_map.59 = (f32[5,16,16,64]{3,2,1,0:T(8,128)}, f32[5,8,4096]{2,1,0:T(8,128)}, f32[20,4,128]{2,1,0:T(4,128)}, s32[16]{0:T(128)}) custom-call(s32[2048]{0:T(1024)} %parent_hbm.1, s32[16,128]{1,0:T(8,128)} %bitcast.5, s32[3,2048]{1,0:T(4,128)} %bitcast.6, f32[5,16,16,64]{3,2,1,0:T(8,128)} %coarse_hbm.1, f32[5,8,4096]{2,1,0:T(8,128)} %bitcast.4), custom_call_target="tpu_custom_call" | custom-call | tf_op jit(solution)/shard_map/pallas_call | solution.py:960
  39.4 2.7 %shard_map.60 = (f32[5,16,16,64]{3,2,1,0:T(8,128)}, f32[5,8,4096]{2,1,0:T(8,128)}) custom-call(f32[5,16,16,64]{3,2,1,0:T(8,128)} %get-tuple-element.8.coarse_in, f32[5,8,4096]{2,1,0:T(8,128)} %get-tuple-element.9.fine_in, f32[20,4,128]{2,1,0:T(4,128)} %get-tuple-element.10.sums_in, s32[16]{0:T(128)} %get-tuple-element.11.spots_in), custom_call_target="tpu_custom_call" | custom-call | tf_op jit(solution)/shard_map/pallas_call | solution.py:1023

commit v8 on v7

--- a/solution.py
+++ b/solution.py
@@ -10,12 +10,12 @@
 GAMMA = 1.4
 COURANT = 0.04
 PRIM_UNROLL = 2
-X_UNROLL = 15
 YZ_UNROLL = 2
-OUTER_UNROLL = 4
+OUTER_UNROLL = 8
+GATHER_UNROLL = 8
 COARSE_UNROLL = 4
 CUT_UNROLL = 4
-SETTLE_UNROLL = 8
+SETTLE_UNROLL = 4
 FIELDS = 5
 REGIONS = 4
 BOXMAX = 8
@@ -107,38 +107,18 @@
         pressure = prim[1, :, where]
         return q, (prim[0, :, where], pressure, prim[2, :, where], q[4] + pressure)
 
-    def x_one(plane, low):
-        here = [load(plane, h) for h in range(2)]
-        after = [load(plane + 1, h) for h in range(2)]
-        high = [
-            face(
-                here[h][0],
-                along(here[h][0], here[h][1], 0),
-                after[h][0],
-                along(after[h][0], after[h][1], 0),
-            )
-            for h in range(2)
-        ]
-        for h in range(2):
-            for f in range(FIELDS):
-                new = here[h][0][f] - (0.5 * COURANT) * (high[h][f] - low[h][f])
-                out[f, :, span(plane, h)] = new
-        return high
-
     none = [[jnp.zeros((BOXMAX, 128), F32)] * FIELDS] * 2
-    high = lax.fori_loop(0, 15, x_one, none, unroll=X_UNROLL)
-    for h in range(2):
-        for f in range(FIELDS):
-            out[f, :, span(15, h)] = cells[f, :, span(15, h)] + (0.5 * COURANT) * high[h][f]
-
-    def yz_one(plane, _):
+
+    def one(plane, x_low):
         cell = [load(plane, h) for h in range(2)]
-        partial = [[out[f, :, span(plane, h)] for f in range(FIELDS)] for h in range(2)]
+        after = [load(jnp.minimum(plane + 1, 15), h) for h in range(2)]
+        partial = [cell[h][0] for h in range(2)]
         for h in range(2):
             q, q_prim = cell[h]
             terms = along(q, q_prim, 2)
             shifted = moved(q, terms, lambda v: roll(v, 1))
             z = face(shifted[0], (shifted[1], shifted[2]), q, terms)
+            partial[h] = list(partial[h])
             for f in range(FIELDS):
                 low = jnp.where(k_first, 0.0, z[f])
                 partial[h][f] = partial[h][f] - (0.5 * COURANT) * (roll(low, -1) - low)
@@ -169,15 +149,27 @@
             change1 = jnp.where(last_row, up0, up1) - y1[f]
             partial[0][f] = partial[0][f] - (0.5 * COURANT) * change0
             partial[1][f] = partial[1][f] - (0.5 * COURANT) * change1
+        x_high = [
+            face(
+                cell[h][0],
+                along(cell[h][0], cell[h][1], 0),
+                after[h][0],
+                along(after[h][0], after[h][1], 0),
+            )
+            for h in range(2)
+        ]
+        x_high = [[jnp.where(plane < 15, v, 0.0) for v in x_high[h]] for h in range(2)]
         for h in range(2):
             for f in range(FIELDS):
-                out[f, :, span(plane, h)] = partial[h][f]
-        return 0
-
-    lax.fori_loop(0, 16, yz_one, 0, unroll=YZ_UNROLL)
-
-
-def fine_outer(cells, prim, rim, reg, filled, out, old):
+                out[f, :, span(plane, h)] = partial[h][f] - (0.5 * COURANT) * (
+                    x_high[h][f] - x_low[h][f]
+                )
+        return x_high
+
+    lax.fori_loop(0, 16, one, none, unroll=YZ_UNROLL)
+
+
+def fine_outer(cells, prim, rim, reg, filled, out, old, edges):
     second = old is not None
     lane = iota((BOXMAX, 128), 1)
     k = lane % 16
@@ -271,25 +263,37 @@
             for f, h, new in news:
                 out[f, :, span(plane, h)] = new
 
+        for f in range(FIELDS):
+            edges[big, f] = y_sum[f]
+            edges[big, FIELDS + f] = z_sum[0][f]
+            edges[big, 2 * FIELDS + f] = z_sum[1][f]
+        return 0
+
+    lax.fori_loop(0, 8, pair, 0, unroll=OUTER_UNROLL)
+
+    def gather(big, totals):
+        y_sum = [edges[big, f] for f in range(FIELDS)]
+        z_sum = [[edges[big, (1 + h) * FIELDS + f] for f in range(FIELDS)] for h in range(2)]
         mine = jnp.logical_and(filled, part == big)
         y_from = (lane % 8) * 2 + jnp.where(low_half, 0, 112)
         z_from = (lane % 4) * 32 + jnp.where(low_half, 0, 15)
-        old_regs = [[reg[3 * f + t] for t in (1, 2)] for f in range(FIELDS)]
+        new_totals = []
         for f in range(FIELDS):
             v = y_sum[f] + roll(y_sum[f], -1)
-            old_regs[f][0] = old_regs[f][0] + jnp.where(mine, pick(v, y_from), 0.0)
+            new_totals.append(totals[2 * f] + jnp.where(mine, pick(v, y_from), 0.0))
             found = []
             for h in range(2):
                 v = z_sum[h][f] + roll(z_sum[h][f], -16)
                 found.append(pick(v, z_from))
             v = jnp.where(lane % 8 < 4, found[0], found[1])
-            old_regs[f][1] = old_regs[f][1] + jnp.where(mine, v, 0.0)
-        for f in range(FIELDS):
-            for t in (1, 2):
-                reg[3 * f + t] = old_regs[f][t - 1]
-        return 0
-
-    lax.fori_loop(0, 8, pair, 0, unroll=OUTER_UNROLL)
+            new_totals.append(totals[2 * f + 1] + jnp.where(mine, v, 0.0))
+        return new_totals
+
+    totals = [reg[3 * f + t] for f in range(FIELDS) for t in (1, 2)]
+    totals = lax.fori_loop(0, 8, gather, totals, unroll=GATHER_UNROLL)
+    for f in range(FIELDS):
+        reg[3 * f + 1] = totals[2 * f]
+        reg[3 * f + 2] = totals[2 * f + 1]
 
 
 def through(tx, ty, tz, group):
@@ -408,7 +412,7 @@
     lax.fori_loop(0, 16, one, (here, here_prim, low), unroll=COARSE_UNROLL)
 
 
-def cut_rims(source, corner, put):
+def cut_rims(source, corner):
     cx, cy, cz = corner
     lane = iota((8, 128), 1)
     row = iota((8, 128), 0)
@@ -418,11 +422,12 @@
     ends = jnp.where(low_half, cz - 1, cz + 8)
     rows_x = row == part
     rows_z = row == lane % 8
+    lines = []
     for f in range(FIELDS):
         low = pick(source(f, cx - 1, cy, 8), along_z)
         high = pick(source(f, cx + 8, cy, 8), along_z)
         v = jnp.where(rows_x, jnp.where(low_half, low, high), 0.0)
-        put(f, 0, jnp.sum(v, axis=0, keepdims=True))
+        lines.append(jnp.sum(v, axis=0, keepdims=True))
         low = jnp.zeros((8, 128), F32)
         high = jnp.zeros((8, 128), F32)
         total = jnp.zeros((8, 128), F32)
@@ -432,8 +437,9 @@
             high = jnp.where(here, jnp.broadcast_to(source(f, cx + big, cy + 8, 1), (8, 128)), high)
             total = jnp.where(part == big, pick(source(f, cx + big, cy, 8), ends), total)
         v = jnp.where(low_half, pick(low, along_z), pick(high, along_z))
-        put(f, 1, jnp.sum(jnp.where(rows_x, v, 0.0), axis=0, keepdims=True))
-        put(f, 2, jnp.sum(jnp.where(rows_z, total, 0.0), axis=0, keepdims=True))
+        lines.append(jnp.sum(jnp.where(rows_x, v, 0.0), axis=0, keepdims=True))
+        lines.append(jnp.sum(jnp.where(rows_z, total, 0.0), axis=0, keepdims=True))
+    return lines
 
 
 def plan_settle(corners, new, x_face, y_low, y_high, z_low, z_high, weight, index):
@@ -522,7 +528,7 @@
             out[f, x] = results[f][:, :64]
         return 0
 
-    lax.fori_loop(0, 8, one, 0, unroll=SETTLE_UNROLL)
+    lax.fori_loop(0, 4, one, 0, unroll=SETTLE_UNROLL)
 
 
 def whole(
@@ -565,6 +571,7 @@
     fine_new,
     coarse_new,
     reg,
+    edges,
     route,
     relay_in,
     relay_out,
@@ -651,7 +658,7 @@
             table[4 * c + k] = spot
             spots[4 * c + k] = spot
         spots[4 * c + 3] = zero
-    corner_store = fetch(spots, spots_out, 9)
+    corner_store = fetch(spots, spots_out, 11)
     child_peer = [child // BOXMAX for child in children]
     own = [parent_ref[start + within * BOXMAX + s] for s in range(BOXMAX)]
     own_peer = [lax.rem(jnp.maximum(own[s], 0), members) for s in range(BOXMAX)]
@@ -673,10 +680,8 @@
         def one(c, _):
             corner = (table[4 * c], table[4 * c + 1], table[4 * c + 2])
 
-            def put(f, v, line):
-                cut[when, c, 3 * f + v : 3 * f + v + 1, :] = line
-
-            cut_rims(source, corner, put)
+            for v, line in enumerate(cut_rims(source, corner)):
+                cut[when, c, v : v + 1, :] = line
             return 0
 
         lax.fori_loop(0, REGIONS, one, 0, unroll=CUT_UNROLL)
@@ -713,9 +718,10 @@
     coarse_load.wait()
     for f in range(FIELDS):
         block[f, 1:17, :, 0:64] = coarse_ref[f]
+    match = row16 == lane16 % 16
+    edge_rows = [(block[f, 1:17, 0, :], block[f, 1:17, 15, :]) for f in range(FIELDS)]
+    columns_found = []
     for f in range(FIELDS):
-        y_stage[0, f] = block[f, 1:17, 0, :]
-        y_stage[1, f] = block[f, 1:17, 15, :]
         for h in range(2):
             low = jnp.zeros((16, 128), F32)
             high = jnp.zeros((16, 128), F32)
@@ -724,13 +730,15 @@
                 here = lane16 // 16 == x
                 low = jnp.where(here, jnp.broadcast_to(plane[:, 0:1], (16, 128)), low)
                 high = jnp.where(here, jnp.broadcast_to(plane[:, 63:64], (16, 128)), high)
-            match = row16 == lane16 % 16
-            z_stage[0, h, f : f + 1, :] = jnp.sum(
-                jnp.where(match, low, 0.0), axis=0, keepdims=True
-            )
-            z_stage[1, h, f : f + 1, :] = jnp.sum(
-                jnp.where(match, high, 0.0), axis=0, keepdims=True
-            )
+            low = jnp.sum(jnp.where(match, low, 0.0), axis=0, keepdims=True)
+            high = jnp.sum(jnp.where(match, high, 0.0), axis=0, keepdims=True)
+            columns_found.append((f, h, low, high))
+    for f in range(FIELDS):
+        y_stage[0, f] = edge_rows[f][0]
+        y_stage[1, f] = edge_rows[f][1]
+    for f, h, low, high in columns_found:
+        z_stage[0, h, f : f + 1, :] = low
+        z_stage[1, h, f : f + 1, :] = high
 
     cut_all(0, lambda f, x, y, n: block[f, x + 1, pl.ds(y, n), :])
     fill_rims(0)
@@ -820,7 +828,7 @@
                 rim[v, s : s + 1, :] = rows[v : v + 1, :]
 
     take_rims(0)
-    fine_outer(fine_ref, prim, rim, reg, filled, half, None)
+    fine_outer(fine_ref, prim, rim, reg, filled, half, None, edges)
     fine_prims(half, prim)
     fine_inner(half, prim, fine_new)
     fine_average(fine_new, reg, filled, sums)
@@ -837,7 +845,7 @@
         relay_in[within] = sums[pl.ds(within * share, share)]
 
     take_rims(1)
-    fine_outer(half, prim, rim, reg, filled, fine_new, fine_ref)
+    fine_outer(half, prim, rim, reg, filled, fine_new, fine_ref, edges)
     fine_store = fetch(fine_new, fine_out, 5)
 
     for s in range(BOXMAX):
@@ -883,14 +891,14 @@
 
     settle_rows(faces, answer_rows, crossed)
     coarse_stores = []
-    for part in range(2):
-        settle(corners, answer_rows, new, weight, index, coarse_new, 8 * part)
-        planes = pl.ds(8 * part, 8)
+    for part in range(4):
+        settle(corners, answer_rows, new, weight, index, coarse_new, 4 * part)
+        planes = pl.ds(4 * part, 4)
         coarse_stores.append(fetch(coarse_new.at[:, planes], coarse_out.at[:, planes], 6 + part))
     wait_relays(sums_in, 4, many_recv)
     for tile in range(4 * FIELDS):
         crossed[tile] = sums_in[tile] + crossed[tile]
-    sums_store = fetch(crossed, sums_out, 8)
+    sums_store = fetch(crossed, sums_out, 10)
     wait_many(rim_out.at[0, others], 0, many_send)
     wait_many(rim_out.at[1, others], 1, many_send)
     wait_relays(sums, 2, many_send)
@@ -997,6 +1005,7 @@
             pltpu.VMEM(fine.shape, F32),
             pltpu.VMEM(coarse_state.shape, F32),
             pltpu.VMEM((rows, BOXMAX, 128), F32),
+            pltpu.VMEM((8, rows, BOXMAX, 128), F32),
             pltpu.VMEM((REGIONS * members, BOXMAX * members), F32),
             pltpu.VMEM((members, share, BOXMAX, 128), F32),
             pltpu.VMEM((members, share, REGIONS, 128), F32),
@@ -1010,7 +1019,7 @@
             pltpu.VMEM((4 * FIELDS, REGIONS, 128), F32),
             pltpu.SMEM((32 + 2 * members,), I32),
             pltpu.SMEM((4 * REGIONS,), I32),
-            pltpu.SemaphoreType.DMA((10,)),
+            pltpu.SemaphoreType.DMA((12,)),
             pltpu.SemaphoreType.DMA((6,)),
             pltpu.SemaphoreType.DMA((6,)),
             pltpu.SemaphoreType.DMA((5,)),

time: 42.6 us -> 41.9 us (0.984)
  no operation moved by 1% of the time
where the time goes in v8:
time: 41.9 us; the launch traced here: 41.8 us
  Pallas kernels  41.2 us (98%)
  between operations  0.64 us (2%)
    pallas_call x1, Pallas kernels, on_device(): pl.pallas_call(functools.partial(whole, sizes), out_shape=(jax.ShapeDtype...  38.5 us
    pallas_call x1, Pallas kernels, on_device(): pl.pallas_call(average_down, out_shape=(jax.ShapeDtypeStruct(coarse_state...  2.7 us

profile of v8, /device:TPU:4, one launch (start us, length us, event | category | flops | bytes accessed | tf_op | source)
XLA Modules:
  0.0 41.8 jit_solution(17921071086691339272)
XLA Ops:
  0.6 38.5 %shard_map.59 = (f32[5,16,16,64]{3,2,1,0:T(8,128)}, f32[5,8,4096]{2,1,0:T(8,128)}, f32[20,4,128]{2,1,0:T(4,128)}, s32[16]{0:T(128)}) custom-call(s32[2048]{0:T(1024)} %parent_hbm.1, s32[16,128]{1,0:T(8,128)} %bitcast.5, s32[3,2048]{1,0:T(4,128)} %bitcast.6, f32[5,16,16,64]{3,2,1,0:T(8,128)} %coarse_hbm.1, f32[5,8,4096]{2,1,0:T(8,128)} %bitcast.4), custom_call_target="tpu_custom_call" | custom-call | tf_op jit(solution)/shard_map/pallas_call | solution.py:968
  39.1 2.7 %shard_map.60 = (f32[5,16,16,64]{3,2,1,0:T(8,128)}, f32[5,8,4096]{2,1,0:T(8,128)}) custom-call(f32[5,16,16,64]{3,2,1,0:T(8,128)} %get-tuple-element.8.coarse_in, f32[5,8,4096]{2,1,0:T(8,128)} %get-tuple-element.9.fine_in, f32[20,4,128]{2,1,0:T(4,128)} %get-tuple-element.10.sums_in, s32[16]{0:T(128)} %get-tuple-element.11.spots_in), custom_call_target="tpu_custom_call" | custom-call | tf_op jit(solution)/shard_map/pallas_call | solution.py:1032

commit v9 on v8

--- a/solution.py
+++ b/solution.py
@@ -316,7 +316,9 @@
 
 def fine_average(cells, reg, filled, sums):
     lane = iota((BOXMAX, 128), 1)
-    squeeze = ((lane % 32) // 8) * 32 + (lane % 8) * 2
+    even_k = lane % 2 == 0
+    even_j = (lane // 16) % 2 == 0
+    squeeze = (2 * ((lane % 32) // 8) + lane // 64) * 16 + (lane % 8) * 2 + (lane % 64) // 32
     faces = [reg[v] for v in range(3 * FIELDS)]
     for group in range(4):
         tiles = []
@@ -325,16 +327,15 @@
                 for h in range(2):
                     plane = 4 * group + 2 * sub
                     tiles.append(cells[f, :, span(plane, h)] + cells[f, :, span(plane + 1, h)])
-        tiles = [v + roll(v, -1) for v in tiles]
-        tiles = [v + roll(v, -16) for v in tiles]
+        tiles = [v + roll(v, 1 if n % 2 else -1) for n, v in enumerate(tiles)]
+        tiles = [jnp.where(even_k, tiles[n], tiles[n + 1]) for n in range(0, 4 * FIELDS, 2)]
+        tiles = [v + roll(v, 16 if n % 2 else -16) for n, v in enumerate(tiles)]
+        tiles = [jnp.where(even_j, tiles[n], tiles[n + 1]) for n in range(0, 2 * FIELDS, 2)]
         tiles = [pick(v, squeeze) for v in tiles]
         crossed = [through(*faces[3 * f : 3 * f + 3], group) for f in range(FIELDS)]
-        results = []
-        for f in range(FIELDS):
-            low = jnp.where(lane < 32, tiles[4 * f], tiles[4 * f + 1])
-            high = jnp.where(lane < 96, tiles[4 * f + 2], tiles[4 * f + 3])
-            v = jnp.where(lane < 64, low, high) - (0.5 * COURANT) * crossed[f]
-            results.append(jnp.where(filled, v, 0.0))
+        results = [
+            jnp.where(filled, tiles[f] - (0.5 * COURANT) * crossed[f], 0.0) for f in range(FIELDS)
+        ]
         for f in range(FIELDS):
             sums[4 * f + group] = results[f]
 
@@ -558,6 +559,7 @@
     y_stage,
     z_stage,
     x_rim,
+    y_packed,
     y_rim,
     z_rim,
     cut,
@@ -719,6 +721,7 @@
     for f in range(FIELDS):
         block[f, 1:17, :, 0:64] = coarse_ref[f]
     match = row16 == lane16 % 16
+    lane8 = iota((8, 128), 1)
     edge_rows = [(block[f, 1:17, 0, :], block[f, 1:17, 15, :]) for f in range(FIELDS)]
     columns_found = []
     for f in range(FIELDS):
@@ -734,8 +737,9 @@
             high = jnp.sum(jnp.where(match, high, 0.0), axis=0, keepdims=True)
             columns_found.append((f, h, low, high))
     for f in range(FIELDS):
-        y_stage[0, f] = edge_rows[f][0]
-        y_stage[1, f] = edge_rows[f][1]
+        for side in range(2):
+            rows = edge_rows[f][side]
+            y_stage[side, f] = jnp.where(lane8 < 64, rows[:8], pltpu.roll(rows[8:], 64, 1))
     for f, h, low, high in columns_found:
         z_stage[0, h, f : f + 1, :] = low
         z_stage[1, h, f : f + 1, :] = high
@@ -760,8 +764,8 @@
     halos = [
         halo(block.at[:, 16], x_rim.at[0], 0, x_next),
         halo(block.at[:, 1], x_rim.at[1], 1, x_prev),
-        halo(y_stage.at[1], y_rim.at[0], 2, y_next),
-        halo(y_stage.at[0], y_rim.at[1], 3, y_prev),
+        halo(y_stage.at[1], y_packed.at[0], 2, y_next),
+        halo(y_stage.at[0], y_packed.at[1], 3, y_prev),
         halo(z_stage.at[1], z_rim.at[0], 4, z_next),
         halo(z_stage.at[0], z_rim.at[1], 5, z_prev),
     ]
@@ -776,6 +780,9 @@
     for f in range(FIELDS):
         block[f, 0] = x_rim[0, f]
         block[f, 17] = x_rim[1, f]
+        for side in range(2):
+            y_rim[side, f, 0:8] = y_packed[side, f]
+            y_rim[side, f, 8:16] = pltpu.roll(y_packed[side, f], 64, 1)
     coarse_step(block, y_rim, z_rim, new, x_face, y_low, y_high, z_low, z_high)
     cut_all(
         1,
@@ -989,9 +996,10 @@
             pltpu.VMEM(field_block, F32),
             pltpu.VMEM((16, 16, 128), F32),
             pltpu.VMEM((16, REGIONS, 16, 128), I32),
-            pltpu.VMEM((2, FIELDS, 16, 128), F32),
+            pltpu.VMEM((2, FIELDS, 8, 128), F32),
             pltpu.VMEM((2, 2, FIELDS, 128), F32),
             pltpu.VMEM((2, FIELDS, 16, 128), F32),
+            pltpu.VMEM((2, FIELDS, 8, 128), F32),
             pltpu.VMEM((2, FIELDS, 16, 128), F32),
             pltpu.VMEM((2, 2, FIELDS, 128), F32),
             pltpu.VMEM((2, REGIONS, 3 * FIELDS, 128), F32),

time: 41.9 us -> 41.2 us (0.983)
  Pallas kernels: 41.2 us -> 40.4 us
    pallas_call x1, Pallas kernels: 38.5 us -> 37.7 us  [on_device(): pl.pallas_call(functools.partial(whole, sizes), out_shape=(jax.ShapeDtype...]
where the time goes in v9:
time: 41.2 us; the launch traced here: 41 us
  Pallas kernels  40.4 us (98%)
  between operations  0.64 us (2%)
    pallas_call x1, Pallas kernels, on_device(): pl.pallas_call(functools.partial(whole, sizes), out_shape=(jax.ShapeDtype...  37.7 us
    pallas_call x1, Pallas kernels, on_device(): pl.pallas_call(average_down, out_shape=(jax.ShapeDtypeStruct(coarse_state...  2.7 us

profile of v9, /device:TPU:4, one launch (start us, length us, event | category | flops | bytes accessed | tf_op | source)
XLA Modules:
  0.0 41.0 jit_solution(17027007596555963671)
XLA Ops:
  0.6 37.7 %shard_map.59 = (f32[5,16,16,64]{3,2,1,0:T(8,128)}, f32[5,8,4096]{2,1,0:T(8,128)}, f32[20,4,128]{2,1,0:T(4,128)}, s32[16]{0:T(128)}) custom-call(s32[2048]{0:T(1024)} %parent_hbm.1, s32[16,128]{1,0:T(8,128)} %bitcast.5, s32[3,2048]{1,0:T(4,128)} %bitcast.6, f32[5,16,16,64]{3,2,1,0:T(8,128)} %coarse_hbm.1, f32[5,8,4096]{2,1,0:T(8,128)} %bitcast.4), custom_call_target="tpu_custom_call" | custom-call | tf_op jit(solution)/shard_map/pallas_call | solution.py:975
  38.3 2.7 %shard_map.60 = (f32[5,16,16,64]{3,2,1,0:T(8,128)}, f32[5,8,4096]{2,1,0:T(8,128)}) custom-call(f32[5,16,16,64]{3,2,1,0:T(8,128)} %get-tuple-element.8.coarse_in, f32[5,8,4096]{2,1,0:T(8,128)} %get-tuple-element.9.fine_in, f32[20,4,128]{2,1,0:T(4,128)} %get-tuple-element.10.sums_in, s32[16]{0:T(128)} %get-tuple-element.11.spots_in), custom_call_target="tpu_custom_call" | custom-call | tf_op jit(solution)/shard_map/pallas_call | solution.py:1040

commit v10 on v9

--- a/solution.py
+++ b/solution.py
@@ -95,6 +95,13 @@
     lax.fori_loop(0, 16, one, 0, unroll=PRIM_UNROLL)
 
 
+def pulled(q, prim, axis, by):
+    cells = [roll(v, by) for v in q]
+    inverse, pressure, sound = [roll(v, by) for v in prim[:3]]
+    flux, signal = along(cells, (inverse, pressure, sound, cells[4] + pressure), axis)
+    return cells, flux, signal
+
+
 def fine_inner(cells, prim, out):
     lane = iota((BOXMAX, 128), 1)
     first_row = lane < 16
@@ -116,7 +123,7 @@
         for h in range(2):
             q, q_prim = cell[h]
             terms = along(q, q_prim, 2)
-            shifted = moved(q, terms, lambda v: roll(v, 1))
+            shifted = pulled(q, q_prim, 2, 1)
             z = face(shifted[0], (shifted[1], shifted[2]), q, terms)
             partial[h] = list(partial[h])
             for f in range(FIELDS):
@@ -126,8 +133,8 @@
         q1, prim1 = cell[1]
         terms0 = along(q0, prim0, 1)
         terms1 = along(q1, prim1, 1)
-        shifted0 = moved(q0, terms0, lambda v: roll(v, 16))
-        shifted1 = moved(q1, terms1, lambda v: roll(v, 16))
+        shifted0 = pulled(q0, prim0, 1, 16)
+        shifted1 = pulled(q1, prim1, 1, 16)
 
         def seam(low, high):
             return jnp.where(first_row, low, high)

time: 41.2 us -> 40.6 us (0.985)
  Pallas kernels: 40.4 us -> 39.5 us
    pallas_call x1, Pallas kernels: 37.7 us -> 36.8 us  [on_device(): pl.pallas_call(functools.partial(whole, sizes), out_shape=(jax.ShapeDtype...]
where the time goes in v10:
time: 40.6 us; the launch traced here: 40.1 us
  Pallas kernels  39.5 us (97%)
  between operations  0.64 us (2%)
    pallas_call x1, Pallas kernels, on_device(): pl.pallas_call(functools.partial(whole, sizes), out_shape=(jax.ShapeDtype...  36.8 us
    pallas_call x1, Pallas kernels, on_device(): pl.pallas_call(average_down, out_shape=(jax.ShapeDtypeStruct(coarse_state...  2.7 us

profile of v10, /device:TPU:4, one launch (start us, length us, event | category | flops | bytes accessed | tf_op | source)
XLA Modules:
  0.0 40.1 jit_solution(14321017491249909969)
XLA Ops:
  0.6 36.8 %shard_map.59 = (f32[5,16,16,64]{3,2,1,0:T(8,128)}, f32[5,8,4096]{2,1,0:T(8,128)}, f32[20,4,128]{2,1,0:T(4,128)}, s32[16]{0:T(128)}) custom-call(s32[2048]{0:T(1024)} %parent_hbm.1, s32[16,128]{1,0:T(8,128)} %bitcast.5, s32[3,2048]{1,0:T(4,128)} %bitcast.6, f32[5,16,16,64]{3,2,1,0:T(8,128)} %coarse_hbm.1, f32[5,8,4096]{2,1,0:T(8,128)} %bitcast.4), custom_call_target="tpu_custom_call" | custom-call | tf_op jit(solution)/shard_map/pallas_call | solution.py:982
  37.4 2.7 %shard_map.60 = (f32[5,16,16,64]{3,2,1,0:T(8,128)}, f32[5,8,4096]{2,1,0:T(8,128)}) custom-call(f32[5,16,16,64]{3,2,1,0:T(8,128)} %get-tuple-element.8.coarse_in, f32[5,8,4096]{2,1,0:T(8,128)} %get-tuple-element.9.fine_in, f32[20,4,128]{2,1,0:T(4,128)} %get-tuple-element.10.sums_in, s32[16]{0:T(128)} %get-tuple-element.11.spots_in), custom_call_target="tpu_custom_call" | custom-call | tf_op jit(solution)/shard_map/pallas_call | solution.py:1047
